TPU v7x, 32 devices: a whole 2x2x4 slice. The times are simulated.
32 devices in a mesh: groups: 2 (over x), blk: 16 (over z, y, core).
Axes of the slice: x: 2, y: 2, z: 4, core: 2. Of those that a mesh axis runs over, the one named last changes fastest.
Arguments:
- trans_east: float32 [1024, 16, 128], P(('groups', 'blk')), parts along dimension 0, may hold values from 2 to 20
- trans_north: float32 [1024, 16, 128], P(('groups', 'blk')), parts along dimension 0, may hold values from 0.05 to 3
- trans_up: float32 [1024, 16, 128], P(('groups', 'blk')), parts along dimension 0, may hold values from 0.05 to 3
- storage: float32 [1024, 16, 128], P(('groups', 'blk')), parts along dimension 0, may hold values from 0.2 to 4
- support_reach: int32 [64, 8, 4], P(('groups', 'blk')), parts along dimension 0, may hold values from 1 to 16, as said below
Outputs:
- basis_out: float32 [64, 8, 48, 16, 128], P(('groups', 'blk')), parts along dimension 0
There are 2 independent parts, one for each index of `groups`. A program takes and returns all parts, laid end to end along the dimension named above; each array names one. Nothing has to cross between parts.
Inputs may be any that keep to these rules, and one draw needn't show every extreme that they name: `support_reach`: at least one coarse block reaches the full 16 cells in all four directions.
All inputs are finite; a program needn't handle non-finite values.
Results may differ from a plain program's by a relative error of at most 0.0003.
Values sent between devices are 32-bit elements; how exact they have to be, the bound alone decides.
No kernel may reach another device: no remote copies, remote signals or barrier semaphores. Data moves between devices by JAX's collectives and lax.ppermute only.
A program may use at most 128 MiB of HBM per device.

v0:
```python
import functools

import jax
import jax.numpy as jnp
from jax import lax
from jax.experimental import pallas as pl
from jax.experimental.pallas import tpu as pltpu
from jax.sharding import PartitionSpec as P


TAIL = 8


class Lanes:
    def __init__(self, shape, width):
        lane = lax.broadcasted_iota(jnp.int32, shape, 1)
        self.width = width
        self.lanes = shape[1]
        self.rows = shape[0]
        self.lane = lane
        self.block = lane // width
        self.local = lane - self.block * width
        self.first = self.local == 0
        self.last = self.local == width - 1
        self.upper = self.local >= width // 2
        self.other = jnp.where(self.upper, self.block + 1, self.block - 1)
        self.row0 = lax.broadcasted_iota(jnp.int32, shape, 0) == 0
        self.lane0 = lane == 0

    def zm(self, v):
        return pltpu.roll(v, 1, 1)

    def zp(self, v):
        return pltpu.roll(v, self.lanes - 1, 1)

    def ym(self, v):
        return pltpu.roll(v, 1, 0)

    def yp(self, v):
        return pltpu.roll(v, self.rows - 1, 0)


class Plane:
    def __init__(self, ln, tx, txn, ty, tz, s, valid=None):
        self.ln = ln
        self.tx, self.txn = tx, txn
        self.ty = jnp.where(ln.row0, 0.0, ty)
        self.tz = jnp.where(ln.lane0, 0.0, tz)
        self.typ = ln.yp(self.ty)
        self.tzp = ln.zp(self.tz)
        e = s * (1.0 / 3.0) + ((tx + txn) + (self.ty + self.typ) + (self.tz + self.tzp))
        if valid is not None:
            e = jnp.where(valid, e, 1.0)
        self.half = 0.5 * e + s * (1.0 / 3.0)
        self.all = 1.5 * e
        self.q = 1.0 / self.all
        self.z1 = self.q * jnp.where(ln.first, self.tz, jnp.where(ln.last, self.tzp, 0.0))
        self.zm = ln.zm(self.z1)
        self.zp = ln.zp(self.z1)

    def toward(self, low):
        return self.tx if low else self.txn

    def inward(self, low):
        return self.txn if low else self.tx

    def edge(self, low):
        self.x1 = self.q * self.toward(low)
        self.o1 = 1.0 - self.z1 - self.x1

    def rim(self):
        return self.tz * self.zm + self.tzp * self.zp

    def along_y(self, v):
        return self.ty * self.ln.ym(v) + self.typ * self.ln.yp(v)


def middle(p, below, above, mz):
    ln = p.ln
    vz = p.half * p.z1 + p.tx * below.z1 + p.txn * above.z1 + p.along_y(p.z1)
    vz = vz + p.tz * jnp.where(ln.first, 1.0 - p.zm, p.zm)
    vz = vz + p.tzp * jnp.where(ln.last, 1.0 - p.zp, p.zp)
    kept = vz * mz
    return p.all - vz, kept, p.all - (vz - kept)


def second(p, edge, inner, low, mz, mx):
    below, above = (edge, inner) if low else (inner, edge)
    ln = p.ln
    first_o = ln.zm(p.z1)
    vz = p.half * p.z1 + p.tx * below.z1 + p.txn * above.z1 + p.along_y(p.z1)
    vz = vz + p.tz * jnp.where(ln.first, 1.0 - first_o, first_o)
    vz = vz + p.tzp * jnp.where(ln.last, 1.0 - p.zp, p.zp)
    vx = p.toward(low) * edge.x1
    kept_z, kept_x = vz * mz, vx * mx
    total = p.all - (vz - kept_z) - (vx - kept_x)
    return p.all - vz - vx, kept_z, kept_x, total


def edge_own(p, inner_o1, inner_z1, outer_x1, low, mz):
    ln = p.ln
    om, op = ln.zm(p.o1), ln.zp(p.o1)
    vo = p.half * p.o1 + p.toward(low) * outer_x1 + p.inward(low) * inner_o1 + p.along_y(p.o1)
    vo = vo + p.tz * jnp.where(ln.first, p.zm, om) + p.tzp * jnp.where(ln.last, p.zp, op)
    vz = p.half * p.z1 + p.inward(low) * inner_z1 + p.along_y(p.z1)
    vz = vz + p.tz * jnp.where(ln.first, om, p.zm) + p.tzp * jnp.where(ln.last, op, p.zp)
    return vo, vz * mz


def edge_total(p, mz):
    rim = p.rim()
    return p.all - (rim - rim * mz)


def edge_spill(p, own, low):
    ln = p.ln
    xm, xp = ln.zm(p.x1), ln.zp(p.x1)
    face = p.toward(low)
    vx = p.half * p.x1 + face * own.o1 + p.along_y(p.x1)
    vx = vx + p.tz * jnp.where(ln.first, 0.0, xm) + p.tzp * jnp.where(ln.last, 0.0, xp)
    vd = face * own.z1 + p.tz * jnp.where(ln.first, xm, 0.0) + p.tzp * jnp.where(ln.last, xp, 0.0)
    return vx, vd


def second_spill(p, edge, low, mz, mx):
    vx = p.toward(low) * edge.x1
    kept = vx * mx
    return kept, edge_total(p, mz) - (vx - kept)


def store(ln, dst, layer, plane, blocks, own, other, total):
    scale = 1.0 / total
    own = own * scale
    other = jnp.zeros_like(own) if other is None else other * scale
    for k in range(blocks):
        dst[layer, k, plane] = jnp.where(ln.block == k, own, jnp.where(ln.other == k, other, 0.0))


def pack_kernel(
    n, width, axis, tx, ty, tz, s, reach, msg_a, msg_b, masks, faces, held_reach, sems
):
    layers, _, blocks = held_reach.shape
    lanes = masks.shape[-1]
    even = lax.rem(lax.axis_index(axis), 2) == 0

    def planes(down, up):
        pairs = [(tx.at[pl.ds(0, 3)], down.at[pl.ds(0, 3)])]
        for i, a in enumerate((ty, tz, s)):
            pairs.append((a.at[pl.ds(0, 2)], down.at[pl.ds(3 + 2 * i, 2)]))
        for i, a in enumerate((tx, ty, tz, s)):
            pairs.append((a.at[pl.ds(n - 2, 2)], up.at[pl.ds(2 * i, 2)]))
        return [pltpu.make_async_copy(src, dst, sems.at[i]) for i, (src, dst) in enumerate(pairs)]

    fetch = pltpu.make_async_copy(reach, held_reach, sems.at[8])
    fetch.start()

    @pl.when(even)
    def _():
        for c in planes(msg_b, msg_a):
            c.start()

    @pl.when(jnp.logical_not(even))
    def _():
        for c in planes(msg_a, msg_b):
            c.start()

    keeps = [
        pltpu.make_async_copy(a, faces.at[i], sems.at[9 + i]) for i, a in enumerate((tx, ty, tz, s))
    ]
    for c in keeps:
        c.start()
    masks[...] = jnp.zeros(masks.shape, jnp.float32)
    lane = lax.broadcasted_iota(jnp.int32, (4, lanes), 1)
    block = lane // width
    local = lane - block * width
    fetch.wait()
    for layer in range(layers):
        r = jnp.zeros((4, lanes), jnp.int32)
        for k in range(blocks):
            r = jnp.where(block == k, held_reach[layer, :, k : k + 1], r)
        low = pltpu.roll(r, width, 1)
        high = pltpu.roll(r, lanes - width, 1)
        near = jnp.where(
            local[0:1] < width // 2,
            jnp.where(low[3:4] >= local[0:1] + 1, 1.0, 0.0),
            jnp.where(high[2:3] >= width - local[0:1], 1.0, 0.0),
        )
        masks[layer, 0:1] = near
        masks[layer, 1:3] = jnp.where(r[0:2] >= 2, 1.0, 0.0)

    def finish(down, up):
        down[9, 0:TAIL] = masks[0]
        up[8, 0:TAIL] = masks[layers - 1]
        for c in planes(down, up):
            c.wait()

    @pl.when(even)
    def _():
        finish(msg_b, msg_a)

    @pl.when(jnp.logical_not(even))
    def _():
        finish(msg_a, msg_b)

    for c in keeps:
        c.wait()


def bulk_kernel(width, blocks, faces, masks, out, zeros, buf, sems):
    layers = masks.shape[0]
    rows, lanes = faces.shape[2:]
    zeros[...] = jnp.zeros(zeros.shape, jnp.float32)
    depth = zeros.shape[0]
    clears = []
    for layer in range(layers):
        for k in range(blocks):
            for start in (0, 3 * width - depth):
                sem = sems.at[len(clears)]
                c = pltpu.make_async_copy(zeros, out.at[layer, k, pl.ds(start, depth)], sem)
                c.start()
                clears.append(c)
    ln = Lanes((rows, lanes), width)

    def plane(p):
        return Plane(ln, faces[0, p], faces[0, p + 1], faces[1, p], faces[2, p], faces[3, p])

    sends = []
    for layer in range(layers):
        base = layer * width
        mz = masks[layer, 0:1]
        low, high = layer == 0, layer == layers - 1
        origin = base - width
        if not low:
            ma = masks[layer - 1, 0:1]
            to_above, to_below = masks[layer - 1, 2:3], masks[layer, 1:2]
            a3, a2, a1 = (plane(base - i) for i in (3, 2, 1))
            b0, b1, b2 = (plane(base + i) for i in (0, 1, 2))
            a1.edge(False)
            b0.edge(True)
            prev = origin - width
            put = functools.partial(store, ln, buf)
            vo, vz, vx, total = second(a2, a1, a3, False, ma, to_below)
            put(layer - 1, base - 2 - prev - (width - 2), blocks, vo, vz, total)
            put(layer, base - 2 - origin - (width - 2), blocks, vx, None, total)
            vo, vz = edge_own(a1, 1.0 - a2.z1, a2.z1, b0.x1, False, ma)
            vx, vd = edge_spill(a1, b0, False)
            total = edge_total(a1, ma)
            put(layer - 1, base - 1 - prev - (width - 2), blocks, vo, vz, total)
            put(layer, base - 1 - origin - (width - 2), blocks, vx, vd, total)
            vo, vz = edge_own(b0, 1.0 - b1.z1, b1.z1, a1.x1, True, mz)
            vx, vd = edge_spill(b0, a1, True)
            total = edge_total(b0, mz)
            put(layer, base - origin - (width - 2), blocks, vo, vz, total)
            put(layer - 1, base - prev - (width - 2), blocks, vx, vd, total)
            vo, vz, vx, total = second(b1, b0, b2, True, mz, to_above)
            put(layer, base + 1 - origin - (width - 2), blocks, vo, vz, total)
            put(layer - 1, base + 1 - prev - (width - 2), blocks, vx, None, total)
            sends.append(send_layer(layer - 1, layers, width, blocks, buf, out, sems))
        planes = [plane(base + a) for a in range(1, width - 1)]
        for a in range(2, width - 2):
            vo, vz, total = middle(planes[a - 1], planes[a - 2], planes[a], mz)
            store(ln, buf, layer, a + 2, blocks, vo, vz, total)
        if high:
            sends.append(send_layer(layer, layers, width, blocks, buf, out, sems))
    for group in sends:
        for c in group:
            c.wait()
    for c in clears:
        c.wait()


def span(layer, layers, width):
    return (4 if layer == 0 else 0), (width if layer == layers - 1 else width + 4)


def send_layer(layer, layers, width, blocks, buf, out, sems):
    low, high = span(layer, layers, width)
    group = []
    for k in range(blocks):
        c = pltpu.make_async_copy(
            buf.at[layer, k, pl.ds(low, high - low)],
            out.at[layer, k, pl.ds(width - 2 + low, high - low)],
            sems.at[(2 * layers + layer) * blocks + k],
        )
        c.start()
        group.append(c)
    return group


def edge_kernel(
    width, blocks, axis, count, faces, masks, got_a, got_b, held, out, buf, sems
):
    del held
    layers = masks.shape[0]
    me = lax.axis_index(axis)
    even = lax.rem(me, 2) == 0
    n = faces.shape[1]
    lo, hi = faces, faces.at[:, pl.ds(n - 4, 4)]

    class Got:
        def __init__(self, at_even, at_odd):
            self.at_even, self.at_odd = at_even, at_odd

        def __getitem__(self, where):
            return jnp.where(even, self.at_even[where], self.at_odd[where])

    lob, hib = Got(got_b, got_a), Got(got_a, got_b)
    rows, lanes = lo.shape[2:]
    ln = Lanes((rows, lanes), width)
    put = functools.partial(store, ln, buf)
    low_ok, high_ok = me > 0, me < count - 1

    tx0 = jnp.where(low_ok, lo[0, 0], 0.0)
    a2 = Plane(ln, lob[0], lob[1], lob[2], lob[4], lob[6], low_ok)
    a1 = Plane(ln, lob[1], tx0, lob[3], lob[5], lob[7], low_ok)
    ma, to_above = lob[8, 0:1], lob[8, 2:3]
    mz, to_below = masks[0, 0:1], masks[0, 1:2]
    b0 = Plane(ln, tx0, lo[0, 1], lo[1, 0], lo[2, 0], lo[3, 0])
    b1, b2 = (Plane(ln, lo[0, i], lo[0, i + 1], lo[1, i], lo[2, i], lo[3, i]) for i in (1, 2))
    a1.edge(False)
    b0.edge(True)
    vx, total = second_spill(a2, a1, False, ma, to_below)
    put(0, 0, blocks, vx, None, total)
    vx, vd = edge_spill(a1, b0, False)
    put(0, 1, blocks, vx, vd, edge_total(a1, ma))
    vo, vz = edge_own(b0, 1.0 - b1.z1, b1.z1, a1.x1, True, mz)
    put(0, 2, blocks, vo, vz, edge_total(b0, mz))
    vo, vz, _, total = second(b1, b0, b2, True, mz, to_above)
    put(0, 3, blocks, vo, vz, total)
    sends = []

    def send(side, layer, start):
        for k in range(blocks):
            c = pltpu.make_async_copy(
                buf.at[side, k], out.at[layer, k, pl.ds(start, 4)], sems.at[len(sends)]
            )
            c.start()
            sends.append(c)

    send(0, 0, width - 2)

    mz, to_above = masks[layers - 1, 0:1], masks[layers - 1, 2:3]
    mb, to_below = hib[9, 0:1], hib[9, 1:2]
    a3, a2 = (Plane(ln, hi[0, i], hi[0, i + 1], hi[1, i], hi[2, i], hi[3, i]) for i in (1, 2))
    a1 = Plane(ln, hi[0, 3], hib[0], hi[1, 3], hi[2, 3], hi[3, 3])
    b0 = Plane(ln, hib[0], hib[1], hib[3], hib[5], hib[7], high_ok)
    b1 = Plane(ln, hib[1], hib[2], hib[4], hib[6], hib[8], high_ok)
    a1.edge(False)
    b0.edge(True)
    vo, vz, _, total = second(a2, a1, a3, False, mz, to_below)
    put(1, 0, blocks, vo, vz, total)
    vo, vz = edge_own(a1, 1.0 - a2.z1, a2.z1, b0.x1, False, mz)
    put(1, 1, blocks, vo, vz, edge_total(a1, mz))
    vx, vd = edge_spill(b0, a1, True)
    put(1, 2, blocks, vx, vd, edge_total(b0, mb))
    vx, total = second_spill(b1, b0, True, mb, to_above)
    put(1, 3, blocks, vx, None, total)
    send(1, layers - 1, 2 * width - 2)
    for c in sends:
        c.wait()


def swaps(firsts):
    return [pair for i in firsts for pair in ((i, i + 1), (i + 1, i))]


def on_device(trans_east, trans_north, trans_up, storage, support_reach, *, axis, count):
    layers, blocks, _ = support_reach.shape
    n, rows, lanes = trans_east.shape
    width = n // layers
    f32 = jnp.float32
    anywhere = pl.BlockSpec(memory_space=pl.ANY)
    vmem = pl.BlockSpec(memory_space=pltpu.VMEM)
    params = pltpu.CompilerParams(vmem_limit_bytes=16 * 2**20)
    outside = tuple(
        pltpu.with_memory_space_constraint(x, pltpu.HBM)
        for x in (trans_east, trans_north, trans_up, storage)
    )
    reach = jnp.transpose(support_reach, (0, 2, 1))
    reach = pltpu.with_memory_space_constraint(reach, pltpu.HBM)
    message = pltpu.VMEM((10, rows, lanes), f32)
    msg_a, msg_b, masks, faces = pl.pallas_call(
        functools.partial(pack_kernel, n, width, axis),
        out_shape=(
            message,
            message,
            pltpu.VMEM((layers, TAIL, lanes), f32),
            pltpu.VMEM((4, n, rows, lanes), f32),
        ),
        in_specs=[anywhere] * 5,
        out_specs=(vmem,) * 4,
        scratch_shapes=[
            pltpu.VMEM((layers, 4, blocks), jnp.int32),
            pltpu.SemaphoreType.DMA((13,)),
        ],
        compiler_params=params,
        name="pack",
    )(*outside, reach)
    got_b = lax.ppermute(msg_b, axis, swaps(range(1, count - 1, 2)))
    got_a = lax.ppermute(msg_a, axis, swaps(range(0, count - 1, 2)))

    out_shape = jax.ShapeDtypeStruct((layers, blocks, 3 * width, rows, lanes), f32)
    bulk = pl.pallas_call(
        functools.partial(bulk_kernel, width, blocks),
        out_shape=out_shape,
        in_specs=[vmem] * 2,
        out_specs=anywhere,
        scratch_shapes=[
            pltpu.VMEM((width - 2, rows, lanes), f32),
            pltpu.VMEM((layers, blocks, width + 4, rows, lanes), f32),
            pltpu.SemaphoreType.DMA((3 * layers * blocks,)),
        ],
        compiler_params=params,
        cost_estimate=pl.CostEstimate(flops=10**7, bytes_accessed=7 * 10**6, transcendentals=0),
        name="bulk",
    )(faces, masks)
    return pl.pallas_call(
        functools.partial(edge_kernel, width, blocks, axis, count),
        out_shape=out_shape,
        in_specs=[vmem] * 4 + [anywhere],
        out_specs=anywhere,
        scratch_shapes=[
            pltpu.VMEM((2, blocks, 4, rows, lanes), f32),
            pltpu.SemaphoreType.DMA((2 * blocks,)),
        ],
        input_output_aliases={4: 0},
        compiler_params=params,
        cost_estimate=pl.CostEstimate(flops=10**6, bytes_accessed=10**6, transcendentals=0),
        name="edges",
    )(faces, masks, got_a, got_b, bulk)


def solution(mesh):
    spread = P(("groups", "blk"))
    return jax.shard_map(
        functools.partial(on_device, axis="blk", count=mesh.shape["blk"]),
        mesh=mesh,
        in_specs=(spread,) * 5,
        out_specs=spread,
        check_vma=False,
    )
```

profile of v0, /device:TPU:1, one launch (start us, length us, event | category | flops | bytes accessed | tf_op | source)
XLA Modules:
  0.0 11.0 jit_solution(6352340160846733174)
XLA Ops:
  0.0 1.4 %pack.1 = (f32[10,16,128]{2,1,0:T(8,128)S(1)}, f32[10,16,128]{2,1,0:T(8,128)S(1)}, f32[2,8,128]{2,1,0:T(8,128)S(1)}, f32[4,32,16,128]{3,2,1,0:T(8,128)S(1)}) custom-call(f32[32,16,128]{2,1,0:T(8,128)} %tx.1, f32[32,16,128]{2,1,0:T(8,128)} %ty.1, f32[32,16,128]{2,1,0:T(8,128)} %tz.1, f32[32,16,128]{2,1,0:T(8,128)} %s.1, s32[2,4,8]{2,1,0:T(4,128)} %bitcast.1), custom_call_target="tpu_custom_call" | custom-call | tf_op jit(solution)/shard_map/pack/pallas_call | solution.py:382
  1.5 0.1 %collective-permute-start = (f32[10,16,128]{2,1,0:T(8,128)S(1)}, f32[10,16,128]{2,1,0:T(8,128)S(1)}, u32[]{:S(2)}, u32[]{:S(2)}) collective-permute-start(f32[10,16,128]{2,1,0:T(8,128)S(1)} %get-tuple-element.11), channel_id=1, source_target_pairs={{0,1},{1,0},{2,3},{3,2},{4,5},{5,4},{6,7},{7,6},{8,9},{9,8},{10,11... | collective-permute-start | bytes 245768 | tf_op jit(solution)/shard_map/ppermute | solution.py:400
  1.6 4.5 %collective-permute-start.1 = (f32[10,16,128]{2,1,0:T(8,128)S(1)}, f32[10,16,128]{2,1,0:T(8,128)S(1)}, u32[]{:S(2)}, u32[]{:S(2)}) collective-permute-start(f32[10,16,128]{2,1,0:T(8,128)S(1)} %get-tuple-element.12), channel_id=1, source_target_pairs={{1,2},{2,1},{3,4},{4,3},{5,6},{6,5},{7,8},{8,7},{9,10},{10,9},{11,... | collective-permute-start | bytes 245768 | tf_op jit(solution)/shard_map/ppermute | solution.py:399
  6.1 3.8 %bulk.1.held = f32[2,8,48,16,128]{4,3,2,1,0:T(8,128)} custom-call(f32[4,32,16,128]{3,2,1,0:T(8,128)S(1)} %get-tuple-element.9.faces, f32[2,8,128]{2,1,0:T(8,128)S(1)} %get-tuple-element.10.masks), custom_call_target="tpu_custom_call" | custom-call | flops 10000000 | bytes 7000000 | tf_op jit(solution)/shard_map/bulk/pallas_call | solution.py:403
  9.8 0.0 collective-permute-done.got_a
  9.9 0.0 collective-permute-done.1.got_b
  9.9 1.1 %edges.1 = f32[2,8,48,16,128]{4,3,2,1,0:T(8,128)} custom-call(f32[4,32,16,128]{3,2,1,0:T(8,128)S(1)} %get-tuple-element.9.faces, f32[2,8,128]{2,1,0:T(8,128)S(1)} %get-tuple-element.10.masks, f32[10,16,128]{2,1,0:T(8,128)S(1)} %collective-permute-done.got_a, f32[10,16,128]{2,1,0:T(8,128)S(1)} %collective-permute-done.1.got_b, ...), custom_call_target="tpu_custom_call", output_to_operand_aliasing={{}: (4, {})} | custom-call | flops 1000000 | bytes 1000000 | tf_op jit(solution)/shard_map/edges/pallas_call | solution.py:417
Async XLA Ops:
  1.5 8.4 %collective-permute-start = (f32[10,16,128]{2,1,0:T(8,128)S(1)}, f32[10,16,128]{2,1,0:T(8,128)S(1)}, u32[]{:S(2)}, u32[]{:S(2)}) collective-permute-start(f32[10,16,128]{2,1,0:T(8,128)S(1)} %get-tuple-element.11), channel_id=1, source_target_pairs={{0,1},{1,0},{2,3},{3,2},{4,5},{5,4},{6,7},{7,6},{8,9},{9,8},{10,11... | collective-permute-start | bytes 245768 | tf_op jit(solution)/shard_map/ppermute | solution.py:400
  1.6 8.3 %collective-permute-start.1 = (f32[10,16,128]{2,1,0:T(8,128)S(1)}, f32[10,16,128]{2,1,0:T(8,128)S(1)}, u32[]{:S(2)}, u32[]{:S(2)}) collective-permute-start(f32[10,16,128]{2,1,0:T(8,128)S(1)} %get-tuple-element.12), channel_id=1, source_target_pairs={{1,2},{2,1},{3,4},{4,3},{5,6},{6,5},{7,8},{8,7},{9,10},{10,9},{11,... | collective-permute-start | bytes 245768 | tf_op jit(solution)/shard_map/ppermute | solution.py:399
where the time goes:
time: 11.2 us; the launch traced here: 11 us
  Pallas kernels  6.35 us (57%)
  starting transfers between devices  4.62 us (41%)
    ppermute x1, starting transfers between devices, on_device(): got_b = lax.ppermute(msg_b, axis, swaps(range(1, count - 1, 2)))  4.49 us
    pallas_call x1, Pallas kernels, on_device(): pl.pallas_call(functools.partial(bulk_kernel, width, blocks), out_shape=o...  3.76 us
    pallas_call x1, Pallas kernels, on_device(): pl.pallas_call(functools.partial(pack_kernel, n, width, axis), out_shape=...  1.44 us
    pallas_call x1, Pallas kernels, on_device(): pl.pallas_call(functools.partial(edge_kernel, width, blocks, axis, count)...  1.14 us
  transfers between devices with their start and end apart: 2, of which 0 were waited for; matrix products, arithmetic and copies ran while one was open for 0% of the time, Pallas kernels for 34%

commit v1 on v0

--- a/solution.py
+++ b/solution.py
@@ -288,12 +288,14 @@
 
 
 def edge_kernel(
-    width, blocks, axis, count, faces, masks, got_a, got_b, held, out, buf, sems
+    width, blocks, axis, count, faces, masks, got_a, pair_b, held, out, buf, got_b, sems
 ):
     del held
     layers = masks.shape[0]
     me = lax.axis_index(axis)
     even = lax.rem(me, 2) == 0
+    fetch = pltpu.make_async_copy(pair_b.at[lax.rem(me, 2)], got_b, sems.at[2 * blocks])
+    fetch.start()
     n = faces.shape[1]
     lo, hi = faces, faces.at[:, pl.ds(n - 4, 4)]
 
@@ -305,6 +307,7 @@
             return jnp.where(even, self.at_even[where], self.at_odd[where])
 
     lob, hib = Got(got_b, got_a), Got(got_a, got_b)
+    fetch.wait()
     rows, lanes = lo.shape[2:]
     ln = Lanes((rows, lanes), width)
     put = functools.partial(store, ln, buf)
@@ -342,8 +345,9 @@
     mz, to_above = masks[layers - 1, 0:1], masks[layers - 1, 2:3]
     mb, to_below = hib[9, 0:1], hib[9, 1:2]
     a3, a2 = (Plane(ln, hi[0, i], hi[0, i + 1], hi[1, i], hi[2, i], hi[3, i]) for i in (1, 2))
-    a1 = Plane(ln, hi[0, 3], hib[0], hi[1, 3], hi[2, 3], hi[3, 3])
-    b0 = Plane(ln, hib[0], hib[1], hib[3], hib[5], hib[7], high_ok)
+    txn = jnp.where(high_ok, hib[0], 0.0)
+    a1 = Plane(ln, hi[0, 3], txn, hi[1, 3], hi[2, 3], hi[3, 3])
+    b0 = Plane(ln, txn, hib[1], hib[3], hib[5], hib[7], high_ok)
     b1 = Plane(ln, hib[1], hib[2], hib[4], hib[6], hib[8], high_ok)
     a1.edge(False)
     b0.edge(True)
@@ -362,6 +366,10 @@
 
 def swaps(firsts):
     return [pair for i in firsts for pair in ((i, i + 1), (i + 1, i))]
+
+
+def pairs(first, count):
+    return [[i % count, (i + 1) % count] for i in range(first, first + count, 2)]
 
 
 def on_device(trans_east, trans_north, trans_up, storage, support_reach, *, axis, count):
@@ -396,7 +404,7 @@
         compiler_params=params,
         name="pack",
     )(*outside, reach)
-    got_b = lax.ppermute(msg_b, axis, swaps(range(1, count - 1, 2)))
+    got_b = lax.all_gather(msg_b, axis, axis_index_groups=pairs(1, count))
     got_a = lax.ppermute(msg_a, axis, swaps(range(0, count - 1, 2)))
 
     out_shape = jax.ShapeDtypeStruct((layers, blocks, 3 * width, rows, lanes), f32)
@@ -417,17 +425,18 @@
     return pl.pallas_call(
         functools.partial(edge_kernel, width, blocks, axis, count),
         out_shape=out_shape,
-        in_specs=[vmem] * 4 + [anywhere],
+        in_specs=[vmem] * 3 + [anywhere] * 2,
         out_specs=anywhere,
         scratch_shapes=[
             pltpu.VMEM((2, blocks, 4, rows, lanes), f32),
-            pltpu.SemaphoreType.DMA((2 * blocks,)),
+            pltpu.VMEM((10, rows, lanes), f32),
+            pltpu.SemaphoreType.DMA((2 * blocks + 1,)),
         ],
         input_output_aliases={4: 0},
         compiler_params=params,
         cost_estimate=pl.CostEstimate(flops=10**6, bytes_accessed=10**6, transcendentals=0),
         name="edges",
-    )(faces, masks, got_a, got_b, bulk)
+    )(faces, masks, got_a, pltpu.with_memory_space_constraint(got_b, pltpu.HBM), bulk)
 
 
 def solution(mesh):

time: 11.2 us -> 16.5 us (1.47)
  the two profiles are of different devices: /device:TPU:1 before, /device:TPU:0 now
where the time goes in v1:
time: 16.5 us; the launch traced here: 16.3 us
  blocking collectives  8.55 us (52%)
  Pallas kernels  7.24 us (44%)
  starting transfers between devices  0.52 us (3%)
    all_gather x1, blocking collectives, on_device(): got_b = lax.all_gather(msg_b, axis, axis_index_groups=pairs(1, count))  8.55 us
    pallas_call x1, Pallas kernels, on_device(): pl.pallas_call(functools.partial(bulk_kernel, width, blocks), out_shape=o...  3.76 us
    pallas_call x1, Pallas kernels, on_device(): pl.pallas_call(functools.partial(edge_kernel, width, blocks, axis, count)...  2.04 us
    pallas_call x1, Pallas kernels, on_device(): pl.pallas_call(functools.partial(pack_kernel, n, width, axis), out_shape=...  1.44 us
    ppermute x1, starting transfers between devices, on_device(): got_a = lax.ppermute(msg_a, axis, swaps(range(0, count - 1, 2)))  0.52 us
  transfers between devices with their start and end apart: 1, of which 0 were waited for; matrix products, arithmetic and copies ran while one was open for 0% of the time, Pallas kernels for 23%

profile of v1, /device:TPU:0, one launch (start us, length us, event | category | flops | bytes accessed | tf_op | source)
XLA Modules:
  0.0 16.3 jit_solution(1003727345932286779)
XLA Ops:
  0.0 1.4 %pack.1 = (f32[10,16,128]{2,1,0:T(8,128)S(1)}, f32[10,16,128]{2,1,0:T(8,128)S(1)}, f32[2,8,128]{2,1,0:T(8,128)S(1)}, f32[4,32,16,128]{3,2,1,0:T(8,128)S(1)}) custom-call(f32[32,16,128]{2,1,0:T(8,128)} %tx.1, f32[32,16,128]{2,1,0:T(8,128)} %ty.1, f32[32,16,128]{2,1,0:T(8,128)} %tz.1, f32[32,16,128]{2,1,0:T(8,128)} %s.1, s32[2,4,8]{2,1,0:T(4,128)} %bitcast.3), custom_call_target="tpu_custom_call" | custom-call | tf_op jit(solution)/shard_map/pack/pallas_call | solution.py:390
  1.5 0.5 %collective-permute-start = (f32[10,16,128]{2,1,0:T(8,128)S(1)}, f32[10,16,128]{2,1,0:T(8,128)S(1)}, u32[]{:S(2)}, u32[]{:S(2)}) collective-permute-start(f32[10,16,128]{2,1,0:T(8,128)S(1)} %get-tuple-element.11), channel_id=1, source_target_pairs={{0,1},{1,0},{2,3},{3,2},{4,5},{5,4},{6,7},{7,6},{8,9},{9,8},{10,11... | collective-permute-start | bytes 245768 | tf_op jit(solution)/shard_map/ppermute | solution.py:408
  2.0 3.8 %bulk.1.held = f32[2,8,48,16,128]{4,3,2,1,0:T(8,128)} custom-call(f32[4,32,16,128]{3,2,1,0:T(8,128)S(1)} %get-tuple-element.9.faces, f32[2,8,128]{2,1,0:T(8,128)S(1)} %get-tuple-element.10.masks), custom_call_target="tpu_custom_call" | custom-call | flops 10000000 | bytes 7000000 | tf_op jit(solution)/shard_map/bulk/pallas_call | solution.py:411
  5.7 8.5 %all-gather = f32[20,16,128]{2,1,0:T(8,128)} all-gather(f32[10,16,128]{2,1,0:T(8,128)S(1)} %get-tuple-element.12), channel_id=2, replica_groups={{1,2},{3,4},{5,6},{7,8},{9,10},{11,12},{13,14},{15,0},{17,18},{19,20},{..., dimensions={0}, use_global_device_ids=true | all-gather | bytes 245760 | tf_op jit(solution)/shard_map/all_gather | solution.py:407
  14.3 0.0 collective-permute-done.got_a
  14.3 2.0 %edges.1 = f32[2,8,48,16,128]{4,3,2,1,0:T(8,128)} custom-call(f32[4,32,16,128]{3,2,1,0:T(8,128)S(1)} %get-tuple-element.9.faces, f32[2,8,128]{2,1,0:T(8,128)S(1)} %get-tuple-element.10.masks, f32[10,16,128]{2,1,0:T(8,128)S(1)} %collective-permute-done.got_a, f32[2,10,16,128]{3,2,1,0:T(8,128)} %bitcast.2, ...), custom_call_target="tpu_custom_call", output_to_operand_aliasing={{}: (4, {})} | custom-call | flops 1000000 | bytes 1000000 | tf_op jit(solution)/shard_map/edges/pallas_call | solution.py:425
Async XLA Ops:
  1.5 12.8 %collective-permute-start = (f32[10,16,128]{2,1,0:T(8,128)S(1)}, f32[10,16,128]{2,1,0:T(8,128)S(1)}, u32[]{:S(2)}, u32[]{:S(2)}) collective-permute-start(f32[10,16,128]{2,1,0:T(8,128)S(1)} %get-tuple-element.11), channel_id=1, source_target_pairs={{0,1},{1,0},{2,3},{3,2},{4,5},{5,4},{6,7},{7,6},{8,9},{9,8},{10,11... | collective-permute-start | bytes 245768 | tf_op jit(solution)/shard_map/ppermute | solution.py:408

commit v2 on v0

--- a/solution.py
+++ b/solution.py
@@ -9,6 +9,8 @@
 
 
 TAIL = 8
+CHUNK = 4
+SPLIT = 2
 
 
 class Lanes:
@@ -141,33 +143,11 @@
 ):
     layers, _, blocks = held_reach.shape
     lanes = masks.shape[-1]
-    even = lax.rem(lax.axis_index(axis), 2) == 0
-
-    def planes(down, up):
-        pairs = [(tx.at[pl.ds(0, 3)], down.at[pl.ds(0, 3)])]
-        for i, a in enumerate((ty, tz, s)):
-            pairs.append((a.at[pl.ds(0, 2)], down.at[pl.ds(3 + 2 * i, 2)]))
-        for i, a in enumerate((tx, ty, tz, s)):
-            pairs.append((a.at[pl.ds(n - 2, 2)], up.at[pl.ds(2 * i, 2)]))
-        return [pltpu.make_async_copy(src, dst, sems.at[i]) for i, (src, dst) in enumerate(pairs)]
-
-    fetch = pltpu.make_async_copy(reach, held_reach, sems.at[8])
-    fetch.start()
-
-    @pl.when(even)
-    def _():
-        for c in planes(msg_b, msg_a):
-            c.start()
-
-    @pl.when(jnp.logical_not(even))
-    def _():
-        for c in planes(msg_a, msg_b):
-            c.start()
-
-    keeps = [
-        pltpu.make_async_copy(a, faces.at[i], sems.at[9 + i]) for i, a in enumerate((tx, ty, tz, s))
+    fetch = pltpu.make_async_copy(reach, held_reach, sems.at[4])
+    copies = [
+        pltpu.make_async_copy(a, faces.at[i], sems.at[i]) for i, a in enumerate((tx, ty, tz, s))
     ]
-    for c in keeps:
+    for c in [fetch] + copies:
         c.start()
     masks[...] = jnp.zeros(masks.shape, jnp.float32)
     lane = lax.broadcasted_iota(jnp.int32, (4, lanes), 1)
@@ -187,104 +167,116 @@
         )
         masks[layer, 0:1] = near
         masks[layer, 1:3] = jnp.where(r[0:2] >= 2, 1.0, 0.0)
-
-    def finish(down, up):
-        down[9, 0:TAIL] = masks[0]
-        up[8, 0:TAIL] = masks[layers - 1]
-        for c in planes(down, up):
-            c.wait()
-
-    @pl.when(even)
-    def _():
-        finish(msg_b, msg_a)
-
-    @pl.when(jnp.logical_not(even))
-    def _():
-        finish(msg_a, msg_b)
-
-    for c in keeps:
+    even = lax.rem(lax.axis_index(axis), 2) == 0
+
+    def put(tile, up, down):
+        up, down = (v.reshape(-1, TAIL, lanes) for v in (up, down))
+        where = pl.ds(tile, up.shape[0])
+        msg_a[where] = jnp.where(even, up, down)
+        msg_b[where] = jnp.where(even, down, up)
+
+    put(0, masks[layers - 1], masks[0])
+    for c in copies:
         c.wait()
+    for i in range(4):
+        for j in range(2):
+            put(1 + 2 * (2 * i + j), faces[i, n - 2 + j], faces[i, j])
+    put(17, faces[0, n - 1], faces[0, 2])
 
 
 def bulk_kernel(width, blocks, faces, masks, out, zeros, buf, sems):
     layers = masks.shape[0]
     rows, lanes = faces.shape[2:]
+    depth = zeros.shape[0]
     zeros[...] = jnp.zeros(zeros.shape, jnp.float32)
-    depth = zeros.shape[0]
-    clears = []
-    for layer in range(layers):
-        for k in range(blocks):
-            for start in (0, 3 * width - depth):
-                sem = sems.at[len(clears)]
-                c = pltpu.make_async_copy(zeros, out.at[layer, k, pl.ds(start, depth)], sem)
-                c.start()
-                clears.append(c)
+
+    def clears(k):
+        for layer in range(layers):
+            for side, start in enumerate((0, 3 * width - depth)):
+                sem = sems.at[(layer * 2 + side) * blocks + k]
+                yield pltpu.make_async_copy(zeros, out.at[layer, k, pl.ds(start, depth)], sem)
+
+    def send(layer, start, planes, index):
+        for i in range(SPLIT):
+            few = pl.ds(i * (blocks // SPLIT), blocks // SPLIT)
+            yield pltpu.make_async_copy(
+                buf.at[layer, few, pl.ds(start, planes)],
+                out.at[layer, few, pl.ds(width - 2 + start, planes)],
+                sems.at[2 * layers * blocks + index * SPLIT + i],
+            )
+
+    @pl.loop(0, blocks)
+    def _(k):
+        for c in clears(k):
+            c.start()
+
     ln = Lanes((rows, lanes), width)
 
     def plane(p):
         return Plane(ln, faces[0, p], faces[0, p + 1], faces[1, p], faces[2, p], faces[3, p])
 
-    sends = []
+    chunks = (width - 4) // CHUNK
+
+    @pl.loop(0, layers * chunks)
+    def _(i):
+        layer = i // chunks
+        first = 2 + (i - layer * chunks) * CHUNK
+        planes = [plane(layer * width + first + j) for j in range(-1, CHUNK + 1)]
+        mz = masks[layer, 0:1]
+        for j in range(CHUNK):
+            vo, vz, total = middle(planes[j + 1], planes[j], planes[j + 2], mz)
+            store(ln, buf, layer, first + j + 2, blocks, vo, vz, total)
+        for c in send(layer, first + 2, CHUNK, i):
+            c.start()
+
+    @pl.loop(1, layers)
+    def _(layer):
+        base = layer * width
+        ma, mb = masks[layer - 1, 0:1], masks[layer, 0:1]
+        to_above, to_below = masks[layer - 1, 2:3], masks[layer, 1:2]
+        a3, a2, a1 = (plane(base - i) for i in (3, 2, 1))
+        b0, b1, b2 = (plane(base + i) for i in (0, 1, 2))
+        a1.edge(False)
+        b0.edge(True)
+        low = functools.partial(store, ln, buf, layer - 1)
+        high = functools.partial(store, ln, buf, layer)
+        vo, vz, vx, total = second(a2, a1, a3, False, ma, to_below)
+        low(width, blocks, vo, vz, total)
+        high(0, blocks, vx, None, total)
+        vo, vz = edge_own(a1, 1.0 - a2.z1, a2.z1, b0.x1, False, ma)
+        vx, vd = edge_spill(a1, b0, False)
+        total = edge_total(a1, ma)
+        low(width + 1, blocks, vo, vz, total)
+        high(1, blocks, vx, vd, total)
+        vo, vz = edge_own(b0, 1.0 - b1.z1, b1.z1, a1.x1, True, mb)
+        vx, vd = edge_spill(b0, a1, True)
+        total = edge_total(b0, mb)
+        high(2, blocks, vo, vz, total)
+        low(width + 2, blocks, vx, vd, total)
+        vo, vz, vx, total = second(b1, b0, b2, True, mb, to_above)
+        high(3, blocks, vo, vz, total)
+        low(width + 3, blocks, vx, None, total)
+        index = layers * chunks + 2 * (layer - 1)
+        for c in send(layer - 1, width, 4, index):
+            c.start()
+        for c in send(layer, 0, 4, index + 1):
+            c.start()
+
     for layer in range(layers):
-        base = layer * width
-        mz = masks[layer, 0:1]
-        low, high = layer == 0, layer == layers - 1
-        origin = base - width
-        if not low:
-            ma = masks[layer - 1, 0:1]
-            to_above, to_below = masks[layer - 1, 2:3], masks[layer, 1:2]
-            a3, a2, a1 = (plane(base - i) for i in (3, 2, 1))
-            b0, b1, b2 = (plane(base + i) for i in (0, 1, 2))
-            a1.edge(False)
-            b0.edge(True)
-            prev = origin - width
-            put = functools.partial(store, ln, buf)
-            vo, vz, vx, total = second(a2, a1, a3, False, ma, to_below)
-            put(layer - 1, base - 2 - prev - (width - 2), blocks, vo, vz, total)
-            put(layer, base - 2 - origin - (width - 2), blocks, vx, None, total)
-            vo, vz = edge_own(a1, 1.0 - a2.z1, a2.z1, b0.x1, False, ma)
-            vx, vd = edge_spill(a1, b0, False)
-            total = edge_total(a1, ma)
-            put(layer - 1, base - 1 - prev - (width - 2), blocks, vo, vz, total)
-            put(layer, base - 1 - origin - (width - 2), blocks, vx, vd, total)
-            vo, vz = edge_own(b0, 1.0 - b1.z1, b1.z1, a1.x1, True, mz)
-            vx, vd = edge_spill(b0, a1, True)
-            total = edge_total(b0, mz)
-            put(layer, base - origin - (width - 2), blocks, vo, vz, total)
-            put(layer - 1, base - prev - (width - 2), blocks, vx, vd, total)
-            vo, vz, vx, total = second(b1, b0, b2, True, mz, to_above)
-            put(layer, base + 1 - origin - (width - 2), blocks, vo, vz, total)
-            put(layer - 1, base + 1 - prev - (width - 2), blocks, vx, None, total)
-            sends.append(send_layer(layer - 1, layers, width, blocks, buf, out, sems))
-        planes = [plane(base + a) for a in range(1, width - 1)]
-        for a in range(2, width - 2):
-            vo, vz, total = middle(planes[a - 1], planes[a - 2], planes[a], mz)
-            store(ln, buf, layer, a + 2, blocks, vo, vz, total)
-        if high:
-            sends.append(send_layer(layer, layers, width, blocks, buf, out, sems))
-    for group in sends:
-        for c in group:
+        for i in range(chunks):
+            for c in send(layer, 4 + i * CHUNK, CHUNK, layer * chunks + i):
+                c.wait()
+    for layer in range(1, layers):
+        index = layers * chunks + 2 * (layer - 1)
+        for c in send(layer - 1, width, 4, index):
             c.wait()
-    for c in clears:
-        c.wait()
-
-
-def span(layer, layers, width):
-    return (4 if layer == 0 else 0), (width if layer == layers - 1 else width + 4)
-
-
-def send_layer(layer, layers, width, blocks, buf, out, sems):
-    low, high = span(layer, layers, width)
-    group = []
-    for k in range(blocks):
-        c = pltpu.make_async_copy(
-            buf.at[layer, k, pl.ds(low, high - low)],
-            out.at[layer, k, pl.ds(width - 2 + low, high - low)],
-            sems.at[(2 * layers + layer) * blocks + k],
-        )
-        c.start()
-        group.append(c)
-    return group
+        for c in send(layer, 0, 4, index + 1):
+            c.wait()
+
+    @pl.loop(0, blocks)
+    def _(k):
+        for c in clears(k):
+            c.wait()
 
 
 def edge_kernel(
@@ -294,26 +286,30 @@
     layers = masks.shape[0]
     me = lax.axis_index(axis)
     even = lax.rem(me, 2) == 0
-    n = faces.shape[1]
+    n, rows, lanes = faces.shape[1:]
     lo, hi = faces, faces.at[:, pl.ds(n - 4, 4)]
 
     class Got:
         def __init__(self, at_even, at_odd):
             self.at_even, self.at_odd = at_even, at_odd
 
-        def __getitem__(self, where):
-            return jnp.where(even, self.at_even[where], self.at_odd[where])
+        def mask(self, row):
+            return jnp.where(even, self.at_even[0, row : row + 1], self.at_odd[0, row : row + 1])
+
+        def __getitem__(self, place):
+            i, j = place
+            tiles = pl.ds(1 + (rows // TAIL) * (2 * i + j), rows // TAIL)
+            return jnp.where(even, self.at_even[tiles], self.at_odd[tiles]).reshape(rows, lanes)
 
     lob, hib = Got(got_b, got_a), Got(got_a, got_b)
-    rows, lanes = lo.shape[2:]
     ln = Lanes((rows, lanes), width)
     put = functools.partial(store, ln, buf)
     low_ok, high_ok = me > 0, me < count - 1
 
     tx0 = jnp.where(low_ok, lo[0, 0], 0.0)
-    a2 = Plane(ln, lob[0], lob[1], lob[2], lob[4], lob[6], low_ok)
-    a1 = Plane(ln, lob[1], tx0, lob[3], lob[5], lob[7], low_ok)
-    ma, to_above = lob[8, 0:1], lob[8, 2:3]
+    a2 = Plane(ln, lob[0, 0], lob[0, 1], lob[1, 0], lob[2, 0], lob[3, 0], low_ok)
+    a1 = Plane(ln, lob[0, 1], tx0, lob[1, 1], lob[2, 1], lob[3, 1], low_ok)
+    ma, to_above = lob.mask(0), lob.mask(2)
     mz, to_below = masks[0, 0:1], masks[0, 1:2]
     b0 = Plane(ln, tx0, lo[0, 1], lo[1, 0], lo[2, 0], lo[3, 0])
     b1, b2 = (Plane(ln, lo[0, i], lo[0, i + 1], lo[1, i], lo[2, i], lo[3, i]) for i in (1, 2))
@@ -337,14 +333,13 @@
             c.start()
             sends.append(c)
 
-    send(0, 0, width - 2)
 
     mz, to_above = masks[layers - 1, 0:1], masks[layers - 1, 2:3]
-    mb, to_below = hib[9, 0:1], hib[9, 1:2]
+    mb, to_below = hib.mask(0), hib.mask(1)
     a3, a2 = (Plane(ln, hi[0, i], hi[0, i + 1], hi[1, i], hi[2, i], hi[3, i]) for i in (1, 2))
-    a1 = Plane(ln, hi[0, 3], hib[0], hi[1, 3], hi[2, 3], hi[3, 3])
-    b0 = Plane(ln, hib[0], hib[1], hib[3], hib[5], hib[7], high_ok)
-    b1 = Plane(ln, hib[1], hib[2], hib[4], hib[6], hib[8], high_ok)
+    a1 = Plane(ln, hi[0, 3], hib[0, 0], hi[1, 3], hi[2, 3], hi[3, 3])
+    b0 = Plane(ln, hib[0, 0], hib[0, 1], hib[1, 0], hib[2, 0], hib[3, 0], high_ok)
+    b1 = Plane(ln, hib[0, 1], hib[4, 0], hib[1, 1], hib[2, 1], hib[3, 1], high_ok)
     a1.edge(False)
     b0.edge(True)
     vo, vz, _, total = second(a2, a1, a3, False, mz, to_below)
@@ -355,6 +350,7 @@
     put(1, 2, blocks, vx, vd, edge_total(b0, mb))
     vx, total = second_spill(b1, b0, True, mb, to_above)
     put(1, 3, blocks, vx, None, total)
+    send(0, 0, width - 2)
     send(1, layers - 1, 2 * width - 2)
     for c in sends:
         c.wait()
@@ -378,12 +374,12 @@
     )
     reach = jnp.transpose(support_reach, (0, 2, 1))
     reach = pltpu.with_memory_space_constraint(reach, pltpu.HBM)
-    message = pltpu.VMEM((10, rows, lanes), f32)
+    tiles = 1 + 9 * rows // TAIL
     msg_a, msg_b, masks, faces = pl.pallas_call(
         functools.partial(pack_kernel, n, width, axis),
         out_shape=(
-            message,
-            message,
+            pltpu.VMEM((tiles, TAIL, lanes), f32),
+            pltpu.VMEM((tiles + 1, TAIL, lanes), f32),
             pltpu.VMEM((layers, TAIL, lanes), f32),
             pltpu.VMEM((4, n, rows, lanes), f32),
         ),
@@ -391,15 +387,16 @@
         out_specs=(vmem,) * 4,
         scratch_shapes=[
             pltpu.VMEM((layers, 4, blocks), jnp.int32),
-            pltpu.SemaphoreType.DMA((13,)),
+            pltpu.SemaphoreType.DMA((5,)),
         ],
         compiler_params=params,
         name="pack",
     )(*outside, reach)
+    got_a = lax.ppermute(msg_a, axis, swaps(range(0, count - 1, 2)))
     got_b = lax.ppermute(msg_b, axis, swaps(range(1, count - 1, 2)))
-    got_a = lax.ppermute(msg_a, axis, swaps(range(0, count - 1, 2)))
 
     out_shape = jax.ShapeDtypeStruct((layers, blocks, 3 * width, rows, lanes), f32)
+    sends = layers * ((width - 4) // CHUNK) + 2 * (layers - 1)
     bulk = pl.pallas_call(
         functools.partial(bulk_kernel, width, blocks),
         out_shape=out_shape,
@@ -408,7 +405,7 @@
         scratch_shapes=[
             pltpu.VMEM((width - 2, rows, lanes), f32),
             pltpu.VMEM((layers, blocks, width + 4, rows, lanes), f32),
-            pltpu.SemaphoreType.DMA((3 * layers * blocks,)),
+            pltpu.SemaphoreType.DMA((2 * layers * blocks + sends * SPLIT,)),
         ],
         compiler_params=params,
         cost_estimate=pl.CostEstimate(flops=10**7, bytes_accessed=7 * 10**6, transcendentals=0),

time: 11.2 us -> 10.6 us (0.946)
  the two profiles are of different devices: /device:TPU:1 before, /device:TPU:0 now
where the time goes in v2:
time: 10.6 us; the launch traced here: 10.5 us
  Pallas kernels  5.36 us (51%)
  starting transfers between devices  5.06 us (48%)
    ppermute x1, starting transfers between devices, on_device(): got_a = lax.ppermute(msg_a, axis, swaps(range(0, count - 1, 2)))  4.39 us
    pallas_call x1, Pallas kernels, on_device(): pl.pallas_call(functools.partial(bulk_kernel, width, blocks), out_shape=o...  2.94 us
    pallas_call x1, Pallas kernels, on_device(): pl.pallas_call(functools.partial(pack_kernel, n, width, axis), out_shape=...  1.26 us
    pallas_call x1, Pallas kernels, on_device(): pl.pallas_call(functools.partial(edge_kernel, width, blocks, axis, count)...  1.16 us
    ppermute x1, starting transfers between devices, on_device(): got_b = lax.ppermute(msg_b, axis, swaps(range(1, count - 1, 2)))  0.67 us
  transfers between devices with their start and end apart: 2, of which 0 were waited for; matrix products, arithmetic and copies ran while one was open for 0% of the time, Pallas kernels for 28%

profile of v2, /device:TPU:0, one launch (start us, length us, event | category | flops | bytes accessed | tf_op | source)
XLA Modules:
  0.0 10.5 jit_solution(5773441916783940461)
XLA Ops:
  0.0 1.3 %pack.1 = (f32[19,8,128]{2,1,0:T(8,128)S(1)}, f32[20,8,128]{2,1,0:T(8,128)S(1)}, f32[2,8,128]{2,1,0:T(8,128)S(1)}, f32[4,32,16,128]{3,2,1,0:T(8,128)S(1)}) custom-call(f32[32,16,128]{2,1,0:T(8,128)} %tx.1, f32[32,16,128]{2,1,0:T(8,128)} %ty.1, f32[32,16,128]{2,1,0:T(8,128)} %tz.1, f32[32,16,128]{2,1,0:T(8,128)} %s.1, s32[2,4,8]{2,1,0:T(4,128)} %bitcast.1), custom_call_target="tpu_custom_call" | custom-call | tf_op jit(solution)/shard_map/pack/pallas_call | solution.py:378
  1.3 0.7 %collective-permute-start.1 = (f32[20,8,128]{2,1,0:T(8,128)S(1)}, f32[20,8,128]{2,1,0:T(8,128)S(1)}, u32[]{:S(2)}, u32[]{:S(2)}) collective-permute-start(f32[20,8,128]{2,1,0:T(8,128)S(1)} %get-tuple-element.12), channel_id=1, source_target_pairs={{1,2},{2,1},{3,4},{4,3},{5,6},{6,5},{7,8},{8,7},{9,10},{10,9},{11,... | collective-permute-start | bytes 245768 | tf_op jit(solution)/shard_map/ppermute | solution.py:396
  1.9 4.4 %collective-permute-start = (f32[19,8,128]{2,1,0:T(8,128)S(1)}, f32[19,8,128]{2,1,0:T(8,128)S(1)}, u32[]{:S(2)}, u32[]{:S(2)}) collective-permute-start(f32[19,8,128]{2,1,0:T(8,128)S(1)} %get-tuple-element.11), channel_id=1, source_target_pairs={{0,1},{1,0},{2,3},{3,2},{4,5},{5,4},{6,7},{7,6},{8,9},{9,8},{10,11... | collective-permute-start | bytes 233480 | tf_op jit(solution)/shard_map/ppermute | solution.py:395
  6.3 2.9 %bulk.1.held = f32[2,8,48,16,128]{4,3,2,1,0:T(8,128)} custom-call(f32[4,32,16,128]{3,2,1,0:T(8,128)S(1)} %get-tuple-element.9.faces, f32[2,8,128]{2,1,0:T(8,128)S(1)} %get-tuple-element.10.masks), custom_call_target="tpu_custom_call" | custom-call | flops 10000000 | bytes 7000000 | tf_op jit(solution)/shard_map/bulk/pallas_call | solution.py:400
  9.3 0.0 collective-permute-done.got_a
  9.3 0.0 collective-permute-done.1.got_b
  9.3 1.2 %edges.1 = f32[2,8,48,16,128]{4,3,2,1,0:T(8,128)} custom-call(f32[4,32,16,128]{3,2,1,0:T(8,128)S(1)} %get-tuple-element.9.faces, f32[2,8,128]{2,1,0:T(8,128)S(1)} %get-tuple-element.10.masks, f32[19,8,128]{2,1,0:T(8,128)S(1)} %collective-permute-done.got_a, f32[20,8,128]{2,1,0:T(8,128)S(1)} %collective-permute-done.1.got_b, ...), custom_call_target="tpu_custom_call", output_to_operand_aliasing={{}: (4, {})} | custom-call | flops 1000000 | bytes 1000000 | tf_op jit(solution)/shard_map/edges/pallas_call | solution.py:414
Async XLA Ops:
  1.3 8.0 %collective-permute-start.1 = (f32[20,8,128]{2,1,0:T(8,128)S(1)}, f32[20,8,128]{2,1,0:T(8,128)S(1)}, u32[]{:S(2)}, u32[]{:S(2)}) collective-permute-start(f32[20,8,128]{2,1,0:T(8,128)S(1)} %get-tuple-element.12), channel_id=1, source_target_pairs={{1,2},{2,1},{3,4},{4,3},{5,6},{6,5},{7,8},{8,7},{9,10},{10,9},{11,... | collective-permute-start | bytes 245768 | tf_op jit(solution)/shard_map/ppermute | solution.py:396
  1.9 7.3 %collective-permute-start = (f32[19,8,128]{2,1,0:T(8,128)S(1)}, f32[19,8,128]{2,1,0:T(8,128)S(1)}, u32[]{:S(2)}, u32[]{:S(2)}) collective-permute-start(f32[19,8,128]{2,1,0:T(8,128)S(1)} %get-tuple-element.11), channel_id=1, source_target_pairs={{0,1},{1,0},{2,3},{3,2},{4,5},{5,4},{6,7},{7,6},{8,9},{9,8},{10,11... | collective-permute-start | bytes 233480 | tf_op jit(solution)/shard_map/ppermute | solution.py:395

commit v3 on v2

--- a/solution.py
+++ b/solution.py
@@ -9,7 +9,7 @@
 
 
 TAIL = 8
-CHUNK = 4
+CHUNK = 12
 SPLIT = 2
 
 
@@ -77,6 +77,10 @@
         return self.ty * self.ln.ym(v) + self.typ * self.ln.yp(v)
 
 
+def plane_at(ln, faces, p):
+    return Plane(ln, faces[0, p], faces[0, p + 1], faces[1, p], faces[2, p], faces[3, p])
+
+
 def middle(p, below, above, mz):
     ln = p.ln
     vz = p.half * p.z1 + p.tx * below.z1 + p.txn * above.z1 + p.along_y(p.z1)
@@ -124,10 +128,10 @@
     return vx, vd
 
 
-def second_spill(p, edge, low, mz, mx):
-    vx = p.toward(low) * edge.x1
+def second_spill(face, edge, total, mx):
+    vx = face * edge.x1
     kept = vx * mx
-    return kept, edge_total(p, mz) - (vx - kept)
+    return kept, total - (vx - kept)
 
 
 def store(ln, dst, layer, plane, blocks, own, other, total):
@@ -143,12 +147,14 @@
 ):
     layers, _, blocks = held_reach.shape
     lanes = masks.shape[-1]
-    fetch = pltpu.make_async_copy(reach, held_reach, sems.at[4])
-    copies = [
-        pltpu.make_async_copy(a, faces.at[i], sems.at[i]) for i, a in enumerate((tx, ty, tz, s))
-    ]
-    for c in [fetch] + copies:
-        c.start()
+    fetch = pltpu.make_async_copy(reach, held_reach, sems.at[12])
+    fetch.start()
+    copies = []
+    for j, (start, count) in enumerate(((0, 4), (n - 4, 4), (4, n - 8))):
+        for i, a in enumerate((tx, ty, tz, s)):
+            part = pl.ds(start, count)
+            copies.append(pltpu.make_async_copy(a.at[part], faces.at[i, part], sems.at[4 * j + i]))
+            copies[-1].start()
     masks[...] = jnp.zeros(masks.shape, jnp.float32)
     lane = lax.broadcasted_iota(jnp.int32, (4, lanes), 1)
     block = lane // width
@@ -176,12 +182,16 @@
         msg_b[where] = jnp.where(even, down, up)
 
     put(0, masks[layers - 1], masks[0])
-    for c in copies:
+    for c in copies[:8]:
         c.wait()
     for i in range(4):
-        for j in range(2):
-            put(1 + 2 * (2 * i + j), faces[i, n - 2 + j], faces[i, j])
-    put(17, faces[0, n - 1], faces[0, 2])
+        put(1 + 2 * i, faces[i, n - 1], faces[i, 0])
+    put(11, faces[0, n - 1], faces[0, 1])
+    ln = Lanes(faces.shape[2:], width)
+    top, low = plane_at(ln, faces, n - 2), plane_at(ln, faces, 1)
+    put(9, edge_total(top, masks[layers - 1, 0:1]), edge_total(low, masks[0, 0:1]))
+    for c in copies[8:]:
+        c.wait()
 
 
 def bulk_kernel(width, blocks, faces, masks, out, zeros, buf, sems):
@@ -212,9 +222,7 @@
 
     ln = Lanes((rows, lanes), width)
 
-    def plane(p):
-        return Plane(ln, faces[0, p], faces[0, p + 1], faces[1, p], faces[2, p], faces[3, p])
-
+    plane = functools.partial(plane_at, ln, faces)
     chunks = (width - 4) // CHUNK
 
     @pl.loop(0, layers * chunks)
@@ -296,9 +304,8 @@
         def mask(self, row):
             return jnp.where(even, self.at_even[0, row : row + 1], self.at_odd[0, row : row + 1])
 
-        def __getitem__(self, place):
-            i, j = place
-            tiles = pl.ds(1 + (rows // TAIL) * (2 * i + j), rows // TAIL)
+        def __getitem__(self, i):
+            tiles = pl.ds(1 + (rows // TAIL) * i, rows // TAIL)
             return jnp.where(even, self.at_even[tiles], self.at_odd[tiles]).reshape(rows, lanes)
 
     lob, hib = Got(got_b, got_a), Got(got_a, got_b)
@@ -307,15 +314,15 @@
     low_ok, high_ok = me > 0, me < count - 1
 
     tx0 = jnp.where(low_ok, lo[0, 0], 0.0)
-    a2 = Plane(ln, lob[0, 0], lob[0, 1], lob[1, 0], lob[2, 0], lob[3, 0], low_ok)
-    a1 = Plane(ln, lob[0, 1], tx0, lob[1, 1], lob[2, 1], lob[3, 1], low_ok)
+    a1 = Plane(ln, lob[0], tx0, lob[1], lob[2], lob[3], low_ok)
     ma, to_above = lob.mask(0), lob.mask(2)
     mz, to_below = masks[0, 0:1], masks[0, 1:2]
     b0 = Plane(ln, tx0, lo[0, 1], lo[1, 0], lo[2, 0], lo[3, 0])
     b1, b2 = (Plane(ln, lo[0, i], lo[0, i + 1], lo[1, i], lo[2, i], lo[3, i]) for i in (1, 2))
     a1.edge(False)
     b0.edge(True)
-    vx, total = second_spill(a2, a1, False, ma, to_below)
+    outer = jnp.where(low_ok, lob[4], 1.0)
+    vx, total = second_spill(lob[0], a1, outer, to_below)
     put(0, 0, blocks, vx, None, total)
     vx, vd = edge_spill(a1, b0, False)
     put(0, 1, blocks, vx, vd, edge_total(a1, ma))
@@ -337,9 +344,8 @@
     mz, to_above = masks[layers - 1, 0:1], masks[layers - 1, 2:3]
     mb, to_below = hib.mask(0), hib.mask(1)
     a3, a2 = (Plane(ln, hi[0, i], hi[0, i + 1], hi[1, i], hi[2, i], hi[3, i]) for i in (1, 2))
-    a1 = Plane(ln, hi[0, 3], hib[0, 0], hi[1, 3], hi[2, 3], hi[3, 3])
-    b0 = Plane(ln, hib[0, 0], hib[0, 1], hib[1, 0], hib[2, 0], hib[3, 0], high_ok)
-    b1 = Plane(ln, hib[0, 1], hib[4, 0], hib[1, 1], hib[2, 1], hib[3, 1], high_ok)
+    a1 = Plane(ln, hi[0, 3], hib[0], hi[1, 3], hi[2, 3], hi[3, 3])
+    b0 = Plane(ln, hib[0], hib[5], hib[1], hib[2], hib[3], high_ok)
     a1.edge(False)
     b0.edge(True)
     vo, vz, _, total = second(a2, a1, a3, False, mz, to_below)
@@ -348,7 +354,8 @@
     put(1, 1, blocks, vo, vz, edge_total(a1, mz))
     vx, vd = edge_spill(b0, a1, True)
     put(1, 2, blocks, vx, vd, edge_total(b0, mb))
-    vx, total = second_spill(b1, b0, True, mb, to_above)
+    outer = jnp.where(high_ok, hib[4], 1.0)
+    vx, total = second_spill(hib[5], b0, outer, to_above)
     put(1, 3, blocks, vx, None, total)
     send(0, 0, width - 2)
     send(1, layers - 1, 2 * width - 2)
@@ -374,12 +381,12 @@
     )
     reach = jnp.transpose(support_reach, (0, 2, 1))
     reach = pltpu.with_memory_space_constraint(reach, pltpu.HBM)
-    tiles = 1 + 9 * rows // TAIL
+    tiles = 1 + 6 * rows // TAIL
     msg_a, msg_b, masks, faces = pl.pallas_call(
         functools.partial(pack_kernel, n, width, axis),
         out_shape=(
+            pltpu.VMEM((tiles + 1, TAIL, lanes), f32),
             pltpu.VMEM((tiles, TAIL, lanes), f32),
-            pltpu.VMEM((tiles + 1, TAIL, lanes), f32),
             pltpu.VMEM((layers, TAIL, lanes), f32),
             pltpu.VMEM((4, n, rows, lanes), f32),
         ),
@@ -387,7 +394,7 @@
         out_specs=(vmem,) * 4,
         scratch_shapes=[
             pltpu.VMEM((layers, 4, blocks), jnp.int32),
-            pltpu.SemaphoreType.DMA((5,)),
+            pltpu.SemaphoreType.DMA((13,)),
         ],
         compiler_params=params,
         name="pack",

time: 10.6 us -> 10.3 us (0.972)
  the two profiles are of different devices: /device:TPU:0 before, /device:TPU:1 now
where the time goes in v3:
time: 10.3 us; the launch traced here: 10.2 us
  Pallas kernels  5.5 us (53%)
  starting transfers between devices  4.62 us (45%)
    ppermute x1, starting transfers between devices, on_device(): got_b = lax.ppermute(msg_b, axis, swaps(range(1, count - 1, 2)))  4.49 us
    pallas_call x1, Pallas kernels, on_device(): pl.pallas_call(functools.partial(bulk_kernel, width, blocks), out_shape=o...  2.89 us
    pallas_call x1, Pallas kernels, on_device(): pl.pallas_call(functools.partial(pack_kernel, n, width, axis), out_shape=...  1.46 us
    pallas_call x1, Pallas kernels, on_device(): pl.pallas_call(functools.partial(edge_kernel, width, blocks, axis, count)...  1.15 us
  transfers between devices with their start and end apart: 2, of which 0 were waited for; matrix products, arithmetic and copies ran while one was open for 0% of the time, Pallas kernels for 28%

profile of v3, /device:TPU:1, one launch (start us, length us, event | category | flops | bytes accessed | tf_op | source)
XLA Modules:
  0.0 10.2 jit_solution(17428599258946745125)
XLA Ops:
  0.0 1.5 %pack.1 = (f32[14,8,128]{2,1,0:T(8,128)S(1)}, f32[13,8,128]{2,1,0:T(8,128)S(1)}, f32[2,8,128]{2,1,0:T(8,128)S(1)}, f32[4,32,16,128]{3,2,1,0:T(8,128)S(1)}) custom-call(f32[32,16,128]{2,1,0:T(8,128)} %tx.1, f32[32,16,128]{2,1,0:T(8,128)} %ty.1, f32[32,16,128]{2,1,0:T(8,128)} %tz.1, f32[32,16,128]{2,1,0:T(8,128)} %s.1, s32[2,4,8]{2,1,0:T(4,128)} %bitcast.1), custom_call_target="tpu_custom_call" | custom-call | tf_op jit(solution)/shard_map/pack/pallas_call | solution.py:385
  1.5 0.1 %collective-permute-start = (f32[14,8,128]{2,1,0:T(8,128)S(1)}, f32[14,8,128]{2,1,0:T(8,128)S(1)}, u32[]{:S(2)}, u32[]{:S(2)}) collective-permute-start(f32[14,8,128]{2,1,0:T(8,128)S(1)} %get-tuple-element.11), channel_id=1, source_target_pairs={{0,1},{1,0},{2,3},{3,2},{4,5},{5,4},{6,7},{7,6},{8,9},{9,8},{10,11... | collective-permute-start | bytes 172040 | tf_op jit(solution)/shard_map/ppermute | solution.py:402
  1.6 4.5 %collective-permute-start.1 = (f32[13,8,128]{2,1,0:T(8,128)S(1)}, f32[13,8,128]{2,1,0:T(8,128)S(1)}, u32[]{:S(2)}, u32[]{:S(2)}) collective-permute-start(f32[13,8,128]{2,1,0:T(8,128)S(1)} %get-tuple-element.12), channel_id=1, source_target_pairs={{1,2},{2,1},{3,4},{4,3},{5,6},{6,5},{7,8},{8,7},{9,10},{10,9},{11,... | collective-permute-start | bytes 159752 | tf_op jit(solution)/shard_map/ppermute | solution.py:403
  6.1 2.9 %bulk.1.held = f32[2,8,48,16,128]{4,3,2,1,0:T(8,128)} custom-call(f32[4,32,16,128]{3,2,1,0:T(8,128)S(1)} %get-tuple-element.9.faces, f32[2,8,128]{2,1,0:T(8,128)S(1)} %get-tuple-element.10.masks), custom_call_target="tpu_custom_call" | custom-call | flops 10000000 | bytes 7000000 | tf_op jit(solution)/shard_map/bulk/pallas_call | solution.py:407
  9.0 0.0 collective-permute-done.1.got_b
  9.0 0.0 collective-permute-done.got_a
  9.0 1.1 %edges.1 = f32[2,8,48,16,128]{4,3,2,1,0:T(8,128)} custom-call(f32[4,32,16,128]{3,2,1,0:T(8,128)S(1)} %get-tuple-element.9.faces, f32[2,8,128]{2,1,0:T(8,128)S(1)} %get-tuple-element.10.masks, f32[14,8,128]{2,1,0:T(8,128)S(1)} %collective-permute-done.got_a, f32[13,8,128]{2,1,0:T(8,128)S(1)} %collective-permute-done.1.got_b, ...), custom_call_target="tpu_custom_call", output_to_operand_aliasing={{}: (4, {})} | custom-call | flops 1000000 | bytes 1000000 | tf_op jit(solution)/shard_map/edges/pallas_call | solution.py:421
Async XLA Ops:
  1.5 7.5 %collective-permute-start = (f32[14,8,128]{2,1,0:T(8,128)S(1)}, f32[14,8,128]{2,1,0:T(8,128)S(1)}, u32[]{:S(2)}, u32[]{:S(2)}) collective-permute-start(f32[14,8,128]{2,1,0:T(8,128)S(1)} %get-tuple-element.11), channel_id=1, source_target_pairs={{0,1},{1,0},{2,3},{3,2},{4,5},{5,4},{6,7},{7,6},{8,9},{9,8},{10,11... | collective-permute-start | bytes 172040 | tf_op jit(solution)/shard_map/ppermute | solution.py:402
  1.6 7.4 %collective-permute-start.1 = (f32[13,8,128]{2,1,0:T(8,128)S(1)}, f32[13,8,128]{2,1,0:T(8,128)S(1)}, u32[]{:S(2)}, u32[]{:S(2)}) collective-permute-start(f32[13,8,128]{2,1,0:T(8,128)S(1)} %get-tuple-element.12), channel_id=1, source_target_pairs={{1,2},{2,1},{3,4},{4,3},{5,6},{6,5},{7,8},{8,7},{9,10},{10,9},{11,... | collective-permute-start | bytes 159752 | tf_op jit(solution)/shard_map/ppermute | solution.py:403

commit v4 on v2

--- a/solution.py
+++ b/solution.py
@@ -9,7 +9,7 @@
 
 
 TAIL = 8
-CHUNK = 4
+CHUNK = 12
 SPLIT = 2
 
 
@@ -77,6 +77,10 @@
         return self.ty * self.ln.ym(v) + self.typ * self.ln.yp(v)
 
 
+def plane_at(ln, faces, p):
+    return Plane(ln, faces[0, p], faces[0, p + 1], faces[1, p], faces[2, p], faces[3, p])
+
+
 def middle(p, below, above, mz):
     ln = p.ln
     vz = p.half * p.z1 + p.tx * below.z1 + p.txn * above.z1 + p.along_y(p.z1)
@@ -124,18 +128,64 @@
     return vx, vd
 
 
-def second_spill(p, edge, low, mz, mx):
-    vx = p.toward(low) * edge.x1
-    kept = vx * mx
-    return kept, edge_total(p, mz) - (vx - kept)
-
-
-def store(ln, dst, layer, plane, blocks, own, other, total):
+def work_side(ln, low, valid, faces, masks, msg, put):
+    n, rows, lanes = faces.shape[1:]
+    layers = masks.shape[0]
+
+    def own(i, j):
+        return faces[i, jnp.where(low, j, n - 1 - j)]
+
+    def got(i, j):
+        tiles = rows // TAIL
+        return msg[pl.ds(1 + tiles * (2 * i + j), tiles)].reshape(rows, lanes)
+
+    f1, f2, f3 = (faces[0, jnp.where(low, j, n - j)] for j in (1, 2, 3))
+    f0 = jnp.where(valid, jnp.where(low, faces[0, 0], got(0, 0)), 0.0)
+    g1 = jnp.where(low, got(0, 0), got(0, 1))
+    g2 = jnp.where(low, got(0, 1), got(4, 0))
+    a0 = Plane(ln, f0, f1, own(1, 0), own(2, 0), own(3, 0))
+    a1 = Plane(ln, f1, f2, own(1, 1), own(2, 1), own(3, 1))
+    a2 = Plane(ln, f2, f3, own(1, 2), own(2, 2), own(3, 2))
+    b0 = Plane(ln, g1, f0, got(1, 0), got(2, 0), got(3, 0), valid)
+    b1 = Plane(ln, g2, g1, got(1, 1), got(2, 1), got(3, 1), valid)
+    mine = masks[jnp.where(low, 0, layers - 1)]
+    mz, my_reach = mine[0:1], jnp.where(low, mine[1:2], mine[2:3])
+    theirs = msg[0]
+    mo, their_reach = theirs[0:1], jnp.where(low, theirs[2:3], theirs[1:2])
+    a0.edge(True)
+    b0.edge(False)
+    vx = g1 * b0.x1
+    kept = vx * my_reach
+    put(0, kept, None, edge_total(b1, mo) - (vx - kept))
+    vx, vd = edge_spill(b0, a0, False)
+    put(1, vx, vd, edge_total(b0, mo))
+    vo, vz = edge_own(a0, 1.0 - a1.z1, a1.z1, b0.x1, True, mz)
+    put(2, vo, vz, edge_total(a0, mz))
+    vo, vz, _, total = second(a1, a0, a2, True, mz, their_reach)
+    put(3, vo, vz, total)
+
+
+def store_side(ln, buf, low, blocks):
+    def put(i, own, other, total):
+        store(ln, buf, jnp.where(low, i, 3 - i), blocks, own, other, total)
+
+    return put
+
+
+def send_side(buf, out, low, width, sems):
+    layers, blocks = out.shape[:2]
+    layer = jnp.where(low, 0, layers - 1)
+    start = jnp.where(low, width - 2, 2 * width - 2)
+    for k in range(blocks):
+        yield pltpu.make_async_copy(buf.at[k], out.at[layer, k, pl.ds(start, 4)], sems.at[k])
+
+
+def store(ln, dst, plane, blocks, own, other, total):
     scale = 1.0 / total
     own = own * scale
     other = jnp.zeros_like(own) if other is None else other * scale
     for k in range(blocks):
-        dst[layer, k, plane] = jnp.where(ln.block == k, own, jnp.where(ln.other == k, other, 0.0))
+        dst[k, plane] = jnp.where(ln.block == k, own, jnp.where(ln.other == k, other, 0.0))
 
 
 def pack_kernel(
@@ -144,10 +194,11 @@
     layers, _, blocks = held_reach.shape
     lanes = masks.shape[-1]
     fetch = pltpu.make_async_copy(reach, held_reach, sems.at[4])
+    fetch.start()
     copies = [
         pltpu.make_async_copy(a, faces.at[i], sems.at[i]) for i, a in enumerate((tx, ty, tz, s))
     ]
-    for c in [fetch] + copies:
+    for c in copies:
         c.start()
     masks[...] = jnp.zeros(masks.shape, jnp.float32)
     lane = lax.broadcasted_iota(jnp.int32, (4, lanes), 1)
@@ -179,12 +230,12 @@
     for c in copies:
         c.wait()
     for i in range(4):
-        for j in range(2):
-            put(1 + 2 * (2 * i + j), faces[i, n - 2 + j], faces[i, j])
+        put(1 + 4 * i, faces[i, n - 1], faces[i, 0])
+        put(3 + 4 * i, faces[i, n - 2], faces[i, 1])
     put(17, faces[0, n - 1], faces[0, 2])
 
 
-def bulk_kernel(width, blocks, faces, masks, out, zeros, buf, sems):
+def bulk_kernel(width, blocks, axis, count, faces, masks, msg, out, zeros, buf, side, sems, side_sems):
     layers = masks.shape[0]
     rows, lanes = faces.shape[2:]
     depth = zeros.shape[0]
@@ -212,9 +263,7 @@
 
     ln = Lanes((rows, lanes), width)
 
-    def plane(p):
-        return Plane(ln, faces[0, p], faces[0, p + 1], faces[1, p], faces[2, p], faces[3, p])
-
+    plane = functools.partial(plane_at, ln, faces)
     chunks = (width - 4) // CHUNK
 
     @pl.loop(0, layers * chunks)
@@ -225,7 +274,7 @@
         mz = masks[layer, 0:1]
         for j in range(CHUNK):
             vo, vz, total = middle(planes[j + 1], planes[j], planes[j + 2], mz)
-            store(ln, buf, layer, first + j + 2, blocks, vo, vz, total)
+            store(ln, buf.at[layer], first + j + 2, blocks, vo, vz, total)
         for c in send(layer, first + 2, CHUNK, i):
             c.start()
 
@@ -238,8 +287,8 @@
         b0, b1, b2 = (plane(base + i) for i in (0, 1, 2))
         a1.edge(False)
         b0.edge(True)
-        low = functools.partial(store, ln, buf, layer - 1)
-        high = functools.partial(store, ln, buf, layer)
+        low = functools.partial(store, ln, buf.at[layer - 1])
+        high = functools.partial(store, ln, buf.at[layer])
         vo, vz, vx, total = second(a2, a1, a3, False, ma, to_below)
         low(width, blocks, vo, vz, total)
         high(0, blocks, vx, None, total)
@@ -262,6 +311,12 @@
         for c in send(layer, 0, 4, index + 1):
             c.start()
 
+    me = lax.axis_index(axis)
+    lower = lax.rem(me, 2) == 1
+    work_side(ln, lower, lower | (me < count - 1), faces, masks, msg, store_side(ln, side, lower, blocks))
+    for c in send_side(side, out, lower, width, side_sems):
+        c.start()
+
     for layer in range(layers):
         for i in range(chunks):
             for c in send(layer, 4 + i * CHUNK, CHUNK, layer * chunks + i):
@@ -273,86 +328,25 @@
         for c in send(layer, 0, 4, index + 1):
             c.wait()
 
+    for c in send_side(side, out, lower, width, side_sems):
+        c.wait()
+
     @pl.loop(0, blocks)
     def _(k):
         for c in clears(k):
             c.wait()
 
 
-def edge_kernel(
-    width, blocks, axis, count, faces, masks, got_a, got_b, held, out, buf, sems
-):
+def edge_kernel(width, blocks, axis, count, faces, masks, msg, held, out, side, sems):
     del held
-    layers = masks.shape[0]
     me = lax.axis_index(axis)
-    even = lax.rem(me, 2) == 0
-    n, rows, lanes = faces.shape[1:]
-    lo, hi = faces, faces.at[:, pl.ds(n - 4, 4)]
-
-    class Got:
-        def __init__(self, at_even, at_odd):
-            self.at_even, self.at_odd = at_even, at_odd
-
-        def mask(self, row):
-            return jnp.where(even, self.at_even[0, row : row + 1], self.at_odd[0, row : row + 1])
-
-        def __getitem__(self, place):
-            i, j = place
-            tiles = pl.ds(1 + (rows // TAIL) * (2 * i + j), rows // TAIL)
-            return jnp.where(even, self.at_even[tiles], self.at_odd[tiles]).reshape(rows, lanes)
-
-    lob, hib = Got(got_b, got_a), Got(got_a, got_b)
-    ln = Lanes((rows, lanes), width)
-    put = functools.partial(store, ln, buf)
-    low_ok, high_ok = me > 0, me < count - 1
-
-    tx0 = jnp.where(low_ok, lo[0, 0], 0.0)
-    a2 = Plane(ln, lob[0, 0], lob[0, 1], lob[1, 0], lob[2, 0], lob[3, 0], low_ok)
-    a1 = Plane(ln, lob[0, 1], tx0, lob[1, 1], lob[2, 1], lob[3, 1], low_ok)
-    ma, to_above = lob.mask(0), lob.mask(2)
-    mz, to_below = masks[0, 0:1], masks[0, 1:2]
-    b0 = Plane(ln, tx0, lo[0, 1], lo[1, 0], lo[2, 0], lo[3, 0])
-    b1, b2 = (Plane(ln, lo[0, i], lo[0, i + 1], lo[1, i], lo[2, i], lo[3, i]) for i in (1, 2))
-    a1.edge(False)
-    b0.edge(True)
-    vx, total = second_spill(a2, a1, False, ma, to_below)
-    put(0, 0, blocks, vx, None, total)
-    vx, vd = edge_spill(a1, b0, False)
-    put(0, 1, blocks, vx, vd, edge_total(a1, ma))
-    vo, vz = edge_own(b0, 1.0 - b1.z1, b1.z1, a1.x1, True, mz)
-    put(0, 2, blocks, vo, vz, edge_total(b0, mz))
-    vo, vz, _, total = second(b1, b0, b2, True, mz, to_above)
-    put(0, 3, blocks, vo, vz, total)
-    sends = []
-
-    def send(side, layer, start):
-        for k in range(blocks):
-            c = pltpu.make_async_copy(
-                buf.at[side, k], out.at[layer, k, pl.ds(start, 4)], sems.at[len(sends)]
-            )
-            c.start()
-            sends.append(c)
-
-
-    mz, to_above = masks[layers - 1, 0:1], masks[layers - 1, 2:3]
-    mb, to_below = hib.mask(0), hib.mask(1)
-    a3, a2 = (Plane(ln, hi[0, i], hi[0, i + 1], hi[1, i], hi[2, i], hi[3, i]) for i in (1, 2))
-    a1 = Plane(ln, hi[0, 3], hib[0, 0], hi[1, 3], hi[2, 3], hi[3, 3])
-    b0 = Plane(ln, hib[0, 0], hib[0, 1], hib[1, 0], hib[2, 0], hib[3, 0], high_ok)
-    b1 = Plane(ln, hib[0, 1], hib[4, 0], hib[1, 1], hib[2, 1], hib[3, 1], high_ok)
-    a1.edge(False)
-    b0.edge(True)
-    vo, vz, _, total = second(a2, a1, a3, False, mz, to_below)
-    put(1, 0, blocks, vo, vz, total)
-    vo, vz = edge_own(a1, 1.0 - a2.z1, a2.z1, b0.x1, False, mz)
-    put(1, 1, blocks, vo, vz, edge_total(a1, mz))
-    vx, vd = edge_spill(b0, a1, True)
-    put(1, 2, blocks, vx, vd, edge_total(b0, mb))
-    vx, total = second_spill(b1, b0, True, mb, to_above)
-    put(1, 3, blocks, vx, None, total)
-    send(0, 0, width - 2)
-    send(1, layers - 1, 2 * width - 2)
-    for c in sends:
+    lower = lax.rem(me, 2) == 0
+    valid = jnp.where(lower, me > 0, me < count - 1)
+    ln = Lanes(faces.shape[2:], width)
+    work_side(ln, lower, valid, faces, masks, msg, store_side(ln, side, lower, blocks))
+    for c in send_side(side, out, lower, width, sems):
+        c.start()
+    for c in send_side(side, out, lower, width, sems):
         c.wait()
 
 
@@ -378,8 +372,8 @@
     msg_a, msg_b, masks, faces = pl.pallas_call(
         functools.partial(pack_kernel, n, width, axis),
         out_shape=(
+            pltpu.VMEM((tiles + 1, TAIL, lanes), f32),
             pltpu.VMEM((tiles, TAIL, lanes), f32),
-            pltpu.VMEM((tiles + 1, TAIL, lanes), f32),
             pltpu.VMEM((layers, TAIL, lanes), f32),
             pltpu.VMEM((4, n, rows, lanes), f32),
         ),
@@ -397,34 +391,34 @@
 
     out_shape = jax.ShapeDtypeStruct((layers, blocks, 3 * width, rows, lanes), f32)
     sends = layers * ((width - 4) // CHUNK) + 2 * (layers - 1)
+    side = pltpu.VMEM((blocks, 4, rows, lanes), f32)
     bulk = pl.pallas_call(
-        functools.partial(bulk_kernel, width, blocks),
+        functools.partial(bulk_kernel, width, blocks, axis, count),
         out_shape=out_shape,
-        in_specs=[vmem] * 2,
+        in_specs=[vmem] * 3,
         out_specs=anywhere,
         scratch_shapes=[
             pltpu.VMEM((width - 2, rows, lanes), f32),
             pltpu.VMEM((layers, blocks, width + 4, rows, lanes), f32),
+            side,
             pltpu.SemaphoreType.DMA((2 * layers * blocks + sends * SPLIT,)),
+            pltpu.SemaphoreType.DMA((blocks,)),
         ],
         compiler_params=params,
         cost_estimate=pl.CostEstimate(flops=10**7, bytes_accessed=7 * 10**6, transcendentals=0),
         name="bulk",
-    )(faces, masks)
+    )(faces, masks, got_a)
     return pl.pallas_call(
         functools.partial(edge_kernel, width, blocks, axis, count),
         out_shape=out_shape,
-        in_specs=[vmem] * 4 + [anywhere],
+        in_specs=[vmem] * 3 + [anywhere],
         out_specs=anywhere,
-        scratch_shapes=[
-            pltpu.VMEM((2, blocks, 4, rows, lanes), f32),
-            pltpu.SemaphoreType.DMA((2 * blocks,)),
-        ],
-        input_output_aliases={4: 0},
+        scratch_shapes=[side, pltpu.SemaphoreType.DMA((blocks,))],
+        input_output_aliases={3: 0},
         compiler_params=params,
         cost_estimate=pl.CostEstimate(flops=10**6, bytes_accessed=10**6, transcendentals=0),
         name="edges",
-    )(faces, masks, got_a, got_b, bulk)
+    )(faces, masks, got_b, bulk)
 
 
 def solution(mesh):

time: 10.6 us -> 10.1 us (0.953)
  the two profiles are of different devices: /device:TPU:0 before, /device:TPU:1 now
where the time goes in v4:
time: 10.1 us; the launch traced here: 9.91 us
  Pallas kernels  5.25 us (52%)
  starting transfers between devices  4.62 us (46%)
    ppermute x1, starting transfers between devices, on_device(): got_b = lax.ppermute(msg_b, axis, swaps(range(1, count - 1, 2)))  4.49 us
    pallas_call x1, Pallas kernels, on_device(): pl.pallas_call(functools.partial(bulk_kernel, width, blocks, axis, count)...  3.02 us
    pallas_call x1, Pallas kernels, on_device(): pl.pallas_call(functools.partial(pack_kernel, n, width, axis), out_shape=...  1.26 us
    pallas_call x1, Pallas kernels, on_device(): pl.pallas_call(functools.partial(edge_kernel, width, blocks, axis, count)...  0.97 us
  transfers between devices with their start and end apart: 2, of which 0 were waited for; matrix products, arithmetic and copies ran while one was open for 0% of the time, Pallas kernels for 31%

profile of v4, /device:TPU:1, one launch (start us, length us, event | category | flops | bytes accessed | tf_op | source)
XLA Modules:
  0.0 9.9 jit_solution(6039898812936562727)
XLA Ops:
  0.0 1.3 %pack.1 = (f32[20,8,128]{2,1,0:T(8,128)S(1)}, f32[19,8,128]{2,1,0:T(8,128)S(1)}, f32[2,8,128]{2,1,0:T(8,128)S(1)}, f32[4,32,16,128]{3,2,1,0:T(8,128)S(1)}) custom-call(f32[32,16,128]{2,1,0:T(8,128)} %tx.1, f32[32,16,128]{2,1,0:T(8,128)} %ty.1, f32[32,16,128]{2,1,0:T(8,128)} %tz.1, f32[32,16,128]{2,1,0:T(8,128)} %s.1, s32[2,4,8]{2,1,0:T(4,128)} %bitcast.1), custom_call_target="tpu_custom_call" | custom-call | tf_op jit(solution)/shard_map/pack/pallas_call | solution.py:372
  1.3 0.1 %collective-permute-start.1 = (f32[20,8,128]{2,1,0:T(8,128)S(1)}, f32[20,8,128]{2,1,0:T(8,128)S(1)}, u32[]{:S(2)}, u32[]{:S(2)}) collective-permute-start(f32[20,8,128]{2,1,0:T(8,128)S(1)} %get-tuple-element.12), channel_id=1, source_target_pairs={{0,1},{1,0},{2,3},{3,2},{4,5},{5,4},{6,7},{7,6},{8,9},{9,8},{10,11... | collective-permute-start | bytes 245768 | tf_op jit(solution)/shard_map/ppermute | solution.py:389
  1.4 4.5 %collective-permute-start = (f32[19,8,128]{2,1,0:T(8,128)S(1)}, f32[19,8,128]{2,1,0:T(8,128)S(1)}, u32[]{:S(2)}, u32[]{:S(2)}) collective-permute-start(f32[19,8,128]{2,1,0:T(8,128)S(1)} %get-tuple-element.11), channel_id=1, source_target_pairs={{1,2},{2,1},{3,4},{4,3},{5,6},{6,5},{7,8},{8,7},{9,10},{10,9},{11,... | collective-permute-start | bytes 233480 | tf_op jit(solution)/shard_map/ppermute | solution.py:390
  5.9 0.0 collective-permute-done.1.msg
  5.9 3.0 %bulk.1.held = f32[2,8,48,16,128]{4,3,2,1,0:T(8,128)} custom-call(f32[4,32,16,128]{3,2,1,0:T(8,128)S(1)} %get-tuple-element.9.faces, f32[2,8,128]{2,1,0:T(8,128)S(1)} %get-tuple-element.10.masks, f32[20,8,128]{2,1,0:T(8,128)S(1)} %collective-permute-done.1.msg), custom_call_target="tpu_custom_call" | custom-call | flops 10000000 | bytes 7000000 | tf_op jit(solution)/shard_map/bulk/pallas_call | solution.py:395
  8.9 0.0 collective-permute-done.msg
  8.9 1.0 %edges.1 = f32[2,8,48,16,128]{4,3,2,1,0:T(8,128)} custom-call(f32[4,32,16,128]{3,2,1,0:T(8,128)S(1)} %get-tuple-element.9.faces, f32[2,8,128]{2,1,0:T(8,128)S(1)} %get-tuple-element.10.masks, f32[19,8,128]{2,1,0:T(8,128)S(1)} %collective-permute-done.msg, f32[2,8,48,16,128]{4,3,2,1,0:T(8,128)} %bulk.1.held), custom_call_target="tpu_custom_call", output_to_operand_aliasing={{}: (3, {})} | custom-call | flops 1000000 | bytes 1000000 | tf_op jit(solution)/shard_map/edges/pallas_call | solution.py:411
Async XLA Ops:
  1.3 4.6 %collective-permute-start.1 = (f32[20,8,128]{2,1,0:T(8,128)S(1)}, f32[20,8,128]{2,1,0:T(8,128)S(1)}, u32[]{:S(2)}, u32[]{:S(2)}) collective-permute-start(f32[20,8,128]{2,1,0:T(8,128)S(1)} %get-tuple-element.12), channel_id=1, source_target_pairs={{0,1},{1,0},{2,3},{3,2},{4,5},{5,4},{6,7},{7,6},{8,9},{9,8},{10,11... | collective-permute-start | bytes 245768 | tf_op jit(solution)/shard_map/ppermute | solution.py:389
  1.4 7.5 %collective-permute-start = (f32[19,8,128]{2,1,0:T(8,128)S(1)}, f32[19,8,128]{2,1,0:T(8,128)S(1)}, u32[]{:S(2)}, u32[]{:S(2)}) collective-permute-start(f32[19,8,128]{2,1,0:T(8,128)S(1)} %get-tuple-element.11), channel_id=1, source_target_pairs={{1,2},{2,1},{3,4},{4,3},{5,6},{6,5},{7,8},{8,7},{9,10},{10,9},{11,... | collective-permute-start | bytes 233480 | tf_op jit(solution)/shard_map/ppermute | solution.py:390

commit v5 on v4

--- a/solution.py
+++ b/solution.py
@@ -10,6 +10,7 @@
 
 TAIL = 8
 CHUNK = 12
+EARLY = 1
 SPLIT = 2
 
 
@@ -188,8 +189,18 @@
         dst[k, plane] = jnp.where(ln.block == k, own, jnp.where(ln.other == k, other, 0.0))
 
 
+def clear_copies(zeros, out, k, parts, sems):
+    depth = zeros.shape[0]
+    for i, part in enumerate(parts):
+        layer, side = part // 2, part % 2
+        start = side * (out.shape[2] - depth)
+        sem = sems.at[i * out.shape[1] + k]
+        yield pltpu.make_async_copy(zeros, out.at[layer, k, pl.ds(start, depth)], sem)
+
+
 def pack_kernel(
-    n, width, axis, tx, ty, tz, s, reach, msg_a, msg_b, masks, faces, held_reach, sems
+    n, width, axis, tx, ty, tz, s, reach, msg_a, msg_b, masks, faces, out,
+    held_reach, zeros, sems, clear_sems,
 ):
     layers, _, blocks = held_reach.shape
     lanes = masks.shape[-1]
@@ -200,6 +211,13 @@
     ]
     for c in copies:
         c.start()
+    zeros[...] = jnp.zeros(zeros.shape, jnp.float32)
+
+    @pl.loop(0, blocks)
+    def _(k):
+        for c in clear_copies(zeros, out, k, range(EARLY), clear_sems):
+            c.start()
+
     masks[...] = jnp.zeros(masks.shape, jnp.float32)
     lane = lax.broadcasted_iota(jnp.int32, (4, lanes), 1)
     block = lane // width
@@ -234,18 +252,18 @@
         put(3 + 4 * i, faces[i, n - 2], faces[i, 1])
     put(17, faces[0, n - 1], faces[0, 2])
 
-
-def bulk_kernel(width, blocks, axis, count, faces, masks, msg, out, zeros, buf, side, sems, side_sems):
+    @pl.loop(0, blocks)
+    def _(k):
+        for c in clear_copies(zeros, out, k, range(EARLY), clear_sems):
+            c.wait()
+
+
+def bulk_kernel(width, blocks, axis, count, faces, masks, msg, held, out, zeros, buf, side, sems, side_sems, clear_sems):
     layers = masks.shape[0]
     rows, lanes = faces.shape[2:]
-    depth = zeros.shape[0]
+    del held
+    late = range(EARLY, 2 * layers)
     zeros[...] = jnp.zeros(zeros.shape, jnp.float32)
-
-    def clears(k):
-        for layer in range(layers):
-            for side, start in enumerate((0, 3 * width - depth)):
-                sem = sems.at[(layer * 2 + side) * blocks + k]
-                yield pltpu.make_async_copy(zeros, out.at[layer, k, pl.ds(start, depth)], sem)
 
     def send(layer, start, planes, index):
         for i in range(SPLIT):
@@ -253,12 +271,12 @@
             yield pltpu.make_async_copy(
                 buf.at[layer, few, pl.ds(start, planes)],
                 out.at[layer, few, pl.ds(width - 2 + start, planes)],
-                sems.at[2 * layers * blocks + index * SPLIT + i],
+                sems.at[index * SPLIT + i],
             )
 
     @pl.loop(0, blocks)
     def _(k):
-        for c in clears(k):
+        for c in clear_copies(zeros, out, k, late, clear_sems):
             c.start()
 
     ln = Lanes((rows, lanes), width)
@@ -333,7 +351,7 @@
 
     @pl.loop(0, blocks)
     def _(k):
-        for c in clears(k):
+        for c in clear_copies(zeros, out, k, late, clear_sems):
             c.wait()
 
 
@@ -369,19 +387,24 @@
     reach = jnp.transpose(support_reach, (0, 2, 1))
     reach = pltpu.with_memory_space_constraint(reach, pltpu.HBM)
     tiles = 1 + 9 * rows // TAIL
-    msg_a, msg_b, masks, faces = pl.pallas_call(
+    out_shape = jax.ShapeDtypeStruct((layers, blocks, 3 * width, rows, lanes), f32)
+    zeros = pltpu.VMEM((width - 2, rows, lanes), f32)
+    msg_a, msg_b, masks, faces, cleared = pl.pallas_call(
         functools.partial(pack_kernel, n, width, axis),
         out_shape=(
             pltpu.VMEM((tiles + 1, TAIL, lanes), f32),
             pltpu.VMEM((tiles, TAIL, lanes), f32),
             pltpu.VMEM((layers, TAIL, lanes), f32),
             pltpu.VMEM((4, n, rows, lanes), f32),
+            out_shape,
         ),
         in_specs=[anywhere] * 5,
-        out_specs=(vmem,) * 4,
+        out_specs=(vmem,) * 4 + (anywhere,),
         scratch_shapes=[
             pltpu.VMEM((layers, 4, blocks), jnp.int32),
+            zeros,
             pltpu.SemaphoreType.DMA((5,)),
+            pltpu.SemaphoreType.DMA((EARLY * blocks,)),
         ],
         compiler_params=params,
         name="pack",
@@ -389,25 +412,26 @@
     got_a = lax.ppermute(msg_a, axis, swaps(range(0, count - 1, 2)))
     got_b = lax.ppermute(msg_b, axis, swaps(range(1, count - 1, 2)))
 
-    out_shape = jax.ShapeDtypeStruct((layers, blocks, 3 * width, rows, lanes), f32)
     sends = layers * ((width - 4) // CHUNK) + 2 * (layers - 1)
     side = pltpu.VMEM((blocks, 4, rows, lanes), f32)
     bulk = pl.pallas_call(
         functools.partial(bulk_kernel, width, blocks, axis, count),
         out_shape=out_shape,
-        in_specs=[vmem] * 3,
+        in_specs=[vmem] * 3 + [anywhere],
         out_specs=anywhere,
         scratch_shapes=[
-            pltpu.VMEM((width - 2, rows, lanes), f32),
+            zeros,
             pltpu.VMEM((layers, blocks, width + 4, rows, lanes), f32),
             side,
-            pltpu.SemaphoreType.DMA((2 * layers * blocks + sends * SPLIT,)),
+            pltpu.SemaphoreType.DMA((sends * SPLIT,)),
             pltpu.SemaphoreType.DMA((blocks,)),
+            pltpu.SemaphoreType.DMA(((2 * layers - EARLY) * blocks,)),
         ],
+        input_output_aliases={3: 0},
         compiler_params=params,
         cost_estimate=pl.CostEstimate(flops=10**7, bytes_accessed=7 * 10**6, transcendentals=0),
         name="bulk",
-    )(faces, masks, got_a)
+    )(faces, masks, got_a, cleared)
     return pl.pallas_call(
         functools.partial(edge_kernel, width, blocks, axis, count),
         out_shape=out_shape,

time: 10.1 us -> 10.2 us (level)
    pallas_call x1, Pallas kernels: 1.26 us -> 1.7 us  [on_device(): pl.pallas_call(functools.partial(pack_kernel, n, width, axis), out_shape=...]
    pallas_call x1, Pallas kernels: 3.02 us -> 2.67 us  [on_device(): pl.pallas_call(functools.partial(bulk_kernel, width, blocks, axis, count)...]
  transfers between devices with their start and end apart: 2 -> 2, of which waited for: 0 -> 0; matrix products, arithmetic and copies ran while one was open for 0% -> 0% of each run, Pallas kernels for 31% -> 27%
where the time goes in v5:
time: 10.2 us; the launch traced here: 10 us
  Pallas kernels  5.34 us (52%)
  starting transfers between devices  4.62 us (45%)
    ppermute x1, starting transfers between devices, on_device(): got_b = lax.ppermute(msg_b, axis, swaps(range(1, count - 1, 2)))  4.49 us
    pallas_call x1, Pallas kernels, on_device(): pl.pallas_call(functools.partial(bulk_kernel, width, blocks, axis, count)...  2.67 us
    pallas_call x1, Pallas kernels, on_device(): pl.pallas_call(functools.partial(pack_kernel, n, width, axis), out_shape=...  1.7 us
    pallas_call x1, Pallas kernels, on_device(): pl.pallas_call(functools.partial(edge_kernel, width, blocks, axis, count)...  0.97 us
  transfers between devices with their start and end apart: 2, of which 0 were waited for; matrix products, arithmetic and copies ran while one was open for 0% of the time, Pallas kernels for 27%

profile of v5, /device:TPU:1, one launch (start us, length us, event | category | flops | bytes accessed | tf_op | source)
XLA Modules:
  0.0 10.0 jit_solution(910933590335727411)
XLA Ops:
  0.0 1.7 %pack.1 = (f32[20,8,128]{2,1,0:T(8,128)S(1)}, f32[19,8,128]{2,1,0:T(8,128)S(1)}, f32[2,8,128]{2,1,0:T(8,128)S(1)}, f32[4,32,16,128]{3,2,1,0:T(8,128)S(1)}, f32[2,8,48,16,128]{4,3,2,1,0:T(8,128)}) custom-call(f32[32,16,128]{2,1,0:T(8,128)} %tx.1, f32[32,16,128]{2,1,0:T(8,128)} %ty.1, f32[32,16,128]{2,1,0:T(8,128)} %tz.1, f32[32,16,128]{2,1,0:T(8,128)} %s.1, ...), custom_call_target="tpu_custom_call" | custom-call | tf_op jit(solution)/shard_map/pack/pallas_call | solution.py:392
  1.7 0.1 %collective-permute-start.1 = (f32[20,8,128]{2,1,0:T(8,128)S(1)}, f32[20,8,128]{2,1,0:T(8,128)S(1)}, u32[]{:S(2)}, u32[]{:S(2)}) collective-permute-start(f32[20,8,128]{2,1,0:T(8,128)S(1)} %get-tuple-element.13), channel_id=1, source_target_pairs={{0,1},{1,0},{2,3},{3,2},{4,5},{5,4},{6,7},{7,6},{8,9},{9,8},{10,11... | collective-permute-start | bytes 245768 | tf_op jit(solution)/shard_map/ppermute | solution.py:412
  1.8 4.5 %collective-permute-start = (f32[19,8,128]{2,1,0:T(8,128)S(1)}, f32[19,8,128]{2,1,0:T(8,128)S(1)}, u32[]{:S(2)}, u32[]{:S(2)}) collective-permute-start(f32[19,8,128]{2,1,0:T(8,128)S(1)} %get-tuple-element.12), channel_id=1, source_target_pairs={{1,2},{2,1},{3,4},{4,3},{5,6},{6,5},{7,8},{8,7},{9,10},{10,9},{11,... | collective-permute-start | bytes 233480 | tf_op jit(solution)/shard_map/ppermute | solution.py:413
  6.3 0.0 collective-permute-done.1.msg
  6.3 2.7 %bulk.1.held = f32[2,8,48,16,128]{4,3,2,1,0:T(8,128)} custom-call(f32[4,32,16,128]{3,2,1,0:T(8,128)S(1)} %get-tuple-element.10.faces, f32[2,8,128]{2,1,0:T(8,128)S(1)} %get-tuple-element.11.masks, f32[20,8,128]{2,1,0:T(8,128)S(1)} %collective-permute-done.1.msg, f32[2,8,48,16,128]{4,3,2,1,0:T(8,128)} %get-tuple-element.14.held), custom_call_target="tpu_custom_call", output_to_operand_aliasing={{}: (3, {})} | custom-call | flops 10000000 | bytes 7000000 | tf_op jit(solution)/shard_map/bulk/pallas_call | solution.py:417
  9.0 0.0 collective-permute-done.msg
  9.0 1.0 %edges.1 = f32[2,8,48,16,128]{4,3,2,1,0:T(8,128)} custom-call(f32[4,32,16,128]{3,2,1,0:T(8,128)S(1)} %get-tuple-element.10.faces, f32[2,8,128]{2,1,0:T(8,128)S(1)} %get-tuple-element.11.masks, f32[19,8,128]{2,1,0:T(8,128)S(1)} %collective-permute-done.msg, f32[2,8,48,16,128]{4,3,2,1,0:T(8,128)} %bulk.1.held), custom_call_target="tpu_custom_call", output_to_operand_aliasing={{}: (3, {})} | custom-call | flops 1000000 | bytes 1000000 | tf_op jit(solution)/shard_map/edges/pallas_call | solution.py:435
Async XLA Ops:
  1.7 4.6 %collective-permute-start.1 = (f32[20,8,128]{2,1,0:T(8,128)S(1)}, f32[20,8,128]{2,1,0:T(8,128)S(1)}, u32[]{:S(2)}, u32[]{:S(2)}) collective-permute-start(f32[20,8,128]{2,1,0:T(8,128)S(1)} %get-tuple-element.13), channel_id=1, source_target_pairs={{0,1},{1,0},{2,3},{3,2},{4,5},{5,4},{6,7},{7,6},{8,9},{9,8},{10,11... | collective-permute-start | bytes 245768 | tf_op jit(solution)/shard_map/ppermute | solution.py:412
  1.8 7.2 %collective-permute-start = (f32[19,8,128]{2,1,0:T(8,128)S(1)}, f32[19,8,128]{2,1,0:T(8,128)S(1)}, u32[]{:S(2)}, u32[]{:S(2)}) collective-permute-start(f32[19,8,128]{2,1,0:T(8,128)S(1)} %get-tuple-element.12), channel_id=1, source_target_pairs={{1,2},{2,1},{3,4},{4,3},{5,6},{6,5},{7,8},{8,7},{9,10},{10,9},{11,... | collective-permute-start | bytes 233480 | tf_op jit(solution)/shard_map/ppermute | solution.py:413

commit v6 on v4

--- a/solution.py
+++ b/solution.py
@@ -224,7 +224,7 @@
         up, down = (v.reshape(-1, TAIL, lanes) for v in (up, down))
         where = pl.ds(tile, up.shape[0])
         msg_a[where] = jnp.where(even, up, down)
-        msg_b[where] = jnp.where(even, down, up)
+        msg_b[0, where] = msg_b[1, where] = jnp.where(even, down, up)
 
     put(0, masks[layers - 1], masks[0])
     for c in copies:
@@ -343,7 +343,7 @@
     lower = lax.rem(me, 2) == 0
     valid = jnp.where(lower, me > 0, me < count - 1)
     ln = Lanes(faces.shape[2:], width)
-    work_side(ln, lower, valid, faces, masks, msg, store_side(ln, side, lower, blocks))
+    work_side(ln, lower, valid, faces, masks, msg.at[jnp.where(lower, 0, 1)], store_side(ln, side, lower, blocks))
     for c in send_side(side, out, lower, width, sems):
         c.start()
     for c in send_side(side, out, lower, width, sems):
@@ -354,7 +354,13 @@
     return [pair for i in firsts for pair in ((i, i + 1), (i + 1, i))]
 
 
-def on_device(trans_east, trans_north, trans_up, storage, support_reach, *, axis, count):
+def outside_pairs(parts, count):
+    inner = [[p * count + i, p * count + i + 1] for p in range(parts) for i in range(1, count - 1, 2)]
+    ends = [[p * count + i, (p + 1) * count + i] for p in range(0, parts, 2) for i in (0, count - 1)]
+    return inner + ends
+
+
+def on_device(trans_east, trans_north, trans_up, storage, support_reach, *, axis, count, parts):
     layers, blocks, _ = support_reach.shape
     n, rows, lanes = trans_east.shape
     width = n // layers
@@ -373,7 +379,7 @@
         functools.partial(pack_kernel, n, width, axis),
         out_shape=(
             pltpu.VMEM((tiles + 1, TAIL, lanes), f32),
-            pltpu.VMEM((tiles, TAIL, lanes), f32),
+            pltpu.VMEM((2, tiles, TAIL, lanes), f32),
             pltpu.VMEM((layers, TAIL, lanes), f32),
             pltpu.VMEM((4, n, rows, lanes), f32),
         ),
@@ -387,7 +393,7 @@
         name="pack",
     )(*outside, reach)
     got_a = lax.ppermute(msg_a, axis, swaps(range(0, count - 1, 2)))
-    got_b = lax.ppermute(msg_b, axis, swaps(range(1, count - 1, 2)))
+    got_b = lax.all_to_all(msg_b, ("groups", axis), 0, 0, axis_index_groups=outside_pairs(parts, count))
 
     out_shape = jax.ShapeDtypeStruct((layers, blocks, 3 * width, rows, lanes), f32)
     sends = layers * ((width - 4) // CHUNK) + 2 * (layers - 1)
@@ -424,7 +430,7 @@
 def solution(mesh):
     spread = P(("groups", "blk"))
     return jax.shard_map(
-        functools.partial(on_device, axis="blk", count=mesh.shape["blk"]),
+        functools.partial(on_device, axis="blk", count=mesh.shape["blk"], parts=mesh.shape["groups"]),
         mesh=mesh,
         in_specs=(spread,) * 5,
         out_specs=spread,

time: 10.1 us -> 12 us (1.19)
  the two profiles are of different devices: /device:TPU:1 before, /device:TPU:0 now
where the time goes in v6:
time: 12 us; the launch traced here: 11.8 us
  Pallas kernels  5.9 us (49%)
  starting transfers between devices  4.36 us (36%)
  waiting for transfers between devices  1.56 us (13%)
    all_to_all x1, starting transfers between devices, on_device(): lax.all_to_all(msg_b, ('groups', axis), 0, 0, axis_index_groups=outside_p...  4.22 us
    pallas_call x1, Pallas kernels, on_device(): pl.pallas_call(functools.partial(bulk_kernel, width, blocks, axis, count)...  3.02 us
    pallas_call x1, Pallas kernels, on_device(): pl.pallas_call(functools.partial(pack_kernel, n, width, axis), out_shape=...  1.91 us
    ppermute x1, waiting for transfers between devices, on_device(): got_a = lax.ppermute(msg_a, axis, swaps(range(0, count - 1, 2)))  1.13 us
    pallas_call x1, Pallas kernels, on_device(): pl.pallas_call(functools.partial(edge_kernel, width, blocks, axis, count)...  0.96 us
    all_to_all x1, waiting for transfers between devices, on_device(): lax.all_to_all(msg_b, ('groups', axis), 0, 0, axis_index_groups=outside_p...  0.43 us
  transfers between devices with their start and end apart: 2, of which 2 were waited for; matrix products, arithmetic and copies ran while one was open for 0% of the time, Pallas kernels for 26%

profile of v6, /device:TPU:0, one launch (start us, length us, event | category | flops | bytes accessed | tf_op | source)
XLA Modules:
  0.0 11.8 jit_solution(9308916378172531631)
XLA Ops:
  0.0 1.9 %pack.1 = (f32[20,8,128]{2,1,0:T(8,128)S(1)}, f32[2,19,8,128]{3,2,1,0:T(8,128)}, f32[2,8,128]{2,1,0:T(8,128)S(1)}, f32[4,32,16,128]{3,2,1,0:T(8,128)S(1)}) custom-call(f32[32,16,128]{2,1,0:T(8,128)} %tx.1, f32[32,16,128]{2,1,0:T(8,128)} %ty.1, f32[32,16,128]{2,1,0:T(8,128)} %tz.1, f32[32,16,128]{2,1,0:T(8,128)} %s.1, s32[2,4,8]{2,1,0:T(4,128)} %bitcast.1), custom_call_target="tpu_custom_call" | custom-call | tf_op jit(solution)/shard_map/pack/pallas_call | solution.py:378
  1.9 4.2 %all-to-all-start = ((f32[2,19,8,128]{3,2,1,0:T(8,128)}), f32[2,19,8,128]{3,2,1,0:T(8,128)S(1)}, u32[]{:S(2)}, u32[]{:S(2)}) async-start(f32[2,19,8,128]{3,2,1,0:T(8,128)} %get-tuple-element.11), calls=%async_computation | async-start | bytes 311296 | tf_op jit(solution)/shard_map/all_to_all | solution.py:396
  6.1 0.1 %collective-permute-start = (f32[20,8,128]{2,1,0:T(8,128)S(1)}, f32[20,8,128]{2,1,0:T(8,128)S(1)}, u32[]{:S(2)}, u32[]{:S(2)}) collective-permute-start(f32[20,8,128]{2,1,0:T(8,128)S(1)} %get-tuple-element.12), channel_id=1, source_target_pairs={{0,1},{1,0},{2,3},{3,2},{4,5},{5,4},{6,7},{7,6},{8,9},{9,8},{10,11... | collective-permute-start | bytes 245768 | tf_op jit(solution)/shard_map/ppermute | solution.py:395
  6.3 1.1 %collective-permute-done.msg = f32[20,8,128]{2,1,0:T(8,128)S(1)} collective-permute-done((f32[20,8,128]{2,1,0:T(8,128)S(1)}, f32[20,8,128]{2,1,0:T(8,128)S(1)}, u32[]{:S(2)}, u32[]{:S(2)}) %collective-permute-start) | collective-permute-done | bytes 81952 | tf_op jit(solution)/shard_map/ppermute | solution.py:395
  7.4 3.0 %bulk.1.held = f32[2,8,48,16,128]{4,3,2,1,0:T(8,128)} custom-call(f32[4,32,16,128]{3,2,1,0:T(8,128)S(1)} %get-tuple-element.9.faces, f32[2,8,128]{2,1,0:T(8,128)S(1)} %get-tuple-element.10.masks, f32[20,8,128]{2,1,0:T(8,128)S(1)} %collective-permute-done.msg), custom_call_target="tpu_custom_call" | custom-call | flops 10000000 | bytes 7000000 | tf_op jit(solution)/shard_map/bulk/pallas_call | solution.py:401
  10.4 0.4 %all-to-all-done.msg = f32[2,19,8,128]{3,2,1,0:T(8,128)S(1)} async-done(((f32[2,19,8,128]{3,2,1,0:T(8,128)}), f32[2,19,8,128]{3,2,1,0:T(8,128)S(1)}, u32[]{:S(2)}, u32[]{:S(2)}) %all-to-all-start) | async-done | bytes 155680 | tf_op jit(solution)/shard_map/all_to_all | solution.py:396
  10.9 1.0 %edges.1 = f32[2,8,48,16,128]{4,3,2,1,0:T(8,128)} custom-call(f32[4,32,16,128]{3,2,1,0:T(8,128)S(1)} %get-tuple-element.9.faces, f32[2,8,128]{2,1,0:T(8,128)S(1)} %get-tuple-element.10.masks, f32[2,19,8,128]{3,2,1,0:T(8,128)S(1)} %all-to-all-done.msg, f32[2,8,48,16,128]{4,3,2,1,0:T(8,128)} %bulk.1.held), custom_call_target="tpu_custom_call", output_to_operand_aliasing={{}: (3, {})} | custom-call | flops 1000000 | bytes 1000000 | tf_op jit(solution)/shard_map/edges/pallas_call | solution.py:417
Async XLA Ops:
  1.9 9.0 %all-to-all-start = ((f32[2,19,8,128]{3,2,1,0:T(8,128)}), f32[2,19,8,128]{3,2,1,0:T(8,128)S(1)}, u32[]{:S(2)}, u32[]{:S(2)}) async-start(f32[2,19,8,128]{3,2,1,0:T(8,128)} %get-tuple-element.11), calls=%async_computation | async-start | bytes 311296 | tf_op jit(solution)/shard_map/all_to_all | solution.py:396
  6.1 1.3 %collective-permute-start = (f32[20,8,128]{2,1,0:T(8,128)S(1)}, f32[20,8,128]{2,1,0:T(8,128)S(1)}, u32[]{:S(2)}, u32[]{:S(2)}) collective-permute-start(f32[20,8,128]{2,1,0:T(8,128)S(1)} %get-tuple-element.12), channel_id=1, source_target_pairs={{0,1},{1,0},{2,3},{3,2},{4,5},{5,4},{6,7},{7,6},{8,9},{9,8},{10,11... | collective-permute-start | bytes 245768 | tf_op jit(solution)/shard_map/ppermute | solution.py:395

commit v7 on v4

--- a/solution.py
+++ b/solution.py
@@ -9,8 +9,7 @@
 
 
 TAIL = 8
-CHUNK = 12
-SPLIT = 2
+LAST_RUNS = 4
 
 
 class Lanes:
@@ -126,6 +125,14 @@
     vx = vx + p.tz * jnp.where(ln.first, 0.0, xm) + p.tzp * jnp.where(ln.last, 0.0, xp)
     vd = face * own.z1 + p.tz * jnp.where(ln.first, xm, 0.0) + p.tzp * jnp.where(ln.last, xp, 0.0)
     return vx, vd
+
+
+def store(ln, dst, plane, blocks, own, other, total):
+    scale = 1.0 / total
+    own = own * scale
+    other = jnp.zeros_like(own) if other is None else other * scale
+    for k in range(blocks):
+        dst[k, plane] = jnp.where(ln.block == k, own, jnp.where(ln.other == k, other, 0.0))
 
 
 def work_side(ln, low, valid, faces, masks, msg, put):
@@ -172,20 +179,25 @@
     return put
 
 
-def send_side(buf, out, low, width, sems):
-    layers, blocks = out.shape[:2]
+def send_side(buf, out, low, width, layers, sems):
+    blocks = buf.shape[0]
     layer = jnp.where(low, 0, layers - 1)
     start = jnp.where(low, width - 2, 2 * width - 2)
     for k in range(blocks):
-        yield pltpu.make_async_copy(buf.at[k], out.at[layer, k, pl.ds(start, 4)], sems.at[k])
-
-
-def store(ln, dst, plane, blocks, own, other, total):
-    scale = 1.0 / total
-    own = own * scale
-    other = jnp.zeros_like(own) if other is None else other * scale
-    for k in range(blocks):
-        dst[k, plane] = jnp.where(ln.block == k, own, jnp.where(ln.other == k, other, 0.0))
+        there = out.at[pl.ds((layer * blocks + k) * 3 * width + start, 4)]
+        yield pltpu.make_async_copy(buf.at[k], there, sems.at[k])
+
+
+def zero_runs(bases, width):
+    box, far = 3 * width, width - 2
+    return [(0, far)] + [(b * box + 2 * width + 2, 2 * far if b < bases - 1 else far) for b in range(bases)]
+
+
+def zero_copies(zeros, out, runs, sems):
+    return [
+        pltpu.make_async_copy(zeros.at[pl.ds(0, count)], out.at[pl.ds(start, count)], sems.at[i])
+        for i, (start, count) in enumerate(runs)
+    ]
 
 
 def pack_kernel(
@@ -235,48 +247,27 @@
     put(17, faces[0, n - 1], faces[0, 2])
 
 
-def bulk_kernel(width, blocks, axis, count, faces, masks, msg, out, zeros, buf, side, sems, side_sems):
+def bulk_kernel(
+    width, blocks, axis, count, faces, masks, msg, out, zeros, buf, side, sems, side_sems, zero_sems
+):
     layers = masks.shape[0]
     rows, lanes = faces.shape[2:]
-    depth = zeros.shape[0]
+    runs = zero_runs(layers * blocks, width)
+    clears = zero_copies(zeros, out, runs[: len(runs) - LAST_RUNS], zero_sems)
     zeros[...] = jnp.zeros(zeros.shape, jnp.float32)
-
-    def clears(k):
-        for layer in range(layers):
-            for side, start in enumerate((0, 3 * width - depth)):
-                sem = sems.at[(layer * 2 + side) * blocks + k]
-                yield pltpu.make_async_copy(zeros, out.at[layer, k, pl.ds(start, depth)], sem)
-
-    def send(layer, start, planes, index):
-        for i in range(SPLIT):
-            few = pl.ds(i * (blocks // SPLIT), blocks // SPLIT)
+    for c in clears:
+        c.start()
+    ln = Lanes((rows, lanes), width)
+    plane = functools.partial(plane_at, ln, faces)
+
+    def send(layer, start, planes, slot):
+        for k in range(blocks):
+            base = (layer * blocks + k) * 3 * width + width - 2
             yield pltpu.make_async_copy(
-                buf.at[layer, few, pl.ds(start, planes)],
-                out.at[layer, few, pl.ds(width - 2 + start, planes)],
-                sems.at[2 * layers * blocks + index * SPLIT + i],
+                buf.at[layer, k, pl.ds(start, planes)],
+                out.at[pl.ds(base + start, planes)],
+                sems.at[slot * blocks + k],
             )
-
-    @pl.loop(0, blocks)
-    def _(k):
-        for c in clears(k):
-            c.start()
-
-    ln = Lanes((rows, lanes), width)
-
-    plane = functools.partial(plane_at, ln, faces)
-    chunks = (width - 4) // CHUNK
-
-    @pl.loop(0, layers * chunks)
-    def _(i):
-        layer = i // chunks
-        first = 2 + (i - layer * chunks) * CHUNK
-        planes = [plane(layer * width + first + j) for j in range(-1, CHUNK + 1)]
-        mz = masks[layer, 0:1]
-        for j in range(CHUNK):
-            vo, vz, total = middle(planes[j + 1], planes[j], planes[j + 2], mz)
-            store(ln, buf.at[layer], first + j + 2, blocks, vo, vz, total)
-        for c in send(layer, first + 2, CHUNK, i):
-            c.start()
 
     @pl.loop(1, layers)
     def _(layer):
@@ -305,48 +296,56 @@
         vo, vz, vx, total = second(b1, b0, b2, True, mb, to_above)
         high(3, blocks, vo, vz, total)
         low(width + 3, blocks, vx, None, total)
-        index = layers * chunks + 2 * (layer - 1)
-        for c in send(layer - 1, width, 4, index):
+
+    def span(layer):
+        if layers == 1:
+            return 4, width - 4
+        return jnp.where(layer == 0, 4, 0), width
+
+    @pl.loop(0, layers)
+    def _(layer):
+        planes = [plane(layer * width + j) for j in range(1, width - 1)]
+        mz = masks[layer, 0:1]
+        for j in range(2, width - 2):
+            vo, vz, total = middle(planes[j - 1], planes[j - 2], planes[j], mz)
+            store(ln, buf.at[layer], j + 2, blocks, vo, vz, total)
+        for c in send(layer, *span(layer), layer):
             c.start()
-        for c in send(layer, 0, 4, index + 1):
-            c.start()
+
+    rest = [c for layer in range(1, layers - 1) for c in send(layer, width, 4, layers + layer)]
+    for c in rest:
+        c.start()
 
     me = lax.axis_index(axis)
     lower = lax.rem(me, 2) == 1
     work_side(ln, lower, lower | (me < count - 1), faces, masks, msg, store_side(ln, side, lower, blocks))
-    for c in send_side(side, out, lower, width, side_sems):
-        c.start()
-
+    for c in send_side(side, out, lower, width, layers, side_sems):
+        c.start()
     for layer in range(layers):
-        for i in range(chunks):
-            for c in send(layer, 4 + i * CHUNK, CHUNK, layer * chunks + i):
-                c.wait()
-    for layer in range(1, layers):
-        index = layers * chunks + 2 * (layer - 1)
-        for c in send(layer - 1, width, 4, index):
-            c.wait()
-        for c in send(layer, 0, 4, index + 1):
-            c.wait()
-
-    for c in send_side(side, out, lower, width, side_sems):
+        rest += send(layer, *span(layer), layer)
+    rest += send_side(side, out, lower, width, layers, side_sems)
+    for c in clears + rest:
         c.wait()
 
-    @pl.loop(0, blocks)
-    def _(k):
-        for c in clears(k):
-            c.wait()
-
-
-def edge_kernel(width, blocks, axis, count, faces, masks, msg, held, out, side, sems):
+
+def edge_kernel(
+    width, blocks, axis, count, faces, masks, msg, held, out, zeros, side, sems, zero_sems
+):
     del held
+    layers = masks.shape[0]
+    runs = zero_runs(layers * blocks, width)
+    clears = zero_copies(zeros, out, runs[len(runs) - LAST_RUNS :], zero_sems)
+    zeros[...] = jnp.zeros(zeros.shape, jnp.float32)
+    for c in clears:
+        c.start()
     me = lax.axis_index(axis)
     lower = lax.rem(me, 2) == 0
     valid = jnp.where(lower, me > 0, me < count - 1)
     ln = Lanes(faces.shape[2:], width)
     work_side(ln, lower, valid, faces, masks, msg, store_side(ln, side, lower, blocks))
-    for c in send_side(side, out, lower, width, sems):
-        c.start()
-    for c in send_side(side, out, lower, width, sems):
+    for c in send_side(side, out, lower, width, layers, sems):
+        c.start()
+    for c in clears + list(send_side(side, out, lower, width, layers, sems)):
         c.wait()
 
 
@@ -389,36 +388,44 @@
     got_a = lax.ppermute(msg_a, axis, swaps(range(0, count - 1, 2)))
     got_b = lax.ppermute(msg_b, axis, swaps(range(1, count - 1, 2)))
 
-    out_shape = jax.ShapeDtypeStruct((layers, blocks, 3 * width, rows, lanes), f32)
-    sends = layers * ((width - 4) // CHUNK) + 2 * (layers - 1)
+    bases = layers * blocks
+    out_shape = jax.ShapeDtypeStruct((bases * 3 * width, rows, lanes), f32)
     side = pltpu.VMEM((blocks, 4, rows, lanes), f32)
+    zeros = pltpu.VMEM((2 * (width - 2), rows, lanes), f32)
     bulk = pl.pallas_call(
         functools.partial(bulk_kernel, width, blocks, axis, count),
         out_shape=out_shape,
         in_specs=[vmem] * 3,
         out_specs=anywhere,
         scratch_shapes=[
-            pltpu.VMEM((width - 2, rows, lanes), f32),
+            zeros,
             pltpu.VMEM((layers, blocks, width + 4, rows, lanes), f32),
             side,
-            pltpu.SemaphoreType.DMA((2 * layers * blocks + sends * SPLIT,)),
+            pltpu.SemaphoreType.DMA((2 * layers * blocks,)),
             pltpu.SemaphoreType.DMA((blocks,)),
+            pltpu.SemaphoreType.DMA((bases + 1 - LAST_RUNS,)),
         ],
         compiler_params=params,
         cost_estimate=pl.CostEstimate(flops=10**7, bytes_accessed=7 * 10**6, transcendentals=0),
         name="bulk",
     )(faces, masks, got_a)
-    return pl.pallas_call(
+    out = pl.pallas_call(
         functools.partial(edge_kernel, width, blocks, axis, count),
         out_shape=out_shape,
         in_specs=[vmem] * 3 + [anywhere],
         out_specs=anywhere,
-        scratch_shapes=[side, pltpu.SemaphoreType.DMA((blocks,))],
+        scratch_shapes=[
+            zeros,
+            side,
+            pltpu.SemaphoreType.DMA((blocks,)),
+            pltpu.SemaphoreType.DMA((LAST_RUNS,)),
+        ],
         input_output_aliases={3: 0},
         compiler_params=params,
         cost_estimate=pl.CostEstimate(flops=10**6, bytes_accessed=10**6, transcendentals=0),
         name="edges",
     )(faces, masks, got_b, bulk)
+    return out.reshape(layers, blocks, 3 * width, rows, lanes)
 
 
 def solution(mesh):

time: 10.1 us -> 10.2 us (level)
    pallas_call x1, Pallas kernels: 0.97 us -> 1.19 us  [on_device(): pl.pallas_call(functools.partial(edge_kernel, width, blocks, axis, count)...]
    pallas_call x1, Pallas kernels: 3.02 us -> 2.89 us  [on_device(): pl.pallas_call(functools.partial(bulk_kernel, width, blocks, axis, count)...]
  transfers between devices with their start and end apart: 2 -> 2, of which waited for: 0 -> 0; matrix products, arithmetic and copies ran while one was open for 0% -> 0% of each run, Pallas kernels for 31% -> 29%
where the time goes in v7:
time: 10.2 us; the launch traced here: 10 us
  Pallas kernels  5.33 us (52%)
  starting transfers between devices  4.62 us (45%)
    ppermute x1, starting transfers between devices, on_device(): got_b = lax.ppermute(msg_b, axis, swaps(range(1, count - 1, 2)))  4.49 us
    pallas_call x1, Pallas kernels, on_device(): pl.pallas_call(functools.partial(bulk_kernel, width, blocks, axis, count)...  2.89 us
    pallas_call x1, Pallas kernels, on_device(): pl.pallas_call(functools.partial(pack_kernel, n, width, axis), out_shape=...  1.26 us
    pallas_call x1, Pallas kernels, on_device(): pl.pallas_call(functools.partial(edge_kernel, width, blocks, axis, count)...  1.19 us
  transfers between devices with their start and end apart: 2, of which 0 were waited for; matrix products, arithmetic and copies ran while one was open for 0% of the time, Pallas kernels for 29%

profile of v7, /device:TPU:1, one launch (start us, length us, event | category | flops | bytes accessed | tf_op | source)
XLA Modules:
  0.0 10.0 jit_solution(10872911251573007285)
XLA Ops:
  0.0 1.3 %pack.1 = (f32[20,8,128]{2,1,0:T(8,128)S(1)}, f32[19,8,128]{2,1,0:T(8,128)S(1)}, f32[2,8,128]{2,1,0:T(8,128)S(1)}, f32[4,32,16,128]{3,2,1,0:T(8,128)S(1)}) custom-call(f32[32,16,128]{2,1,0:T(8,128)} %tx.1, f32[32,16,128]{2,1,0:T(8,128)} %ty.1, f32[32,16,128]{2,1,0:T(8,128)} %tz.1, f32[32,16,128]{2,1,0:T(8,128)} %s.1, s32[2,4,8]{2,1,0:T(4,128)} %bitcast.2), custom_call_target="tpu_custom_call" | custom-call | tf_op jit(solution)/shard_map/pack/pallas_call | solution.py:371
  1.3 0.1 %collective-permute-start.1 = (f32[20,8,128]{2,1,0:T(8,128)S(1)}, f32[20,8,128]{2,1,0:T(8,128)S(1)}, u32[]{:S(2)}, u32[]{:S(2)}) collective-permute-start(f32[20,8,128]{2,1,0:T(8,128)S(1)} %get-tuple-element.12), channel_id=1, source_target_pairs={{0,1},{1,0},{2,3},{3,2},{4,5},{5,4},{6,7},{7,6},{8,9},{9,8},{10,11... | collective-permute-start | bytes 245768 | tf_op jit(solution)/shard_map/ppermute | solution.py:388
  1.4 4.5 %collective-permute-start = (f32[19,8,128]{2,1,0:T(8,128)S(1)}, f32[19,8,128]{2,1,0:T(8,128)S(1)}, u32[]{:S(2)}, u32[]{:S(2)}) collective-permute-start(f32[19,8,128]{2,1,0:T(8,128)S(1)} %get-tuple-element.11), channel_id=1, source_target_pairs={{1,2},{2,1},{3,4},{4,3},{5,6},{6,5},{7,8},{8,7},{9,10},{10,9},{11,... | collective-permute-start | bytes 233480 | tf_op jit(solution)/shard_map/ppermute | solution.py:389
  5.9 0.0 collective-permute-done.1.msg
  5.9 2.9 %bulk.1.held = f32[768,16,128]{2,1,0:T(8,128)} custom-call(f32[4,32,16,128]{3,2,1,0:T(8,128)S(1)} %get-tuple-element.9.faces, f32[2,8,128]{2,1,0:T(8,128)S(1)} %get-tuple-element.10.masks, f32[20,8,128]{2,1,0:T(8,128)S(1)} %collective-permute-done.1.msg), custom_call_target="tpu_custom_call" | custom-call | flops 10000000 | bytes 7000000 | tf_op jit(solution)/shard_map/bulk/pallas_call | solution.py:395
  8.8 0.0 collective-permute-done.msg
  8.8 1.2 %edges.1 = f32[768,16,128]{2,1,0:T(8,128)} custom-call(f32[4,32,16,128]{3,2,1,0:T(8,128)S(1)} %get-tuple-element.9.faces, f32[2,8,128]{2,1,0:T(8,128)S(1)} %get-tuple-element.10.masks, f32[19,8,128]{2,1,0:T(8,128)S(1)} %collective-permute-done.msg, f32[768,16,128]{2,1,0:T(8,128)} %bulk.1.held), custom_call_target="tpu_custom_call", output_to_operand_aliasing={{}: (3, {})} | custom-call | flops 1000000 | bytes 1000000 | tf_op jit(solution)/shard_map/edges/pallas_call | solution.py:412
Async XLA Ops:
  1.3 4.6 %collective-permute-start.1 = (f32[20,8,128]{2,1,0:T(8,128)S(1)}, f32[20,8,128]{2,1,0:T(8,128)S(1)}, u32[]{:S(2)}, u32[]{:S(2)}) collective-permute-start(f32[20,8,128]{2,1,0:T(8,128)S(1)} %get-tuple-element.12), channel_id=1, source_target_pairs={{0,1},{1,0},{2,3},{3,2},{4,5},{5,4},{6,7},{7,6},{8,9},{9,8},{10,11... | collective-permute-start | bytes 245768 | tf_op jit(solution)/shard_map/ppermute | solution.py:388
  1.4 7.4 %collective-permute-start = (f32[19,8,128]{2,1,0:T(8,128)S(1)}, f32[19,8,128]{2,1,0:T(8,128)S(1)}, u32[]{:S(2)}, u32[]{:S(2)}) collective-permute-start(f32[19,8,128]{2,1,0:T(8,128)S(1)} %get-tuple-element.11), channel_id=1, source_target_pairs={{1,2},{2,1},{3,4},{4,3},{5,6},{6,5},{7,8},{8,7},{9,10},{10,9},{11,... | collective-permute-start | bytes 233480 | tf_op jit(solution)/shard_map/ppermute | solution.py:389

commit v8 on v7

--- a/solution.py
+++ b/solution.py
@@ -9,24 +9,28 @@
 
 
 TAIL = 8
-LAST_RUNS = 4
 
 
 class Lanes:
     def __init__(self, shape, width):
-        lane = lax.broadcasted_iota(jnp.int32, shape, 1)
+        tile = lax.broadcasted_iota(jnp.int32, (TAIL, shape[1]), 1)
+
+        def rows(v):
+            return jnp.concatenate([v] * (shape[0] // TAIL), axis=0)
+
+        self.rows, self.lanes = shape
         self.width = width
-        self.lanes = shape[1]
-        self.rows = shape[0]
-        self.lane = lane
-        self.block = lane // width
-        self.local = lane - self.block * width
+        self.lane = rows(tile)
+        self.local = rows(lax.rem(tile, width))
         self.first = self.local == 0
         self.last = self.local == width - 1
-        self.upper = self.local >= width // 2
-        self.other = jnp.where(self.upper, self.block + 1, self.block - 1)
+        self.odd = rows(lax.rem(tile // width, 2)) == 1
         self.row0 = lax.broadcasted_iota(jnp.int32, shape, 0) == 0
-        self.lane0 = lane == 0
+        self.lane0 = self.lane == 0
+
+    def around(self, k):
+        start = k * self.width - self.width // 2
+        return (self.lane >= start) & (self.lane < start + 2 * self.width)
 
     def zm(self, v):
         return pltpu.roll(v, 1, 1)
@@ -39,6 +43,11 @@
 
     def yp(self, v):
         return pltpu.roll(v, self.rows - 1, 0)
+
+
+def reciprocal(x):
+    r = pl.reciprocal(x, approx=True)
+    return r * (2.0 - x * r)
 
 
 class Plane:
@@ -54,7 +63,7 @@
             e = jnp.where(valid, e, 1.0)
         self.half = 0.5 * e + s * (1.0 / 3.0)
         self.all = 1.5 * e
-        self.q = 1.0 / self.all
+        self.q = reciprocal(self.all)
         self.z1 = self.q * jnp.where(ln.first, self.tz, jnp.where(ln.last, self.tzp, 0.0))
         self.zm = ln.zm(self.z1)
         self.zp = ln.zp(self.z1)
@@ -128,11 +137,12 @@
 
 
 def store(ln, dst, plane, blocks, own, other, total):
-    scale = 1.0 / total
+    scale = reciprocal(total)
     own = own * scale
     other = jnp.zeros_like(own) if other is None else other * scale
+    even, odd = jnp.where(ln.odd, other, own), jnp.where(ln.odd, own, other)
     for k in range(blocks):
-        dst[k, plane] = jnp.where(ln.block == k, own, jnp.where(ln.other == k, other, 0.0))
+        dst[k, plane] = jnp.where(ln.around(k), odd if k % 2 else even, 0.0)
 
 
 def work_side(ln, low, valid, faces, masks, msg, put):
@@ -179,25 +189,11 @@
     return put
 
 
-def send_side(buf, out, low, width, layers, sems):
-    blocks = buf.shape[0]
+def send_one_side(buf, out, low, width, layers, sems, k):
     layer = jnp.where(low, 0, layers - 1)
     start = jnp.where(low, width - 2, 2 * width - 2)
-    for k in range(blocks):
-        there = out.at[pl.ds((layer * blocks + k) * 3 * width + start, 4)]
-        yield pltpu.make_async_copy(buf.at[k], there, sems.at[k])
-
-
-def zero_runs(bases, width):
-    box, far = 3 * width, width - 2
-    return [(0, far)] + [(b * box + 2 * width + 2, 2 * far if b < bases - 1 else far) for b in range(bases)]
-
-
-def zero_copies(zeros, out, runs, sems):
-    return [
-        pltpu.make_async_copy(zeros.at[pl.ds(0, count)], out.at[pl.ds(start, count)], sems.at[i])
-        for i, (start, count) in enumerate(runs)
-    ]
+    there = out.at[pl.ds((layer * buf.shape[0] + k) * 3 * width + start, 4)]
+    return pltpu.make_async_copy(buf.at[k], there, sems.at[k])
 
 
 def pack_kernel(
@@ -252,25 +248,37 @@
 ):
     layers = masks.shape[0]
     rows, lanes = faces.shape[2:]
-    runs = zero_runs(layers * blocks, width)
-    clears = zero_copies(zeros, out, runs[: len(runs) - LAST_RUNS], zero_sems)
+    box, depth = 3 * width, width - 2
+    bases = layers * blocks
     zeros[...] = jnp.zeros(zeros.shape, jnp.float32)
-    for c in clears:
-        c.start()
+
+    def clear(b, count):
+        there = out.at[pl.ds(b * box - depth, count)]
+        return pltpu.make_async_copy(zeros.at[pl.ds(0, count)], there, zero_sems.at[b])
+
+    first = pltpu.make_async_copy(zeros.at[pl.ds(0, depth)], out.at[pl.ds(0, depth)], zero_sems.at[0])
+    first.start()
+    clear(bases, depth).start()
+
+    @pl.loop(1, bases)
+    def _(b):
+        clear(b, 2 * depth).start()
+
     ln = Lanes((rows, lanes), width)
     plane = functools.partial(plane_at, ln, faces)
-
-    def send(layer, start, planes, slot):
-        for k in range(blocks):
-            base = (layer * blocks + k) * 3 * width + width - 2
-            yield pltpu.make_async_copy(
-                buf.at[layer, k, pl.ds(start, planes)],
-                out.at[pl.ds(base + start, planes)],
-                sems.at[slot * blocks + k],
-            )
-
-    @pl.loop(1, layers)
-    def _(layer):
+    me = lax.axis_index(axis)
+    lower = lax.rem(me, 2) == 1
+
+    def send(k, layer):
+        start = 4 if layer == 0 else 0
+        count = width + 4 - start - (4 if layer == layers - 1 else 0)
+        return pltpu.make_async_copy(
+            buf.at[layer, k, pl.ds(start, count)],
+            out.at[pl.ds((layer * blocks + k) * box + depth + start, count)],
+            sems.at[layer * blocks + k],
+        )
+
+    def between(layer):
         base = layer * width
         ma, mb = masks[layer - 1, 0:1], masks[layer, 0:1]
         to_above, to_below = masks[layer - 1, 2:3], masks[layer, 1:2]
@@ -297,55 +305,50 @@
         high(3, blocks, vo, vz, total)
         low(width + 3, blocks, vx, None, total)
 
-    def span(layer):
-        if layers == 1:
-            return 4, width - 4
-        return jnp.where(layer == 0, 4, 0), width
-
-    @pl.loop(0, layers)
-    def _(layer):
+    for layer in range(layers):
         planes = [plane(layer * width + j) for j in range(1, width - 1)]
         mz = masks[layer, 0:1]
         for j in range(2, width - 2):
             vo, vz, total = middle(planes[j - 1], planes[j - 2], planes[j], mz)
             store(ln, buf.at[layer], j + 2, blocks, vo, vz, total)
-        for c in send(layer, *span(layer), layer):
-            c.start()
-
-    rest = [c for layer in range(1, layers - 1) for c in send(layer, width, 4, layers + layer)]
-    for c in rest:
-        c.start()
-
-    me = lax.axis_index(axis)
-    lower = lax.rem(me, 2) == 1
-    work_side(ln, lower, lower | (me < count - 1), faces, masks, msg, store_side(ln, side, lower, blocks))
-    for c in send_side(side, out, lower, width, layers, side_sems):
-        c.start()
-    for layer in range(layers):
-        rest += send(layer, *span(layer), layer)
-    rest += send_side(side, out, lower, width, layers, side_sems)
-    for c in clears + rest:
-        c.wait()
-
-
-def edge_kernel(
-    width, blocks, axis, count, faces, masks, msg, held, out, zeros, side, sems, zero_sems
-):
+        if layer < layers - 1:
+            between(layer + 1)
+        else:
+            valid = lower | (me < count - 1)
+            work_side(ln, lower, valid, faces, masks, msg, store_side(ln, side, lower, blocks))
+
+        @pl.loop(0, blocks)
+        def _(k):
+            send(k, layer).start()
+            if layer == layers - 1:
+                send_one_side(side, out, lower, width, layers, side_sems, k).start()
+
+    first.wait()
+    clear(bases, depth).wait()
+
+    @pl.loop(1, bases)
+    def _(b):
+        clear(b, 2 * depth).wait()
+
+    @pl.loop(0, blocks)
+    def _(k):
+        for layer in range(layers):
+            send(k, layer).wait()
+        send_one_side(side, out, lower, width, layers, side_sems, k).wait()
+
+
+def edge_kernel(width, blocks, axis, count, faces, masks, msg, held, out, side, sems):
     del held
     layers = masks.shape[0]
-    runs = zero_runs(layers * blocks, width)
-    clears = zero_copies(zeros, out, runs[len(runs) - LAST_RUNS :], zero_sems)
-    zeros[...] = jnp.zeros(zeros.shape, jnp.float32)
-    for c in clears:
-        c.start()
     me = lax.axis_index(axis)
     lower = lax.rem(me, 2) == 0
     valid = jnp.where(lower, me > 0, me < count - 1)
     ln = Lanes(faces.shape[2:], width)
     work_side(ln, lower, valid, faces, masks, msg, store_side(ln, side, lower, blocks))
-    for c in send_side(side, out, lower, width, layers, sems):
+    copies = [send_one_side(side, out, lower, width, layers, sems, k) for k in range(blocks)]
+    for c in copies:
         c.start()
-    for c in clears + list(send_side(side, out, lower, width, layers, sems)):
+    for c in copies:
         c.wait()
 
 
@@ -401,9 +404,9 @@
             zeros,
             pltpu.VMEM((layers, blocks, width + 4, rows, lanes), f32),
             side,
-            pltpu.SemaphoreType.DMA((2 * layers * blocks,)),
+            pltpu.SemaphoreType.DMA((bases,)),
             pltpu.SemaphoreType.DMA((blocks,)),
-            pltpu.SemaphoreType.DMA((bases + 1 - LAST_RUNS,)),
+            pltpu.SemaphoreType.DMA((bases + 1,)),
         ],
         compiler_params=params,
         cost_estimate=pl.CostEstimate(flops=10**7, bytes_accessed=7 * 10**6, transcendentals=0),
@@ -415,10 +418,8 @@
         in_specs=[vmem] * 3 + [anywhere],
         out_specs=anywhere,
         scratch_shapes=[
-            zeros,
             side,
             pltpu.SemaphoreType.DMA((blocks,)),
-            pltpu.SemaphoreType.DMA((LAST_RUNS,)),
         ],
         input_output_aliases={3: 0},
         compiler_params=params,

time: 10.2 us -> 9.98 us (0.978)
  Pallas kernels: 5.33 us -> 5.14 us
    pallas_call x1, Pallas kernels: 1.19 us -> 0.97 us  [on_device(): pl.pallas_call(functools.partial(edge_kernel, width, blocks, axis, count)...]
  transfers between devices with their start and end apart: 2 -> 2, of which waited for: 0 -> 0; matrix products, arithmetic and copies ran while one was open for 0% -> 0% of each run, Pallas kernels for 29% -> 30%
where the time goes in v8:
time: 9.98 us; the launch traced here: 9.8 us
  Pallas kernels  5.14 us (52%)
  starting transfers between devices  4.62 us (46%)
    ppermute x1, starting transfers between devices, on_device(): got_b = lax.ppermute(msg_b, axis, swaps(range(1, count - 1, 2)))  4.49 us
    pallas_call x1, Pallas kernels, on_device(): pl.pallas_call(functools.partial(bulk_kernel, width, blocks, axis, count)...  2.91 us
    pallas_call x1, Pallas kernels, on_device(): pl.pallas_call(functools.partial(pack_kernel, n, width, axis), out_shape=...  1.26 us
    pallas_call x1, Pallas kernels, on_device(): pl.pallas_call(functools.partial(edge_kernel, width, blocks, axis, count)...  0.97 us
  transfers between devices with their start and end apart: 2, of which 0 were waited for; matrix products, arithmetic and copies ran while one was open for 0% of the time, Pallas kernels for 30%

profile of v8, /device:TPU:1, one launch (start us, length us, event | category | flops | bytes accessed | tf_op | source)
XLA Modules:
  0.0 9.8 jit_solution(2942632425345653597)
XLA Ops:
  0.0 1.3 %pack.1 = (f32[20,8,128]{2,1,0:T(8,128)S(1)}, f32[19,8,128]{2,1,0:T(8,128)S(1)}, f32[2,8,128]{2,1,0:T(8,128)S(1)}, f32[4,32,16,128]{3,2,1,0:T(8,128)S(1)}) custom-call(f32[32,16,128]{2,1,0:T(8,128)} %tx.1, f32[32,16,128]{2,1,0:T(8,128)} %ty.1, f32[32,16,128]{2,1,0:T(8,128)} %tz.1, f32[32,16,128]{2,1,0:T(8,128)} %s.1, s32[2,4,8]{2,1,0:T(4,128)} %bitcast.2), custom_call_target="tpu_custom_call" | custom-call | tf_op jit(solution)/shard_map/pack/pallas_call | solution.py:374
  1.3 0.1 %collective-permute-start.1 = (f32[20,8,128]{2,1,0:T(8,128)S(1)}, f32[20,8,128]{2,1,0:T(8,128)S(1)}, u32[]{:S(2)}, u32[]{:S(2)}) collective-permute-start(f32[20,8,128]{2,1,0:T(8,128)S(1)} %get-tuple-element.12), channel_id=1, source_target_pairs={{0,1},{1,0},{2,3},{3,2},{4,5},{5,4},{6,7},{7,6},{8,9},{9,8},{10,11... | collective-permute-start | bytes 245768 | tf_op jit(solution)/shard_map/ppermute | solution.py:391
  1.4 4.5 %collective-permute-start = (f32[19,8,128]{2,1,0:T(8,128)S(1)}, f32[19,8,128]{2,1,0:T(8,128)S(1)}, u32[]{:S(2)}, u32[]{:S(2)}) collective-permute-start(f32[19,8,128]{2,1,0:T(8,128)S(1)} %get-tuple-element.11), channel_id=1, source_target_pairs={{1,2},{2,1},{3,4},{4,3},{5,6},{6,5},{7,8},{8,7},{9,10},{10,9},{11,... | collective-permute-start | bytes 233480 | tf_op jit(solution)/shard_map/ppermute | solution.py:392
  5.9 0.0 collective-permute-done.1.msg
  5.9 2.9 %bulk.1.held = f32[768,16,128]{2,1,0:T(8,128)} custom-call(f32[4,32,16,128]{3,2,1,0:T(8,128)S(1)} %get-tuple-element.9.faces, f32[2,8,128]{2,1,0:T(8,128)S(1)} %get-tuple-element.10.masks, f32[20,8,128]{2,1,0:T(8,128)S(1)} %collective-permute-done.1.msg), custom_call_target="tpu_custom_call" | custom-call | flops 10000000 | bytes 7000000 | tf_op jit(solution)/shard_map/bulk/pallas_call | solution.py:398
  8.8 0.0 collective-permute-done.msg
  8.8 1.0 %edges.1 = f32[768,16,128]{2,1,0:T(8,128)} custom-call(f32[4,32,16,128]{3,2,1,0:T(8,128)S(1)} %get-tuple-element.9.faces, f32[2,8,128]{2,1,0:T(8,128)S(1)} %get-tuple-element.10.masks, f32[19,8,128]{2,1,0:T(8,128)S(1)} %collective-permute-done.msg, f32[768,16,128]{2,1,0:T(8,128)} %bulk.1.held), custom_call_target="tpu_custom_call", output_to_operand_aliasing={{}: (3, {})} | custom-call | flops 1000000 | bytes 1000000 | tf_op jit(solution)/shard_map/edges/pallas_call | solution.py:415
Async XLA Ops:
  1.3 4.6 %collective-permute-start.1 = (f32[20,8,128]{2,1,0:T(8,128)S(1)}, f32[20,8,128]{2,1,0:T(8,128)S(1)}, u32[]{:S(2)}, u32[]{:S(2)}) collective-permute-start(f32[20,8,128]{2,1,0:T(8,128)S(1)} %get-tuple-element.12), channel_id=1, source_target_pairs={{0,1},{1,0},{2,3},{3,2},{4,5},{5,4},{6,7},{7,6},{8,9},{9,8},{10,11... | collective-permute-start | bytes 245768 | tf_op jit(solution)/shard_map/ppermute | solution.py:391
  1.4 7.4 %collective-permute-start = (f32[19,8,128]{2,1,0:T(8,128)S(1)}, f32[19,8,128]{2,1,0:T(8,128)S(1)}, u32[]{:S(2)}, u32[]{:S(2)}) collective-permute-start(f32[19,8,128]{2,1,0:T(8,128)S(1)} %get-tuple-element.11), channel_id=1, source_target_pairs={{1,2},{2,1},{3,4},{4,3},{5,6},{6,5},{7,8},{8,7},{9,10},{10,9},{11,... | collective-permute-start | bytes 233480 | tf_op jit(solution)/shard_map/ppermute | solution.py:392

commit v9 on v8

--- a/solution.py
+++ b/solution.py
@@ -9,6 +9,7 @@
 
 
 TAIL = 8
+EARLY = 4
 
 
 class Lanes:
@@ -50,18 +51,26 @@
     return r * (2.0 - x * r)
 
 
+def cross(ln, ty, tz, s):
+    ty = jnp.where(ln.row0, 0.0, ty)
+    tz = jnp.where(ln.lane0, 0.0, tz)
+    typ, tzp = ln.yp(ty), ln.zp(tz)
+    return s * (1.0 / 3.0) + ((ty + typ) + (tz + tzp)), (ty, typ, tz, tzp)
+
+
 class Plane:
     def __init__(self, ln, tx, txn, ty, tz, s, valid=None):
         self.ln = ln
         self.tx, self.txn = tx, txn
-        self.ty = jnp.where(ln.row0, 0.0, ty)
-        self.tz = jnp.where(ln.lane0, 0.0, tz)
-        self.typ = ln.yp(self.ty)
-        self.tzp = ln.zp(self.tz)
-        e = s * (1.0 / 3.0) + ((tx + txn) + (self.ty + self.typ) + (self.tz + self.tzp))
+        e, (self.ty, self.typ, self.tz, self.tzp) = cross(ln, ty, tz, s)
+        e = e + (tx + txn)
         if valid is not None:
             e = jnp.where(valid, e, 1.0)
         self.half = 0.5 * e + s * (1.0 / 3.0)
+        self.spread(e)
+
+    def spread(self, e):
+        ln = self.ln
         self.all = 1.5 * e
         self.q = reciprocal(self.all)
         self.z1 = self.q * jnp.where(ln.first, self.tz, jnp.where(ln.last, self.tzp, 0.0))
@@ -83,6 +92,14 @@
 
     def along_y(self, v):
         return self.ty * self.ln.ym(v) + self.typ * self.ln.yp(v)
+
+
+class Rim(Plane):
+    def __init__(self, ln, e, tz):
+        self.ln = ln
+        self.tz = jnp.where(ln.lane0, 0.0, tz)
+        self.tzp = ln.zp(self.tz)
+        self.spread(e)
 
 
 def plane_at(ln, faces, p):
@@ -152,19 +169,18 @@
     def own(i, j):
         return faces[i, jnp.where(low, j, n - 1 - j)]
 
-    def got(i, j):
+    def got(i):
         tiles = rows // TAIL
-        return msg[pl.ds(1 + tiles * (2 * i + j), tiles)].reshape(rows, lanes)
+        return msg[pl.ds(1 + tiles * i, tiles)].reshape(rows, lanes)
 
     f1, f2, f3 = (faces[0, jnp.where(low, j, n - j)] for j in (1, 2, 3))
-    f0 = jnp.where(valid, jnp.where(low, faces[0, 0], got(0, 0)), 0.0)
-    g1 = jnp.where(low, got(0, 0), got(0, 1))
-    g2 = jnp.where(low, got(0, 1), got(4, 0))
+    f0 = jnp.where(valid, jnp.where(low, faces[0, 0], got(6)), 0.0)
+    g1 = got(0)
     a0 = Plane(ln, f0, f1, own(1, 0), own(2, 0), own(3, 0))
     a1 = Plane(ln, f1, f2, own(1, 1), own(2, 1), own(3, 1))
     a2 = Plane(ln, f2, f3, own(1, 2), own(2, 2), own(3, 2))
-    b0 = Plane(ln, g1, f0, got(1, 0), got(2, 0), got(3, 0), valid)
-    b1 = Plane(ln, g2, g1, got(1, 1), got(2, 1), got(3, 1), valid)
+    b0 = Plane(ln, g1, f0, got(1), got(2), got(3), valid)
+    b1 = Rim(ln, jnp.where(valid, got(4) + g1, 1.0), got(5))
     mine = masks[jnp.where(low, 0, layers - 1)]
     mz, my_reach = mine[0:1], jnp.where(low, mine[1:2], mine[2:3])
     theirs = msg[0]
@@ -196,8 +212,21 @@
     return pltpu.make_async_copy(buf.at[k], there, sems.at[k])
 
 
+def clear_run(zeros, out, b, bases, width, sem):
+    depth = width - 2
+    ends = isinstance(b, int) and b in (0, bases)
+    count = depth if ends else 2 * depth
+    start = 0 if ends and b == 0 else b * 3 * width - depth
+    return pltpu.make_async_copy(zeros.at[pl.ds(0, count)], out.at[pl.ds(start, count)], sem)
+
+
+def early_runs(bases):
+    return range(bases - EARLY, bases)
+
+
 def pack_kernel(
-    n, width, axis, tx, ty, tz, s, reach, msg_a, msg_b, masks, faces, held_reach, sems
+    n, width, axis, tx, ty, tz, s, reach, msg_a, msg_b, masks, faces, out,
+    held_reach, zeros, sems, zero_sems,
 ):
     layers, _, blocks = held_reach.shape
     lanes = masks.shape[-1]
@@ -208,6 +237,17 @@
     ]
     for c in copies:
         c.start()
+    rows = faces.shape[2]
+    bases = layers * blocks
+    clears = [clear_run(zeros, out, b, bases, width, zero_sems.at[i]) for i, b in enumerate(early_runs(bases))]
+    even = lax.rem(lax.axis_index(axis), 2) == 0
+
+    @pl.when(jnp.logical_not(even))
+    def _():
+        zeros[...] = jnp.zeros(zeros.shape, jnp.float32)
+        for c in clears:
+            c.start()
+
     masks[...] = jnp.zeros(masks.shape, jnp.float32)
     lane = lax.broadcasted_iota(jnp.int32, (4, lanes), 1)
     block = lane // width
@@ -226,7 +266,6 @@
         )
         masks[layer, 0:1] = near
         masks[layer, 1:3] = jnp.where(r[0:2] >= 2, 1.0, 0.0)
-    even = lax.rem(lax.axis_index(axis), 2) == 0
 
     def put(tile, up, down):
         up, down = (v.reshape(-1, TAIL, lanes) for v in (up, down))
@@ -237,37 +276,55 @@
     put(0, masks[layers - 1], masks[0])
     for c in copies:
         c.wait()
-    for i in range(4):
-        put(1 + 4 * i, faces[i, n - 1], faces[i, 0])
-        put(3 + 4 * i, faces[i, n - 2], faces[i, 1])
-    put(17, faces[0, n - 1], faces[0, 2])
+    ln = Lanes(faces.shape[2:], width)
+    top, _ = cross(ln, faces[1, n - 2], faces[2, n - 2], faces[3, n - 2])
+    low, _ = cross(ln, faces[1, 1], faces[2, 1], faces[3, 1])
+    ups = [faces[0, n - 1]] + [faces[i, n - 1] for i in (1, 2, 3)]
+    ups += [top + faces[0, n - 2], faces[2, n - 2], faces[0, n - 1]]
+    downs = [faces[0, 1]] + [faces[i, 0] for i in (1, 2, 3)]
+    downs += [low + faces[0, 2], faces[2, 1], faces[0, 0]]
+    for i, (up, down) in enumerate(zip(ups, downs)):
+        put(1 + i * (rows // TAIL), up, down)
+
+    @pl.when(jnp.logical_not(even))
+    def _():
+        for c in clears:
+            c.wait()
 
 
 def bulk_kernel(
-    width, blocks, axis, count, faces, masks, msg, out, zeros, buf, side, sems, side_sems, zero_sems
+    width, blocks, axis, count, faces, masks, msg, held, out, zeros, buf, side, sems, side_sems, zero_sems
 ):
+    del held
     layers = masks.shape[0]
     rows, lanes = faces.shape[2:]
     box, depth = 3 * width, width - 2
     bases = layers * blocks
     zeros[...] = jnp.zeros(zeros.shape, jnp.float32)
 
-    def clear(b, count):
-        there = out.at[pl.ds(b * box - depth, count)]
-        return pltpu.make_async_copy(zeros.at[pl.ds(0, count)], there, zero_sems.at[b])
-
-    first = pltpu.make_async_copy(zeros.at[pl.ds(0, depth)], out.at[pl.ds(0, depth)], zero_sems.at[0])
-    first.start()
-    clear(bases, depth).start()
-
-    @pl.loop(1, bases)
-    def _(b):
-        clear(b, 2 * depth).start()
-
+    me = lax.axis_index(axis)
+    lower = lax.rem(me, 2) == 1
+    early = early_runs(bases)
+
+    def clear(b):
+        return clear_run(zeros, out, b, bases, width, zero_sems.at[b])
+
+    def each_run(act):
+        act(clear(0))
+        act(clear(bases))
+
+        @pl.loop(1, early.start)
+        def _(b):
+            act(clear(b))
+
+        @pl.when(jnp.logical_not(lower))
+        def _():
+            for b in early:
+                act(clear(b))
+
+    each_run(lambda c: c.start())
     ln = Lanes((rows, lanes), width)
     plane = functools.partial(plane_at, ln, faces)
-    me = lax.axis_index(axis)
-    lower = lax.rem(me, 2) == 1
 
     def send(k, layer):
         start = 4 if layer == 0 else 0
@@ -323,12 +380,7 @@
             if layer == layers - 1:
                 send_one_side(side, out, lower, width, layers, side_sems, k).start()
 
-    first.wait()
-    clear(bases, depth).wait()
-
-    @pl.loop(1, bases)
-    def _(b):
-        clear(b, 2 * depth).wait()
+    each_run(lambda c: c.wait())
 
     @pl.loop(0, blocks)
     def _(k):
@@ -370,20 +422,27 @@
     )
     reach = jnp.transpose(support_reach, (0, 2, 1))
     reach = pltpu.with_memory_space_constraint(reach, pltpu.HBM)
-    tiles = 1 + 9 * rows // TAIL
-    msg_a, msg_b, masks, faces = pl.pallas_call(
+    bases = layers * blocks
+    out_shape = jax.ShapeDtypeStruct((bases * 3 * width, rows, lanes), f32)
+    side = pltpu.VMEM((blocks, 4, rows, lanes), f32)
+    zeros = pltpu.VMEM((2 * (width - 2), rows, lanes), f32)
+    tiles = 1 + 7 * rows // TAIL
+    msg_a, msg_b, masks, faces, cleared = pl.pallas_call(
         functools.partial(pack_kernel, n, width, axis),
         out_shape=(
             pltpu.VMEM((tiles + 1, TAIL, lanes), f32),
             pltpu.VMEM((tiles, TAIL, lanes), f32),
             pltpu.VMEM((layers, TAIL, lanes), f32),
             pltpu.VMEM((4, n, rows, lanes), f32),
+            out_shape,
         ),
         in_specs=[anywhere] * 5,
-        out_specs=(vmem,) * 4,
+        out_specs=(vmem,) * 4 + (anywhere,),
         scratch_shapes=[
             pltpu.VMEM((layers, 4, blocks), jnp.int32),
+            zeros,
             pltpu.SemaphoreType.DMA((5,)),
+            pltpu.SemaphoreType.DMA((EARLY,)),
         ],
         compiler_params=params,
         name="pack",
@@ -391,14 +450,10 @@
     got_a = lax.ppermute(msg_a, axis, swaps(range(0, count - 1, 2)))
     got_b = lax.ppermute(msg_b, axis, swaps(range(1, count - 1, 2)))
 
-    bases = layers * blocks
-    out_shape = jax.ShapeDtypeStruct((bases * 3 * width, rows, lanes), f32)
-    side = pltpu.VMEM((blocks, 4, rows, lanes), f32)
-    zeros = pltpu.VMEM((2 * (width - 2), rows, lanes), f32)
     bulk = pl.pallas_call(
         functools.partial(bulk_kernel, width, blocks, axis, count),
         out_shape=out_shape,
-        in_specs=[vmem] * 3,
+        in_specs=[vmem] * 3 + [anywhere],
         out_specs=anywhere,
         scratch_shapes=[
             zeros,
@@ -408,10 +463,11 @@
             pltpu.SemaphoreType.DMA((blocks,)),
             pltpu.SemaphoreType.DMA((bases + 1,)),
         ],
+        input_output_aliases={3: 0},
         compiler_params=params,
         cost_estimate=pl.CostEstimate(flops=10**7, bytes_accessed=7 * 10**6, transcendentals=0),
         name="bulk",
-    )(faces, masks, got_a)
+    )(faces, masks, got_a, cleared)
     out = pl.pallas_call(
         functools.partial(edge_kernel, width, blocks, axis, count),
         out_shape=out_shape,

time: 9.98 us -> 9.95 us (level)
  starting transfers between devices: 4.62 us -> 4.42 us
  Pallas kernels: 5.14 us -> 5.3 us
    pallas_call x1, Pallas kernels: 1.26 us -> 1.7 us  [on_device(): pl.pallas_call(functools.partial(pack_kernel, n, width, axis), out_shape=...]
    pallas_call x1, Pallas kernels: 2.91 us -> 2.64 us  [on_device(): pl.pallas_call(functools.partial(bulk_kernel, width, blocks, axis, count)...]
    ppermute x1, starting transfers between devices: 4.49 us -> 4.35 us  [on_device(): got_b = lax.ppermute(msg_b, axis, swaps(range(1, count - 1, 2)))]
  transfers between devices with their start and end apart: 2 -> 2, of which waited for: 0 -> 0; matrix products, arithmetic and copies ran while one was open for 0% -> 0% of each run, Pallas kernels for 30% -> 27%
where the time goes in v9:
time: 9.95 us; the launch traced here: 9.77 us
  Pallas kernels  5.3 us (53%)
  starting transfers between devices  4.42 us (44%)
    ppermute x1, starting transfers between devices, on_device(): got_b = lax.ppermute(msg_b, axis, swaps(range(1, count - 1, 2)))  4.35 us
    pallas_call x1, Pallas kernels, on_device(): pl.pallas_call(functools.partial(bulk_kernel, width, blocks, axis, count)...  2.64 us
    pallas_call x1, Pallas kernels, on_device(): pl.pallas_call(functools.partial(pack_kernel, n, width, axis), out_shape=...  1.7 us
    pallas_call x1, Pallas kernels, on_device(): pl.pallas_call(functools.partial(edge_kernel, width, blocks, axis, count)...  0.97 us
  transfers between devices with their start and end apart: 2, of which 0 were waited for; matrix products, arithmetic and copies ran while one was open for 0% of the time, Pallas kernels for 27%

profile of v9, /device:TPU:1, one launch (start us, length us, event | category | flops | bytes accessed | tf_op | source)
XLA Modules:
  0.0 9.8 jit_solution(15968553695391687217)
XLA Ops:
  0.0 1.7 %pack.1 = (f32[16,8,128]{2,1,0:T(8,128)S(1)}, f32[15,8,128]{2,1,0:T(8,128)S(1)}, f32[2,8,128]{2,1,0:T(8,128)S(1)}, f32[4,32,16,128]{3,2,1,0:T(8,128)S(1)}, f32[768,16,128]{2,1,0:T(8,128)}) custom-call(f32[32,16,128]{2,1,0:T(8,128)} %tx.1, f32[32,16,128]{2,1,0:T(8,128)} %ty.1, f32[32,16,128]{2,1,0:T(8,128)} %tz.1, f32[32,16,128]{2,1,0:T(8,128)} %s.1, ...), custom_call_target="tpu_custom_call" | custom-call | tf_op jit(solution)/shard_map/pack/pallas_call | solution.py:430
  1.7 0.1 collective-permute-start.1
  1.8 4.3 %collective-permute-start = (f32[15,8,128]{2,1,0:T(8,128)S(1)}, f32[15,8,128]{2,1,0:T(8,128)S(1)}, u32[]{:S(2)}, u32[]{:S(2)}) collective-permute-start(f32[15,8,128]{2,1,0:T(8,128)S(1)} %get-tuple-element.12), channel_id=1, source_target_pairs={{1,2},{2,1},{3,4},{4,3},{5,6},{6,5},{7,8},{8,7},{9,10},{10,9},{11,... | collective-permute-start | bytes 184328 | tf_op jit(solution)/shard_map/ppermute | solution.py:451
  6.1 0.0 collective-permute-done.1.msg
  6.1 2.6 %bulk.1.held = f32[768,16,128]{2,1,0:T(8,128)} custom-call(f32[4,32,16,128]{3,2,1,0:T(8,128)S(1)} %get-tuple-element.10.faces, f32[2,8,128]{2,1,0:T(8,128)S(1)} %get-tuple-element.11.masks, f32[16,8,128]{2,1,0:T(8,128)S(1)} %collective-permute-done.1.msg, f32[768,16,128]{2,1,0:T(8,128)} %get-tuple-element.14.held), custom_call_target="tpu_custom_call", output_to_operand_aliasing={{}: (3, {})} | custom-call | flops 10000000 | bytes 7000000 | tf_op jit(solution)/shard_map/bulk/pallas_call | solution.py:453
  8.8 0.0 collective-permute-done.msg
  8.8 1.0 %edges.1 = f32[768,16,128]{2,1,0:T(8,128)} custom-call(f32[4,32,16,128]{3,2,1,0:T(8,128)S(1)} %get-tuple-element.10.faces, f32[2,8,128]{2,1,0:T(8,128)S(1)} %get-tuple-element.11.masks, f32[15,8,128]{2,1,0:T(8,128)S(1)} %collective-permute-done.msg, f32[768,16,128]{2,1,0:T(8,128)} %bulk.1.held), custom_call_target="tpu_custom_call", output_to_operand_aliasing={{}: (3, {})} | custom-call | flops 1000000 | bytes 1000000 | tf_op jit(solution)/shard_map/edges/pallas_call | solution.py:471
Async XLA Ops:
  1.7 4.4 %collective-permute-start.1 = (f32[16,8,128]{2,1,0:T(8,128)S(1)}, f32[16,8,128]{2,1,0:T(8,128)S(1)}, u32[]{:S(2)}, u32[]{:S(2)}) collective-permute-start(f32[16,8,128]{2,1,0:T(8,128)S(1)} %get-tuple-element.13), channel_id=1, source_target_pairs={{0,1},{1,0},{2,3},{3,2},{4,5},{5,4},{6,7},{7,6},{8,9},{9,8},{10,11... | collective-permute-start | bytes 196616 | tf_op jit(solution)/shard_map/ppermute | solution.py:450
  1.8 7.0 %collective-permute-start = (f32[15,8,128]{2,1,0:T(8,128)S(1)}, f32[15,8,128]{2,1,0:T(8,128)S(1)}, u32[]{:S(2)}, u32[]{:S(2)}) collective-permute-start(f32[15,8,128]{2,1,0:T(8,128)S(1)} %get-tuple-element.12), channel_id=1, source_target_pairs={{1,2},{2,1},{3,4},{4,3},{5,6},{6,5},{7,8},{8,7},{9,10},{10,9},{11,... | collective-permute-start | bytes 184328 | tf_op jit(solution)/shard_map/ppermute | solution.py:451

commit v10 on v9

--- a/solution.py
+++ b/solution.py
@@ -9,7 +9,7 @@
 
 
 TAIL = 8
-EARLY = 4
+EARLY = 8
 
 
 class Lanes:
@@ -67,10 +67,6 @@
         if valid is not None:
             e = jnp.where(valid, e, 1.0)
         self.half = 0.5 * e + s * (1.0 / 3.0)
-        self.spread(e)
-
-    def spread(self, e):
-        ln = self.ln
         self.all = 1.5 * e
         self.q = reciprocal(self.all)
         self.z1 = self.q * jnp.where(ln.first, self.tz, jnp.where(ln.last, self.tzp, 0.0))
@@ -92,14 +88,6 @@
 
     def along_y(self, v):
         return self.ty * self.ln.ym(v) + self.typ * self.ln.yp(v)
-
-
-class Rim(Plane):
-    def __init__(self, ln, e, tz):
-        self.ln = ln
-        self.tz = jnp.where(ln.lane0, 0.0, tz)
-        self.tzp = ln.zp(self.tz)
-        self.spread(e)
 
 
 def plane_at(ln, faces, p):
@@ -174,13 +162,13 @@
         return msg[pl.ds(1 + tiles * i, tiles)].reshape(rows, lanes)
 
     f1, f2, f3 = (faces[0, jnp.where(low, j, n - j)] for j in (1, 2, 3))
-    f0 = jnp.where(valid, jnp.where(low, faces[0, 0], got(6)), 0.0)
+    f0 = jnp.where(valid, jnp.where(low, faces[0, 0], got(5)), 0.0)
     g1 = got(0)
     a0 = Plane(ln, f0, f1, own(1, 0), own(2, 0), own(3, 0))
     a1 = Plane(ln, f1, f2, own(1, 1), own(2, 1), own(3, 1))
     a2 = Plane(ln, f2, f3, own(1, 2), own(2, 2), own(3, 2))
     b0 = Plane(ln, g1, f0, got(1), got(2), got(3), valid)
-    b1 = Rim(ln, jnp.where(valid, got(4) + g1, 1.0), got(5))
+    b1_total = jnp.where(valid, got(4), 1.0)
     mine = masks[jnp.where(low, 0, layers - 1)]
     mz, my_reach = mine[0:1], jnp.where(low, mine[1:2], mine[2:3])
     theirs = msg[0]
@@ -189,7 +177,7 @@
     b0.edge(False)
     vx = g1 * b0.x1
     kept = vx * my_reach
-    put(0, kept, None, edge_total(b1, mo) - (vx - kept))
+    put(0, kept, None, b1_total - (vx - kept))
     vx, vd = edge_spill(b0, a0, False)
     put(1, vx, vd, edge_total(b0, mo))
     vo, vz = edge_own(a0, 1.0 - a1.z1, a1.z1, b0.x1, True, mz)
@@ -230,19 +218,22 @@
 ):
     layers, _, blocks = held_reach.shape
     lanes = masks.shape[-1]
-    fetch = pltpu.make_async_copy(reach, held_reach, sems.at[4])
+    fetch = pltpu.make_async_copy(reach, held_reach, sems.at[12])
     fetch.start()
-    copies = [
-        pltpu.make_async_copy(a, faces.at[i], sems.at[i]) for i, a in enumerate((tx, ty, tz, s))
-    ]
-    for c in copies:
-        c.start()
+    copies = []
+    for start, size in ((0, 4), (n - 4, 4), (4, n - 8)):
+        for i, a in enumerate((tx, ty, tz, s)):
+            part = pl.ds(start, size)
+            copies.append(pltpu.make_async_copy(a.at[part], faces.at[i, part], sems.at[len(copies)]))
+            copies[-1].start()
     rows = faces.shape[2]
     bases = layers * blocks
     clears = [clear_run(zeros, out, b, bases, width, zero_sems.at[i]) for i, b in enumerate(early_runs(bases))]
     even = lax.rem(lax.axis_index(axis), 2) == 0
 
-    @pl.when(jnp.logical_not(even))
+    eager = lax.axis_index(axis) == 1
+
+    @pl.when(eager)
     def _():
         zeros[...] = jnp.zeros(zeros.shape, jnp.float32)
         for c in clears:
@@ -274,19 +265,20 @@
         msg_b[where] = jnp.where(even, down, up)
 
     put(0, masks[layers - 1], masks[0])
-    for c in copies:
+    for c in copies[:8]:
         c.wait()
     ln = Lanes(faces.shape[2:], width)
-    top, _ = cross(ln, faces[1, n - 2], faces[2, n - 2], faces[3, n - 2])
-    low, _ = cross(ln, faces[1, 1], faces[2, 1], faces[3, 1])
-    ups = [faces[0, n - 1]] + [faces[i, n - 1] for i in (1, 2, 3)]
-    ups += [top + faces[0, n - 2], faces[2, n - 2], faces[0, n - 1]]
-    downs = [faces[0, 1]] + [faces[i, 0] for i in (1, 2, 3)]
-    downs += [low + faces[0, 2], faces[2, 1], faces[0, 0]]
+    top = edge_total(plane_at(ln, faces, n - 2), masks[layers - 1, 0:1])
+    low = edge_total(plane_at(ln, faces, 1), masks[0, 0:1])
+    ups = [faces[i, n - 1] for i in range(4)] + [top, faces[0, n - 1]]
+    downs = [faces[0, 1]] + [faces[i, 0] for i in (1, 2, 3)] + [low, faces[0, 0]]
     for i, (up, down) in enumerate(zip(ups, downs)):
         put(1 + i * (rows // TAIL), up, down)
 
-    @pl.when(jnp.logical_not(even))
+    for c in copies[8:]:
+        c.wait()
+
+    @pl.when(eager)
     def _():
         for c in clears:
             c.wait()
@@ -317,7 +309,7 @@
         def _(b):
             act(clear(b))
 
-        @pl.when(jnp.logical_not(lower))
+        @pl.when(me != 1)
         def _():
             for b in early:
                 act(clear(b))
@@ -426,7 +418,7 @@
     out_shape = jax.ShapeDtypeStruct((bases * 3 * width, rows, lanes), f32)
     side = pltpu.VMEM((blocks, 4, rows, lanes), f32)
     zeros = pltpu.VMEM((2 * (width - 2), rows, lanes), f32)
-    tiles = 1 + 7 * rows // TAIL
+    tiles = 1 + 6 * rows // TAIL
     msg_a, msg_b, masks, faces, cleared = pl.pallas_call(
         functools.partial(pack_kernel, n, width, axis),
         out_shape=(
@@ -441,7 +433,7 @@
         scratch_shapes=[
             pltpu.VMEM((layers, 4, blocks), jnp.int32),
             zeros,
-            pltpu.SemaphoreType.DMA((5,)),
+            pltpu.SemaphoreType.DMA((13,)),
             pltpu.SemaphoreType.DMA((EARLY,)),
         ],
         compiler_params=params,

time: 9.95 us -> 9.76 us (0.981)
  the two profiles are of different devices: /device:TPU:1 before, /device:TPU:5 now
where the time goes in v10:
time: 9.76 us; the launch traced here: 9.58 us
  Pallas kernels  5.4 us (55%)
  starting transfers between devices  3.79 us (39%)
  waiting for transfers between devices  0.36 us (4%)
    ppermute x1, starting transfers between devices, on_device(): got_b = lax.ppermute(msg_b, axis, swaps(range(1, count - 1, 2)))  3.05 us
    pallas_call x1, Pallas kernels, on_device(): pl.pallas_call(functools.partial(bulk_kernel, width, blocks, axis, count)...  2.91 us
    pallas_call x1, Pallas kernels, on_device(): pl.pallas_call(functools.partial(pack_kernel, n, width, axis), out_shape=...  1.53 us
    pallas_call x1, Pallas kernels, on_device(): pl.pallas_call(functools.partial(edge_kernel, width, blocks, axis, count)...  0.96 us
    ppermute x1, starting transfers between devices, on_device(): got_a = lax.ppermute(msg_a, axis, swaps(range(0, count - 1, 2)))  0.74 us
    ppermute x1, waiting for transfers between devices, on_device(): got_b = lax.ppermute(msg_b, axis, swaps(range(1, count - 1, 2)))  0.36 us
  transfers between devices with their start and end apart: 2, of which 1 were waited for; matrix products, arithmetic and copies ran while one was open for 0% of the time, Pallas kernels for 30%

profile of v10, /device:TPU:5, one launch (start us, length us, event | category | flops | bytes accessed | tf_op | source)
XLA Modules:
  0.0 9.6 jit_solution(11190167570995458573)
XLA Ops:
  0.0 1.5 %pack.1 = (f32[14,8,128]{2,1,0:T(8,128)S(1)}, f32[13,8,128]{2,1,0:T(8,128)S(1)}, f32[2,8,128]{2,1,0:T(8,128)S(1)}, f32[4,32,16,128]{3,2,1,0:T(8,128)S(1)}, f32[768,16,128]{2,1,0:T(8,128)}) custom-call(f32[32,16,128]{2,1,0:T(8,128)} %tx.1, f32[32,16,128]{2,1,0:T(8,128)} %ty.1, f32[32,16,128]{2,1,0:T(8,128)} %tz.1, f32[32,16,128]{2,1,0:T(8,128)} %s.1, ...), custom_call_target="tpu_custom_call" | custom-call | tf_op jit(solution)/shard_map/pack/pallas_call | solution.py:422
  1.5 0.7 %collective-permute-start.1 = (f32[14,8,128]{2,1,0:T(8,128)S(1)}, f32[14,8,128]{2,1,0:T(8,128)S(1)}, u32[]{:S(2)}, u32[]{:S(2)}) collective-permute-start(f32[14,8,128]{2,1,0:T(8,128)S(1)} %get-tuple-element.13), channel_id=1, source_target_pairs={{0,1},{1,0},{2,3},{3,2},{4,5},{5,4},{6,7},{7,6},{8,9},{9,8},{10,11... | collective-permute-start | bytes 172040 | tf_op jit(solution)/shard_map/ppermute | solution.py:442
  2.3 3.0 %collective-permute-start = (f32[13,8,128]{2,1,0:T(8,128)S(1)}, f32[13,8,128]{2,1,0:T(8,128)S(1)}, u32[]{:S(2)}, u32[]{:S(2)}) collective-permute-start(f32[13,8,128]{2,1,0:T(8,128)S(1)} %get-tuple-element.12), channel_id=1, source_target_pairs={{1,2},{2,1},{3,4},{4,3},{5,6},{6,5},{7,8},{8,7},{9,10},{10,9},{11,... | collective-permute-start | bytes 159752 | tf_op jit(solution)/shard_map/ppermute | solution.py:443
  5.3 0.0 collective-permute-done.1.msg
  5.3 2.9 %bulk.1.held = f32[768,16,128]{2,1,0:T(8,128)} custom-call(f32[4,32,16,128]{3,2,1,0:T(8,128)S(1)} %get-tuple-element.10.faces, f32[2,8,128]{2,1,0:T(8,128)S(1)} %get-tuple-element.11.masks, f32[14,8,128]{2,1,0:T(8,128)S(1)} %collective-permute-done.1.msg, f32[768,16,128]{2,1,0:T(8,128)} %get-tuple-element.14.held), custom_call_target="tpu_custom_call", output_to_operand_aliasing={{}: (3, {})} | custom-call | flops 10000000 | bytes 7000000 | tf_op jit(solution)/shard_map/bulk/pallas_call | solution.py:445
  8.3 0.4 %collective-permute-done.msg = f32[13,8,128]{2,1,0:T(8,128)S(1)} collective-permute-done((f32[13,8,128]{2,1,0:T(8,128)S(1)}, f32[13,8,128]{2,1,0:T(8,128)S(1)}, u32[]{:S(2)}, u32[]{:S(2)}) %collective-permute-start) | collective-permute-done | bytes 53280 | tf_op jit(solution)/shard_map/ppermute | solution.py:443
  8.6 1.0 %edges.1 = f32[768,16,128]{2,1,0:T(8,128)} custom-call(f32[4,32,16,128]{3,2,1,0:T(8,128)S(1)} %get-tuple-element.10.faces, f32[2,8,128]{2,1,0:T(8,128)S(1)} %get-tuple-element.11.masks, f32[13,8,128]{2,1,0:T(8,128)S(1)} %collective-permute-done.msg, f32[768,16,128]{2,1,0:T(8,128)} %bulk.1.held), custom_call_target="tpu_custom_call", output_to_operand_aliasing={{}: (3, {})} | custom-call | flops 1000000 | bytes 1000000 | tf_op jit(solution)/shard_map/edges/pallas_call | solution.py:463
Async XLA Ops:
  1.5 3.8 %collective-permute-start.1 = (f32[14,8,128]{2,1,0:T(8,128)S(1)}, f32[14,8,128]{2,1,0:T(8,128)S(1)}, u32[]{:S(2)}, u32[]{:S(2)}) collective-permute-start(f32[14,8,128]{2,1,0:T(8,128)S(1)} %get-tuple-element.13), channel_id=1, source_target_pairs={{0,1},{1,0},{2,3},{3,2},{4,5},{5,4},{6,7},{7,6},{8,9},{9,8},{10,11... | collective-permute-start | bytes 172040 | tf_op jit(solution)/shard_map/ppermute | solution.py:442
  2.3 6.3 %collective-permute-start = (f32[13,8,128]{2,1,0:T(8,128)S(1)}, f32[13,8,128]{2,1,0:T(8,128)S(1)}, u32[]{:S(2)}, u32[]{:S(2)}) collective-permute-start(f32[13,8,128]{2,1,0:T(8,128)S(1)} %get-tuple-element.12), channel_id=1, source_target_pairs={{1,2},{2,1},{3,4},{4,3},{5,6},{6,5},{7,8},{8,7},{9,10},{10,9},{11,... | collective-permute-start | bytes 159752 | tf_op jit(solution)/shard_map/ppermute | solution.py:443

commit v11 on v9

--- a/solution.py
+++ b/solution.py
@@ -9,7 +9,7 @@
 
 
 TAIL = 8
-EARLY = 4
+EARLY = 8
 
 
 class Lanes:
@@ -51,10 +51,19 @@
     return r * (2.0 - x * r)
 
 
+def within_y(ln, ty):
+    ty = jnp.where(ln.row0, 0.0, ty)
+    return ty, ln.yp(ty)
+
+
+def within_z(ln, tz):
+    tz = jnp.where(ln.lane0, 0.0, tz)
+    return tz, ln.zp(tz)
+
+
 def cross(ln, ty, tz, s):
-    ty = jnp.where(ln.row0, 0.0, ty)
-    tz = jnp.where(ln.lane0, 0.0, tz)
-    typ, tzp = ln.yp(ty), ln.zp(tz)
+    ty, typ = within_y(ln, ty)
+    tz, tzp = within_z(ln, tz)
     return s * (1.0 / 3.0) + ((ty + typ) + (tz + tzp)), (ty, typ, tz, tzp)
 
 
@@ -235,14 +244,16 @@
     copies = [
         pltpu.make_async_copy(a, faces.at[i], sems.at[i]) for i, a in enumerate((tx, ty, tz, s))
     ]
-    for c in copies:
-        c.start()
+    for i in (1, 2, 0, 3):
+        copies[i].start()
     rows = faces.shape[2]
     bases = layers * blocks
     clears = [clear_run(zeros, out, b, bases, width, zero_sems.at[i]) for i, b in enumerate(early_runs(bases))]
     even = lax.rem(lax.axis_index(axis), 2) == 0
 
-    @pl.when(jnp.logical_not(even))
+    eager = lax.axis_index(axis) == 1
+
+    @pl.when(eager)
     def _():
         zeros[...] = jnp.zeros(zeros.shape, jnp.float32)
         for c in clears:
@@ -274,19 +285,28 @@
         msg_b[where] = jnp.where(even, down, up)
 
     put(0, masks[layers - 1], masks[0])
-    for c in copies:
-        c.wait()
     ln = Lanes(faces.shape[2:], width)
-    top, _ = cross(ln, faces[1, n - 2], faces[2, n - 2], faces[3, n - 2])
-    low, _ = cross(ln, faces[1, 1], faces[2, 1], faces[3, 1])
-    ups = [faces[0, n - 1]] + [faces[i, n - 1] for i in (1, 2, 3)]
-    ups += [top + faces[0, n - 2], faces[2, n - 2], faces[0, n - 1]]
-    downs = [faces[0, 1]] + [faces[i, 0] for i in (1, 2, 3)]
-    downs += [low + faces[0, 2], faces[2, 1], faces[0, 0]]
-    for i, (up, down) in enumerate(zip(ups, downs)):
-        put(1 + i * (rows // TAIL), up, down)
-
-    @pl.when(jnp.logical_not(even))
+    behind = {}
+
+    def plane(slot, up, down):
+        put(1 + slot * (rows // TAIL), up, down)
+
+    for i, across in ((1, lambda v: within_y(ln, v)), (2, lambda v: within_z(ln, v))):
+        copies[i].wait()
+        plane(i, faces[i, n - 1], faces[i, 0])
+        for p in (n - 2, 1):
+            v, v_next = across(faces[i, p])
+            behind[p] = behind.get(p, 0.0) + (v + v_next)
+    plane(5, faces[2, n - 2], faces[2, 1])
+    copies[0].wait()
+    plane(0, faces[0, n - 1], faces[0, 1])
+    plane(6, faces[0, n - 1], faces[0, 0])
+    behind = {p: behind[p] + faces[0, q] for p, q in ((n - 2, n - 2), (1, 2))}
+    copies[3].wait()
+    plane(3, faces[3, n - 1], faces[3, 0])
+    plane(4, *(behind[p] + faces[3, p] * (1.0 / 3.0) for p in (n - 2, 1)))
+
+    @pl.when(eager)
     def _():
         for c in clears:
             c.wait()
@@ -317,7 +337,7 @@
         def _(b):
             act(clear(b))
 
-        @pl.when(jnp.logical_not(lower))
+        @pl.when(me != 1)
         def _():
             for b in early:
                 act(clear(b))

time: 9.95 us -> 9.64 us (0.969)
  the two profiles are of different devices: /device:TPU:1 before, /device:TPU:5 now
where the time goes in v11:
time: 9.64 us; the launch traced here: 9.46 us
  Pallas kernels  5.19 us (54%)
  starting transfers between devices  3.79 us (39%)
  waiting for transfers between devices  0.45 us (5%)
    ppermute x1, starting transfers between devices, on_device(): got_b = lax.ppermute(msg_b, axis, swaps(range(1, count - 1, 2)))  3.05 us
    pallas_call x1, Pallas kernels, on_device(): pl.pallas_call(functools.partial(bulk_kernel, width, blocks, axis, count)...  2.91 us
    pallas_call x1, Pallas kernels, on_device(): pl.pallas_call(functools.partial(pack_kernel, n, width, axis), out_shape=...  1.32 us
    pallas_call x1, Pallas kernels, on_device(): pl.pallas_call(functools.partial(edge_kernel, width, blocks, axis, count)...  0.96 us
    ppermute x1, starting transfers between devices, on_device(): got_a = lax.ppermute(msg_a, axis, swaps(range(0, count - 1, 2)))  0.74 us
    ppermute x1, waiting for transfers between devices, on_device(): got_b = lax.ppermute(msg_b, axis, swaps(range(1, count - 1, 2)))  0.44 us
  transfers between devices with their start and end apart: 2, of which 1 were waited for; matrix products, arithmetic and copies ran while one was open for 0% of the time, Pallas kernels for 31%

profile of v11, /device:TPU:5, one launch (start us, length us, event | category | flops | bytes accessed | tf_op | source)
XLA Modules:
  0.0 9.5 jit_solution(12090580667905498229)
XLA Ops:
  0.0 1.3 %pack.1 = (f32[16,8,128]{2,1,0:T(8,128)S(1)}, f32[15,8,128]{2,1,0:T(8,128)S(1)}, f32[2,8,128]{2,1,0:T(8,128)S(1)}, f32[4,32,16,128]{3,2,1,0:T(8,128)S(1)}, f32[768,16,128]{2,1,0:T(8,128)}) custom-call(f32[32,16,128]{2,1,0:T(8,128)} %tx.1, f32[32,16,128]{2,1,0:T(8,128)} %ty.1, f32[32,16,128]{2,1,0:T(8,128)} %tz.1, f32[32,16,128]{2,1,0:T(8,128)} %s.1, ...), custom_call_target="tpu_custom_call" | custom-call | tf_op jit(solution)/shard_map/pack/pallas_call | solution.py:450
  1.3 0.7 %collective-permute-start.1 = (f32[16,8,128]{2,1,0:T(8,128)S(1)}, f32[16,8,128]{2,1,0:T(8,128)S(1)}, u32[]{:S(2)}, u32[]{:S(2)}) collective-permute-start(f32[16,8,128]{2,1,0:T(8,128)S(1)} %get-tuple-element.13), channel_id=1, source_target_pairs={{0,1},{1,0},{2,3},{3,2},{4,5},{5,4},{6,7},{7,6},{8,9},{9,8},{10,11... | collective-permute-start | bytes 196616 | tf_op jit(solution)/shard_map/ppermute | solution.py:470
  2.1 3.0 %collective-permute-start = (f32[15,8,128]{2,1,0:T(8,128)S(1)}, f32[15,8,128]{2,1,0:T(8,128)S(1)}, u32[]{:S(2)}, u32[]{:S(2)}) collective-permute-start(f32[15,8,128]{2,1,0:T(8,128)S(1)} %get-tuple-element.12), channel_id=1, source_target_pairs={{1,2},{2,1},{3,4},{4,3},{5,6},{6,5},{7,8},{8,7},{9,10},{10,9},{11,... | collective-permute-start | bytes 184328 | tf_op jit(solution)/shard_map/ppermute | solution.py:471
  5.1 0.0 collective-permute-done.1.msg
  5.1 2.9 %bulk.1.held = f32[768,16,128]{2,1,0:T(8,128)} custom-call(f32[4,32,16,128]{3,2,1,0:T(8,128)S(1)} %get-tuple-element.10.faces, f32[2,8,128]{2,1,0:T(8,128)S(1)} %get-tuple-element.11.masks, f32[16,8,128]{2,1,0:T(8,128)S(1)} %collective-permute-done.1.msg, f32[768,16,128]{2,1,0:T(8,128)} %get-tuple-element.14.held), custom_call_target="tpu_custom_call", output_to_operand_aliasing={{}: (3, {})} | custom-call | flops 10000000 | bytes 7000000 | tf_op jit(solution)/shard_map/bulk/pallas_call | solution.py:473
  8.1 0.4 %collective-permute-done.msg = f32[15,8,128]{2,1,0:T(8,128)S(1)} collective-permute-done((f32[15,8,128]{2,1,0:T(8,128)S(1)}, f32[15,8,128]{2,1,0:T(8,128)S(1)}, u32[]{:S(2)}, u32[]{:S(2)}) %collective-permute-start) | collective-permute-done | bytes 61472 | tf_op jit(solution)/shard_map/ppermute | solution.py:471
  8.5 1.0 %edges.1 = f32[768,16,128]{2,1,0:T(8,128)} custom-call(f32[4,32,16,128]{3,2,1,0:T(8,128)S(1)} %get-tuple-element.10.faces, f32[2,8,128]{2,1,0:T(8,128)S(1)} %get-tuple-element.11.masks, f32[15,8,128]{2,1,0:T(8,128)S(1)} %collective-permute-done.msg, f32[768,16,128]{2,1,0:T(8,128)} %bulk.1.held), custom_call_target="tpu_custom_call", output_to_operand_aliasing={{}: (3, {})} | custom-call | flops 1000000 | bytes 1000000 | tf_op jit(solution)/shard_map/edges/pallas_call | solution.py:491
Async XLA Ops:
  1.3 3.8 %collective-permute-start.1 = (f32[16,8,128]{2,1,0:T(8,128)S(1)}, f32[16,8,128]{2,1,0:T(8,128)S(1)}, u32[]{:S(2)}, u32[]{:S(2)}) collective-permute-start(f32[16,8,128]{2,1,0:T(8,128)S(1)} %get-tuple-element.13), channel_id=1, source_target_pairs={{0,1},{1,0},{2,3},{3,2},{4,5},{5,4},{6,7},{7,6},{8,9},{9,8},{10,11... | collective-permute-start | bytes 196616 | tf_op jit(solution)/shard_map/ppermute | solution.py:470
  2.1 6.4 %collective-permute-start = (f32[15,8,128]{2,1,0:T(8,128)S(1)}, f32[15,8,128]{2,1,0:T(8,128)S(1)}, u32[]{:S(2)}, u32[]{:S(2)}) collective-permute-start(f32[15,8,128]{2,1,0:T(8,128)S(1)} %get-tuple-element.12), channel_id=1, source_target_pairs={{1,2},{2,1},{3,4},{4,3},{5,6},{6,5},{7,8},{8,7},{9,10},{10,9},{11,... | collective-permute-start | bytes 184328 | tf_op jit(solution)/shard_map/ppermute | solution.py:471

commit v12 on v8

--- a/solution.py
+++ b/solution.py
@@ -9,6 +9,7 @@
 
 
 TAIL = 8
+EARLY = 12
 
 
 class Lanes:
@@ -196,18 +197,43 @@
     return pltpu.make_async_copy(buf.at[k], there, sems.at[k])
 
 
+def clear_run(zeros, out, b, bases, width, sem):
+    depth = width - 2
+    ends = isinstance(b, int) and b in (0, bases)
+    count = depth if ends else 2 * depth
+    start = 0 if ends and b == 0 else b * 3 * width - depth
+    return pltpu.make_async_copy(zeros.at[pl.ds(0, count)], out.at[pl.ds(start, count)], sem)
+
+
+def clear_runs(act, zeros, out, first, last, bases, width, sems):
+    def body(b, _):
+        act(clear_run(zeros, out, b, bases, width, sems.at[b]))
+
+    lax.fori_loop(first, last, body, None)
+
+
 def pack_kernel(
-    n, width, axis, tx, ty, tz, s, reach, msg_a, msg_b, masks, faces, held_reach, sems
+    n, width, axis, tx, ty, tz, s, reach, msg_a, msg_b, masks, faces, out,
+    held_reach, zeros, buf, read_sems, sems, zero_sems,
 ):
     layers, _, blocks = held_reach.shape
     lanes = masks.shape[-1]
-    fetch = pltpu.make_async_copy(reach, held_reach, sems.at[4])
+    fetch = pltpu.make_async_copy(reach, held_reach, read_sems.at[4])
     fetch.start()
     copies = [
-        pltpu.make_async_copy(a, faces.at[i], sems.at[i]) for i, a in enumerate((tx, ty, tz, s))
+        pltpu.make_async_copy(a, faces.at[i], read_sems.at[i]) for i, a in enumerate((tx, ty, tz, s))
     ]
     for c in copies:
         c.start()
+    bases = layers * blocks
+    me = lax.axis_index(axis)
+    late = bases - EARLY
+
+    @pl.when(me == 1)
+    def _():
+        zeros[...] = jnp.zeros(zeros.shape, jnp.float32)
+        clear_runs(lambda c: c.start(), zeros, out, late, bases, bases, width, zero_sems)
+
     masks[...] = jnp.zeros(masks.shape, jnp.float32)
     lane = lax.broadcasted_iota(jnp.int32, (4, lanes), 1)
     block = lane // width
@@ -226,7 +252,7 @@
         )
         masks[layer, 0:1] = near
         masks[layer, 1:3] = jnp.where(r[0:2] >= 2, 1.0, 0.0)
-    even = lax.rem(lax.axis_index(axis), 2) == 0
+    even = lax.rem(me, 2) == 0
 
     def put(tile, up, down):
         up, down = (v.reshape(-1, TAIL, lanes) for v in (up, down))
@@ -242,32 +268,30 @@
         put(3 + 4 * i, faces[i, n - 2], faces[i, 1])
     put(17, faces[0, n - 1], faces[0, 2])
 
-
-def bulk_kernel(
-    width, blocks, axis, count, faces, masks, msg, out, zeros, buf, side, sems, side_sems, zero_sems
-):
-    layers = masks.shape[0]
+    @pl.when(me == 1)
+    def _():
+        clear_runs(lambda c: c.wait(), zeros, out, late, bases, bases, width, zero_sems)
+
+    @pl.when(me == 0)
+    def _():
+        inner_planes(width, bases, faces, masks, out, zeros, buf, sems, zero_sems)
+
+
+def inner_planes(width, last_run, faces, masks, out, zeros, buf, sems, zero_sems):
+    layers, blocks = buf.shape[:2]
     rows, lanes = faces.shape[2:]
     box, depth = 3 * width, width - 2
     bases = layers * blocks
     zeros[...] = jnp.zeros(zeros.shape, jnp.float32)
 
-    def clear(b, count):
-        there = out.at[pl.ds(b * box - depth, count)]
-        return pltpu.make_async_copy(zeros.at[pl.ds(0, count)], there, zero_sems.at[b])
-
-    first = pltpu.make_async_copy(zeros.at[pl.ds(0, depth)], out.at[pl.ds(0, depth)], zero_sems.at[0])
-    first.start()
-    clear(bases, depth).start()
-
-    @pl.loop(1, bases)
-    def _(b):
-        clear(b, 2 * depth).start()
-
+    def each_run(act):
+        for b in (0, bases):
+            act(clear_run(zeros, out, b, bases, width, zero_sems.at[b]))
+        clear_runs(act, zeros, out, 1, last_run, bases, width, zero_sems)
+
+    each_run(lambda c: c.start())
     ln = Lanes((rows, lanes), width)
     plane = functools.partial(plane_at, ln, faces)
-    me = lax.axis_index(axis)
-    lower = lax.rem(me, 2) == 1
 
     def send(k, layer):
         start = 4 if layer == 0 else 0
@@ -313,39 +337,43 @@
             store(ln, buf.at[layer], j + 2, blocks, vo, vz, total)
         if layer < layers - 1:
             between(layer + 1)
-        else:
-            valid = lower | (me < count - 1)
-            work_side(ln, lower, valid, faces, masks, msg, store_side(ln, side, lower, blocks))
 
         @pl.loop(0, blocks)
         def _(k):
             send(k, layer).start()
-            if layer == layers - 1:
-                send_one_side(side, out, lower, width, layers, side_sems, k).start()
-
-    first.wait()
-    clear(bases, depth).wait()
-
-    @pl.loop(1, bases)
-    def _(b):
-        clear(b, 2 * depth).wait()
+
+    each_run(lambda c: c.wait())
 
     @pl.loop(0, blocks)
     def _(k):
         for layer in range(layers):
             send(k, layer).wait()
-        send_one_side(side, out, lower, width, layers, side_sems, k).wait()
-
-
-def edge_kernel(width, blocks, axis, count, faces, masks, msg, held, out, side, sems):
+
+
+def bulk_kernel(width, axis, faces, masks, held, out, zeros, buf, sems, zero_sems):
+    del held
+    me = lax.axis_index(axis)
+    bases = sems.shape[0]
+
+    @pl.when(me != 0)
+    def _():
+        last_run = jnp.where(me == 1, bases - EARLY, bases)
+        inner_planes(width, last_run, faces, masks, out, zeros, buf, sems, zero_sems)
+
+
+def edge_kernel(
+    width, blocks, axis, count, faces, masks, got_a, got_b, held, out, side_a, side_b, sems_a, sems_b
+):
     del held
     layers = masks.shape[0]
     me = lax.axis_index(axis)
-    lower = lax.rem(me, 2) == 0
-    valid = jnp.where(lower, me > 0, me < count - 1)
+    odd = lax.rem(me, 2) == 1
     ln = Lanes(faces.shape[2:], width)
-    work_side(ln, lower, valid, faces, masks, msg, store_side(ln, side, lower, blocks))
-    copies = [send_one_side(side, out, lower, width, layers, sems, k) for k in range(blocks)]
+    copies = []
+    for low, msg, side, sems in ((odd, got_a, side_a, sems_a), (jnp.logical_not(odd), got_b, side_b, sems_b)):
+        valid = jnp.where(low, me > 0, me < count - 1)
+        work_side(ln, low, valid, faces, masks, msg, store_side(ln, side, low, blocks))
+        copies += [send_one_side(side, out, low, width, layers, sems, k) for k in range(blocks)]
     for c in copies:
         c.start()
     for c in copies:
@@ -370,20 +398,30 @@
     )
     reach = jnp.transpose(support_reach, (0, 2, 1))
     reach = pltpu.with_memory_space_constraint(reach, pltpu.HBM)
+    bases = layers * blocks
+    out_shape = jax.ShapeDtypeStruct((bases * 3 * width, rows, lanes), f32)
+    inner = [
+        pltpu.VMEM((2 * (width - 2), rows, lanes), f32),
+        pltpu.VMEM((layers, blocks, width + 4, rows, lanes), f32),
+    ]
+    inner_sems = [pltpu.SemaphoreType.DMA((bases,)), pltpu.SemaphoreType.DMA((bases + 1,))]
     tiles = 1 + 9 * rows // TAIL
-    msg_a, msg_b, masks, faces = pl.pallas_call(
+    msg_a, msg_b, masks, faces, started = pl.pallas_call(
         functools.partial(pack_kernel, n, width, axis),
         out_shape=(
+            pltpu.VMEM((tiles, TAIL, lanes), f32),
             pltpu.VMEM((tiles + 1, TAIL, lanes), f32),
-            pltpu.VMEM((tiles, TAIL, lanes), f32),
             pltpu.VMEM((layers, TAIL, lanes), f32),
             pltpu.VMEM((4, n, rows, lanes), f32),
+            out_shape,
         ),
         in_specs=[anywhere] * 5,
-        out_specs=(vmem,) * 4,
+        out_specs=(vmem,) * 4 + (anywhere,),
         scratch_shapes=[
             pltpu.VMEM((layers, 4, blocks), jnp.int32),
+            *inner,
             pltpu.SemaphoreType.DMA((5,)),
+            *inner_sems,
         ],
         compiler_params=params,
         name="pack",
@@ -391,41 +429,29 @@
     got_a = lax.ppermute(msg_a, axis, swaps(range(0, count - 1, 2)))
     got_b = lax.ppermute(msg_b, axis, swaps(range(1, count - 1, 2)))
 
-    bases = layers * blocks
-    out_shape = jax.ShapeDtypeStruct((bases * 3 * width, rows, lanes), f32)
-    side = pltpu.VMEM((blocks, 4, rows, lanes), f32)
-    zeros = pltpu.VMEM((2 * (width - 2), rows, lanes), f32)
     bulk = pl.pallas_call(
-        functools.partial(bulk_kernel, width, blocks, axis, count),
+        functools.partial(bulk_kernel, width, axis),
         out_shape=out_shape,
-        in_specs=[vmem] * 3,
+        in_specs=[vmem] * 2 + [anywhere],
         out_specs=anywhere,
-        scratch_shapes=[
-            zeros,
-            pltpu.VMEM((layers, blocks, width + 4, rows, lanes), f32),
-            side,
-            pltpu.SemaphoreType.DMA((bases,)),
-            pltpu.SemaphoreType.DMA((blocks,)),
-            pltpu.SemaphoreType.DMA((bases + 1,)),
-        ],
+        scratch_shapes=inner + inner_sems,
+        input_output_aliases={2: 0},
         compiler_params=params,
         cost_estimate=pl.CostEstimate(flops=10**7, bytes_accessed=7 * 10**6, transcendentals=0),
         name="bulk",
-    )(faces, masks, got_a)
+    )(faces, masks, started)
+    side = [pltpu.VMEM((blocks, 4, rows, lanes), f32)] * 2
     out = pl.pallas_call(
         functools.partial(edge_kernel, width, blocks, axis, count),
         out_shape=out_shape,
-        in_specs=[vmem] * 3 + [anywhere],
+        in_specs=[vmem] * 4 + [anywhere],
         out_specs=anywhere,
-        scratch_shapes=[
-            side,
-            pltpu.SemaphoreType.DMA((blocks,)),
-        ],
-        input_output_aliases={3: 0},
+        scratch_shapes=side + [pltpu.SemaphoreType.DMA((blocks,))] * 2,
+        input_output_aliases={4: 0},
         compiler_params=params,
         cost_estimate=pl.CostEstimate(flops=10**6, bytes_accessed=10**6, transcendentals=0),
         name="edges",
-    )(faces, masks, got_b, bulk)
+    )(faces, masks, got_a, got_b, bulk)
     return out.reshape(layers, blocks, 3 * width, rows, lanes)
 
 

time: 9.98 us -> 9.62 us (0.964)
  starting transfers between devices: 4.62 us -> 3.8 us
  Pallas kernels: 5.14 us -> 5.58 us
    pallas_call x1, Pallas kernels: 1.26 us -> 2.36 us  [on_device(): pl.pallas_call(functools.partial(pack_kernel, n, width, axis), out_shape=...]
    pallas_call x1, Pallas kernels: 2.91 us -> 2.05 us  [on_device(): pl.pallas_call(functools.partial(bulk_kernel, width, axis), out_shape=out...]
    ppermute x1, starting transfers between devices: 4.49 us -> 3.73 us  [on_device(): got_b = lax.ppermute(msg_b, axis, swaps(range(1, count - 1, 2)))]
    pallas_call x1, Pallas kernels: 0.97 us -> 1.17 us  [on_device(): pl.pallas_call(functools.partial(edge_kernel, width, blocks, axis, count)...]
  transfers between devices with their start and end apart: 2 -> 2, of which waited for: 0 -> 0; matrix products, arithmetic and copies ran while one was open for 0% -> 0% of each run, Pallas kernels for 30% -> 22%
where the time goes in v12:
time: 9.62 us; the launch traced here: 9.43 us
  Pallas kernels  5.58 us (58%)
  starting transfers between devices  3.8 us (40%)
    ppermute x1, starting transfers between devices, on_device(): got_b = lax.ppermute(msg_b, axis, swaps(range(1, count - 1, 2)))  3.73 us
    pallas_call x1, Pallas kernels, on_device(): pl.pallas_call(functools.partial(pack_kernel, n, width, axis), out_shape=...  2.36 us
    pallas_call x1, Pallas kernels, on_device(): pl.pallas_call(functools.partial(bulk_kernel, width, axis), out_shape=out...  2.05 us
    pallas_call x1, Pallas kernels, on_device(): pl.pallas_call(functools.partial(edge_kernel, width, blocks, axis, count)...  1.17 us
  transfers between devices with their start and end apart: 2, of which 0 were waited for; matrix products, arithmetic and copies ran while one was open for 0% of the time, Pallas kernels for 22%

profile of v12, /device:TPU:1, one launch (start us, length us, event | category | flops | bytes accessed | tf_op | source)
XLA Modules:
  0.0 9.4 jit_solution(5049675649861913833)
XLA Ops:
  0.0 2.4 %pack.1 = (f32[19,8,128]{2,1,0:T(8,128)S(1)}, f32[20,8,128]{2,1,0:T(8,128)S(1)}, f32[2,8,128]{2,1,0:T(8,128)S(1)}, f32[4,32,16,128]{3,2,1,0:T(8,128)S(1)}, f32[768,16,128]{2,1,0:T(8,128)}) custom-call(f32[32,16,128]{2,1,0:T(8,128)} %tx.1, f32[32,16,128]{2,1,0:T(8,128)} %ty.1, f32[32,16,128]{2,1,0:T(8,128)} %tz.1, f32[32,16,128]{2,1,0:T(8,128)} %s.1, ...), custom_call_target="tpu_custom_call" | custom-call | tf_op jit(solution)/shard_map/pack/pallas_call | solution.py:409
  2.4 3.7 %collective-permute-start.1 = (f32[20,8,128]{2,1,0:T(8,128)S(1)}, f32[20,8,128]{2,1,0:T(8,128)S(1)}, u32[]{:S(2)}, u32[]{:S(2)}) collective-permute-start(f32[20,8,128]{2,1,0:T(8,128)S(1)} %get-tuple-element.13), channel_id=1, source_target_pairs={{1,2},{2,1},{3,4},{4,3},{5,6},{6,5},{7,8},{8,7},{9,10},{10,9},{11,... | collective-permute-start | bytes 245768 | tf_op jit(solution)/shard_map/ppermute | solution.py:430
  6.1 0.1 collective-permute-start
  6.2 2.0 %bulk.1.held = f32[768,16,128]{2,1,0:T(8,128)} custom-call(f32[4,32,16,128]{3,2,1,0:T(8,128)S(1)} %get-tuple-element.10.faces, f32[2,8,128]{2,1,0:T(8,128)S(1)} %get-tuple-element.11.masks, f32[768,16,128]{2,1,0:T(8,128)} %get-tuple-element.14.held), custom_call_target="tpu_custom_call", output_to_operand_aliasing={{}: (2, {})} | custom-call | flops 10000000 | bytes 7000000 | tf_op jit(solution)/shard_map/bulk/pallas_call | solution.py:432
  8.2 0.0 collective-permute-done.got_a
  8.3 0.0 collective-permute-done.1.got_b
  8.3 1.2 %edges.1 = f32[768,16,128]{2,1,0:T(8,128)} custom-call(f32[4,32,16,128]{3,2,1,0:T(8,128)S(1)} %get-tuple-element.10.faces, f32[2,8,128]{2,1,0:T(8,128)S(1)} %get-tuple-element.11.masks, f32[19,8,128]{2,1,0:T(8,128)S(1)} %collective-permute-done.got_a, f32[20,8,128]{2,1,0:T(8,128)S(1)} %collective-permute-done.1.got_b, ...), custom_call_target="tpu_custom_call", output_to_operand_aliasing={{}: (4, {})} | custom-call | flops 1000000 | bytes 1000000 | tf_op jit(solution)/shard_map/edges/pallas_call | solution.py:444
Async XLA Ops:
  2.4 5.9 %collective-permute-start.1 = (f32[20,8,128]{2,1,0:T(8,128)S(1)}, f32[20,8,128]{2,1,0:T(8,128)S(1)}, u32[]{:S(2)}, u32[]{:S(2)}) collective-permute-start(f32[20,8,128]{2,1,0:T(8,128)S(1)} %get-tuple-element.13), channel_id=1, source_target_pairs={{1,2},{2,1},{3,4},{4,3},{5,6},{6,5},{7,8},{8,7},{9,10},{10,9},{11,... | collective-permute-start | bytes 245768 | tf_op jit(solution)/shard_map/ppermute | solution.py:430
  6.1 2.1 %collective-permute-start = (f32[19,8,128]{2,1,0:T(8,128)S(1)}, f32[19,8,128]{2,1,0:T(8,128)S(1)}, u32[]{:S(2)}, u32[]{:S(2)}) collective-permute-start(f32[19,8,128]{2,1,0:T(8,128)S(1)} %get-tuple-element.12), channel_id=1, source_target_pairs={{0,1},{1,0},{2,3},{3,2},{4,5},{5,4},{6,7},{7,6},{8,9},{9,8},{10,11... | collective-permute-start | bytes 233480 | tf_op jit(solution)/shard_map/ppermute | solution.py:429

commit v13 on v12

--- a/solution.py
+++ b/solution.py
@@ -10,6 +10,7 @@
 
 TAIL = 8
 EARLY = 12
+STEP = 6
 
 
 class Lanes:
@@ -294,12 +295,18 @@
     plane = functools.partial(plane_at, ln, faces)
 
     def send(k, layer):
-        start = 4 if layer == 0 else 0
-        count = width + 4 - start - (4 if layer == layers - 1 else 0)
+        start, size = (4, width - 4) if layers == 1 else (jnp.where(layer == 0, 4, 0), width)
         return pltpu.make_async_copy(
-            buf.at[layer, k, pl.ds(start, count)],
-            out.at[pl.ds((layer * blocks + k) * box + depth + start, count)],
+            buf.at[layer, k, pl.ds(start, size)],
+            out.at[pl.ds((layer * blocks + k) * box + depth + start, size)],
             sems.at[layer * blocks + k],
+        )
+
+    def send_rest(k, layer):
+        return pltpu.make_async_copy(
+            buf.at[layer, k, pl.ds(width, 4)],
+            out.at[pl.ds((layer * blocks + k) * box + depth + width, 4)],
+            sems.at[bases + (layer - 1) * blocks + k],
         )
 
     def between(layer):
@@ -329,31 +336,46 @@
         high(3, blocks, vo, vz, total)
         low(width + 3, blocks, vx, None, total)
 
-    for layer in range(layers):
-        planes = [plane(layer * width + j) for j in range(1, width - 1)]
+    pl.loop(1, layers)(between)
+
+    @pl.loop(0, layers)
+    def _(layer):
         mz = masks[layer, 0:1]
-        for j in range(2, width - 2):
-            vo, vz, total = middle(planes[j - 1], planes[j - 2], planes[j], mz)
-            store(ln, buf.at[layer], j + 2, blocks, vo, vz, total)
-        if layer < layers - 1:
-            between(layer + 1)
+
+        @pl.loop(0, (width - 4) // STEP)
+        def _(i):
+            first = 2 + i * STEP
+            planes = [plane(layer * width + first + j) for j in range(-1, STEP + 1)]
+            for j in range(STEP):
+                vo, vz, total = middle(planes[j + 1], planes[j], planes[j + 2], mz)
+                store(ln, buf.at[layer], first + j + 2, blocks, vo, vz, total)
 
         @pl.loop(0, blocks)
         def _(k):
             send(k, layer).start()
 
+    @pl.loop(1, layers - 1)
+    def _(layer):
+        for k in range(blocks):
+            send_rest(k, layer).start()
+
     each_run(lambda c: c.wait())
 
-    @pl.loop(0, blocks)
-    def _(k):
-        for layer in range(layers):
+    @pl.loop(0, layers)
+    def _(layer):
+        for k in range(blocks):
             send(k, layer).wait()
+
+    @pl.loop(1, layers - 1)
+    def _(layer):
+        for k in range(blocks):
+            send_rest(k, layer).wait()
 
 
 def bulk_kernel(width, axis, faces, masks, held, out, zeros, buf, sems, zero_sems):
     del held
     me = lax.axis_index(axis)
-    bases = sems.shape[0]
+    bases = sems.shape[0] // 2
 
     @pl.when(me != 0)
     def _():
@@ -404,7 +426,7 @@
         pltpu.VMEM((2 * (width - 2), rows, lanes), f32),
         pltpu.VMEM((layers, blocks, width + 4, rows, lanes), f32),
     ]
-    inner_sems = [pltpu.SemaphoreType.DMA((bases,)), pltpu.SemaphoreType.DMA((bases + 1,))]
+    inner_sems = [pltpu.SemaphoreType.DMA((2 * bases,)), pltpu.SemaphoreType.DMA((bases + 1,))]
     tiles = 1 + 9 * rows // TAIL
     msg_a, msg_b, masks, faces, started = pl.pallas_call(
         functools.partial(pack_kernel, n, width, axis),

time: 9.62 us -> 10.4 us (1.081)
  Pallas kernels: 5.58 us -> 6.32 us
    pallas_call x1, Pallas kernels: 2.05 us -> 2.65 us  [on_device(): pl.pallas_call(functools.partial(bulk_kernel, width, axis), out_shape=out...]
    pallas_call x1, Pallas kernels: 2.36 us -> 2.5 us  [on_device(): pl.pallas_call(functools.partial(pack_kernel, n, width, axis), out_shape=...]
  transfers between devices with their start and end apart: 2 -> 2, of which waited for: 0 -> 0; matrix products, arithmetic and copies ran while one was open for 0% -> 0% of each run, Pallas kernels for 22% -> 26%
where the time goes in v13:
time: 10.4 us; the launch traced here: 10.2 us
  Pallas kernels  6.32 us (61%)
  starting transfers between devices  3.8 us (37%)
    ppermute x1, starting transfers between devices, on_device(): got_b = lax.ppermute(msg_b, axis, swaps(range(1, count - 1, 2)))  3.73 us
    pallas_call x1, Pallas kernels, on_device(): pl.pallas_call(functools.partial(bulk_kernel, width, axis), out_shape=out...  2.65 us
    pallas_call x1, Pallas kernels, on_device(): pl.pallas_call(functools.partial(pack_kernel, n, width, axis), out_shape=...  2.5 us
    pallas_call x1, Pallas kernels, on_device(): pl.pallas_call(functools.partial(edge_kernel, width, blocks, axis, count)...  1.17 us
  transfers between devices with their start and end apart: 2, of which 0 were waited for; matrix products, arithmetic and copies ran while one was open for 0% of the time, Pallas kernels for 26%

profile of v13, /device:TPU:1, one launch (start us, length us, event | category | flops | bytes accessed | tf_op | source)
XLA Modules:
  0.0 10.2 jit_solution(10064112727068126496)
XLA Ops:
  0.0 2.5 %pack.1 = (f32[19,8,128]{2,1,0:T(8,128)S(1)}, f32[20,8,128]{2,1,0:T(8,128)S(1)}, f32[2,8,128]{2,1,0:T(8,128)S(1)}, f32[4,32,16,128]{3,2,1,0:T(8,128)S(1)}, f32[768,16,128]{2,1,0:T(8,128)}) custom-call(f32[32,16,128]{2,1,0:T(8,128)} %tx.1, f32[32,16,128]{2,1,0:T(8,128)} %ty.1, f32[32,16,128]{2,1,0:T(8,128)} %tz.1, f32[32,16,128]{2,1,0:T(8,128)} %s.1, ...), custom_call_target="tpu_custom_call" | custom-call | tf_op jit(solution)/shard_map/pack/pallas_call | solution.py:431
  2.5 3.7 %collective-permute-start.1 = (f32[20,8,128]{2,1,0:T(8,128)S(1)}, f32[20,8,128]{2,1,0:T(8,128)S(1)}, u32[]{:S(2)}, u32[]{:S(2)}) collective-permute-start(f32[20,8,128]{2,1,0:T(8,128)S(1)} %get-tuple-element.13), channel_id=1, source_target_pairs={{1,2},{2,1},{3,4},{4,3},{5,6},{6,5},{7,8},{8,7},{9,10},{10,9},{11,... | collective-permute-start | bytes 245768 | tf_op jit(solution)/shard_map/ppermute | solution.py:452
  6.2 0.1 collective-permute-start
  6.3 2.7 %bulk.1.held = f32[768,16,128]{2,1,0:T(8,128)} custom-call(f32[4,32,16,128]{3,2,1,0:T(8,128)S(1)} %get-tuple-element.10.faces, f32[2,8,128]{2,1,0:T(8,128)S(1)} %get-tuple-element.11.masks, f32[768,16,128]{2,1,0:T(8,128)} %get-tuple-element.14.held), custom_call_target="tpu_custom_call", output_to_operand_aliasing={{}: (2, {})} | custom-call | flops 10000000 | bytes 7000000 | tf_op jit(solution)/shard_map/bulk/pallas_call | solution.py:454
  9.0 0.0 collective-permute-done.got_a
  9.0 0.0 collective-permute-done.1.got_b
  9.0 1.2 %edges.1 = f32[768,16,128]{2,1,0:T(8,128)} custom-call(f32[4,32,16,128]{3,2,1,0:T(8,128)S(1)} %get-tuple-element.10.faces, f32[2,8,128]{2,1,0:T(8,128)S(1)} %get-tuple-element.11.masks, f32[19,8,128]{2,1,0:T(8,128)S(1)} %collective-permute-done.got_a, f32[20,8,128]{2,1,0:T(8,128)S(1)} %collective-permute-done.1.got_b, ...), custom_call_target="tpu_custom_call", output_to_operand_aliasing={{}: (4, {})} | custom-call | flops 1000000 | bytes 1000000 | tf_op jit(solution)/shard_map/edges/pallas_call | solution.py:466
Async XLA Ops:
  2.5 6.5 %collective-permute-start.1 = (f32[20,8,128]{2,1,0:T(8,128)S(1)}, f32[20,8,128]{2,1,0:T(8,128)S(1)}, u32[]{:S(2)}, u32[]{:S(2)}) collective-permute-start(f32[20,8,128]{2,1,0:T(8,128)S(1)} %get-tuple-element.13), channel_id=1, source_target_pairs={{1,2},{2,1},{3,4},{4,3},{5,6},{6,5},{7,8},{8,7},{9,10},{10,9},{11,... | collective-permute-start | bytes 245768 | tf_op jit(solution)/shard_map/ppermute | solution.py:452
  6.2 2.7 %collective-permute-start = (f32[19,8,128]{2,1,0:T(8,128)S(1)}, f32[19,8,128]{2,1,0:T(8,128)S(1)}, u32[]{:S(2)}, u32[]{:S(2)}) collective-permute-start(f32[19,8,128]{2,1,0:T(8,128)S(1)} %get-tuple-element.12), channel_id=1, source_target_pairs={{0,1},{1,0},{2,3},{3,2},{4,5},{5,4},{6,7},{7,6},{8,9},{9,8},{10,11... | collective-permute-start | bytes 233480 | tf_op jit(solution)/shard_map/ppermute | solution.py:451
